TPU v7x, 32 devices: a whole 2x2x4 slice. The times are simulated.
32 devices in a mesh: depth: 8 (over z, y), tile: 4 (over x, core).
Axes of the slice: x: 2, y: 2, z: 4, core: 2. Of those that a mesh axis runs over, the one named last changes fastest.
Arguments:
- density: float32 [16, 512, 2048], P('depth', 'tile'), may hold values from -6 to 6
- bins: int32 [16, 512, 2048], P('depth', 'tile'), may hold values from 0 to 255
- colors: bfloat16 [3, 256], replicated, may hold values from 0.099609375 to 1
- extinction: bfloat16 [256], replicated, may hold values from 0.049804688 to 20
Outputs:
- image: float32 [4, 512, 2048], P(None, 'tile', 'depth')
All inputs are finite; a program needn't handle non-finite values.
Results may differ from a plain program's by a relative error of at most 0.0003.
Values sent between devices are 32-bit elements; how exact they have to be, the bound alone decides.
No kernel may reach another device: no remote copies, remote signals or barrier semaphores. Data moves between devices by JAX's collectives and lax.ppermute only.
A program may use at most 256 MiB of HBM per device.

v0:
```python
import math

import jax
import jax.numpy as jnp
from jax import lax
from jax.sharding import PartitionSpec as P


def padded_2(cells, sides, width):
    for axis, dim in sides:
        count = lax.axis_size(axis)
        ends = count - 1
        head = lax.slice_in_dim(cells, 0, width, axis=dim)
        tail = lax.slice_in_dim(cells, cells.shape[dim] - width, cells.shape[dim], axis=dim)
        cells = jnp.concatenate(
            [
                lax.ppermute(tail, axis, [(i, (i + 1) % count) for i in range(ends)]),
                cells,
                lax.ppermute(head, axis, [((i + 1) % count, i) for i in range(ends)]),
            ],
            axis=dim,
        )
    return cells


def partner(value, axis, stride):
    return lax.ppermute(value, axis, [(i, i ^ 1 << stride) for i in range(lax.axis_size(axis))])


def over_pair(front, back):
    return jnp.concatenate([front[:3] + front[3:] * back[:3], front[3:] * back[3:]], 0)


def per_device(density, bins, colors, extinction):
    depth_cells, row_cells, col_cells = density.shape
    slab_count = lax.axis_size("depth")
    depth_scale = 0.6 / (depth_cells * slab_count)
    padded = padded_2(density, (("depth", 0), ("tile", 1)), 1)
    grad_x = (padded[2:, 1:-1] - padded[:-2, 1:-1]) * 0.5
    grad_y = (padded[1:-1, 2:] - padded[1:-1, :-2]) * 0.5
    col_pad = jnp.pad(density, ((0, 0), (0, 0), (1, 1)))
    grad_z = (col_pad[:, :, 2:] - col_pad[:, :, :-2]) * 0.5
    lit = jnp.abs(0.48 * grad_x + 0.6 * grad_y + 0.64 * grad_z)
    shade = 0.3 + 0.7 * lit / jnp.sqrt(grad_x * grad_x + grad_y * grad_y + grad_z * grad_z + 1.0)
    lookup = jnp.concatenate([colors, extinction[None, :]], 0)
    entry_count = lookup.shape[1]
    low_count = 16
    high_count = entry_count // low_count
    table_rows = lookup.reshape(4, high_count, low_count).reshape(4 * high_count, low_count)
    total_cells = depth_cells * row_cells * col_cells
    block_size = math.gcd(total_cells, 32768)
    low_levels = lax.iota(jnp.int32, low_count)[:, None]
    high_levels = lax.iota(jnp.int32, high_count)[:, None]

    def look_block(bin_block):
        low_digit = bin_block % low_count
        high_digit = bin_block // low_count
        onehot_low = (low_levels == low_digit[None, :]).astype(jnp.bfloat16)
        partial_rows = jnp.dot(table_rows, onehot_low, preferred_element_type=jnp.float32)
        partial_rows = partial_rows.reshape(4, high_count, bin_block.shape[0])
        onehot_high = (high_levels == high_digit[None, :]).astype(jnp.float32)
        return jnp.sum(partial_rows * onehot_high[None], axis=1)

    entries = lax.map(look_block, bins.reshape(-1, block_size))
    entries = jnp.moveaxis(entries, 1, 0).reshape(4, depth_cells, row_cells, col_cells)
    optical = entries[3] * depth_scale
    emitted = entries[:3] * shade * (1.0 - jnp.exp(-optical))
    running = jnp.cumsum(optical, axis=0)
    radiance = jnp.sum(jnp.exp(-(running - optical)) * emitted, axis=1)
    transmit = jnp.exp(-running[-1])
    image_part = jnp.concatenate([radiance, transmit[None]], 0)
    slab_index = lax.axis_index("depth")
    for round_index in range(slab_count.bit_length() - 1):
        half_width = image_part.shape[2] // 2
        lower_part = image_part[:, :, :half_width]
        upper_part = image_part[:, :, half_width:]
        behind = jnp.right_shift(slab_index, round_index) % 2 == 1
        kept_part = jnp.where(behind, upper_part, lower_part)
        sent_part = jnp.where(behind, lower_part, upper_part)
        received = partner(sent_part, "depth", round_index)
        front = jnp.where(behind, received, kept_part)
        back = jnp.where(behind, kept_part, received)
        image_part = over_pair(front, back)
    return jnp.concatenate([image_part[:3], 1.0 - image_part[3:]], 0)


def solution(mesh):
    return jax.shard_map(
        per_device,
        mesh=mesh,
        in_specs=(P("depth", "tile", None), P("depth", "tile", None), P(), P()),
        out_specs=P(None, "tile", "depth"),
        check_vma=False,
    )
```

profile of v0, /device:TPU:0, one launch (start us, length us, event | category | flops | bytes accessed | tf_op | source)
XLA Modules:
  0.0 242.8 jit_solution(4547289311879083230)
XLA Ops:
  0.0 3.1 %fusion.18 = (f32[1,128,2048]{2,1,0:T(8,128)}, f32[1,128,2048]{2,1,0:T(8,128)}) fusion(f32[2,128,2048]{2,1,0:T(8,128)} %param.6), kind=kLoop, calls=%fused_computation.73 | loop fusion | bytes 4194304 | tf_op jit(solution)/shard_map/slice | solution.py:13
  3.1 1.3 collective-permute-start
  4.4 6.5 %collective-permute-start.1 = (f32[1,128,2048]{2,1,0:T(8,128)}, f32[1,128,2048]{2,1,0:T(8,128)}, u32[]{:S(2)}, u32[]{:S(2)}) collective-permute-start(f32[1,128,2048]{2,1,0:T(8,128)} %get-tuple-element.142), channel_id=1, source_target_pairs={{0,4},{4,8},{8,12},{12,16},{16,20},{20,24},{24,28},{1,5},{5,9},{9,... | collective-permute-start | bytes 3145736 | tf_op jit(solution)/shard_map/ppermute | solution.py:17
  11.1 1.8 reshape.70
  12.9 71.8 %while.15 = (s32[]{:T(128)}, f32[16,4,32768]{2,1,0:T(4,128)}, s32[16,32768]{1,0:T(8,128)S(1)}, bf16[64,16]{0,1:T(8,128)(2,1)S(1)}, s32[]{:T(128)}) while((s32[]{:T(128)}, f32[16,4,32768]{2,1,0:T(4,128)}, s32[16,32768]{1,0:T(8,128)S(1)}, bf16[64,16]{0,1:T(8,128)(2,1)S(1)}, s32[]{:T(128)}) %tuple.48), condition=%wide.region_2.3_spmd.clone.clone, body=%wide.region_0.2_spmd.clone.clone.sunk | while | flops 73498624 | bytes 6817873 | solution.py:64
  14.0 2.5 %multiply_reduce_fusion.3 = f32[4,32768]{1,0:T(4,128)S(1)} fusion(f32[16,32768]{1,0:T(8,128)S(1)} %fusion.25, bf16[64,16]{0,1:T(8,128)(2,1)S(1)} %get-tuple-element.191, s32[32768]{0:T(1024)S(1)} %bitcast.31), kind=kOutput, calls=%fused_computation.1.clone.1 | convolution fusion | flops 71696384 | bytes 2754560 | tf_op jit(solution)/shard_map/while/body/eval_jaxpr/dot_general | solution.py:59
  18.5 2.5 %multiply_reduce_fusion.3 = f32[4,32768]{1,0:T(4,128)S(1)} fusion(f32[16,32768]{1,0:T(8,128)S(1)} %fusion.25, bf16[64,16]{0,1:T(8,128)(2,1)S(1)} %get-tuple-element.191, s32[32768]{0:T(1024)S(1)} %bitcast.31), kind=kOutput, calls=%fused_computation.1.clone.1 | convolution fusion | flops 71696384 | bytes 2754560 | tf_op jit(solution)/shard_map/while/body/eval_jaxpr/dot_general | solution.py:59
  23.0 2.5 %multiply_reduce_fusion.3 = f32[4,32768]{1,0:T(4,128)S(1)} fusion(f32[16,32768]{1,0:T(8,128)S(1)} %fusion.25, bf16[64,16]{0,1:T(8,128)(2,1)S(1)} %get-tuple-element.191, s32[32768]{0:T(1024)S(1)} %bitcast.31), kind=kOutput, calls=%fused_computation.1.clone.1 | convolution fusion | flops 71696384 | bytes 2754560 | tf_op jit(solution)/shard_map/while/body/eval_jaxpr/dot_general | solution.py:59
  25.5 0.9 bitcast_dynamic-update-slice_fusion.2
  27.5 2.5 %multiply_reduce_fusion.3 = f32[4,32768]{1,0:T(4,128)S(1)} fusion(f32[16,32768]{1,0:T(8,128)S(1)} %fusion.25, bf16[64,16]{0,1:T(8,128)(2,1)S(1)} %get-tuple-element.191, s32[32768]{0:T(1024)S(1)} %bitcast.31), kind=kOutput, calls=%fused_computation.1.clone.1 | convolution fusion | flops 71696384 | bytes 2754560 | tf_op jit(solution)/shard_map/while/body/eval_jaxpr/dot_general | solution.py:59
  32.0 2.5 %multiply_reduce_fusion.3 = f32[4,32768]{1,0:T(4,128)S(1)} fusion(f32[16,32768]{1,0:T(8,128)S(1)} %fusion.25, bf16[64,16]{0,1:T(8,128)(2,1)S(1)} %get-tuple-element.191, s32[32768]{0:T(1024)S(1)} %bitcast.31), kind=kOutput, calls=%fused_computation.1.clone.1 | convolution fusion | flops 71696384 | bytes 2754560 | tf_op jit(solution)/shard_map/while/body/eval_jaxpr/dot_general | solution.py:59
  34.4 0.8 bitcast_dynamic-update-slice_fusion.2
  36.4 2.5 %multiply_reduce_fusion.3 = f32[4,32768]{1,0:T(4,128)S(1)} fusion(f32[16,32768]{1,0:T(8,128)S(1)} %fusion.25, bf16[64,16]{0,1:T(8,128)(2,1)S(1)} %get-tuple-element.191, s32[32768]{0:T(1024)S(1)} %bitcast.31), kind=kOutput, calls=%fused_computation.1.clone.1 | convolution fusion | flops 71696384 | bytes 2754560 | tf_op jit(solution)/shard_map/while/body/eval_jaxpr/dot_general | solution.py:59
  38.9 0.9 bitcast_dynamic-update-slice_fusion.2
  40.9 2.5 %multiply_reduce_fusion.3 = f32[4,32768]{1,0:T(4,128)S(1)} fusion(f32[16,32768]{1,0:T(8,128)S(1)} %fusion.25, bf16[64,16]{0,1:T(8,128)(2,1)S(1)} %get-tuple-element.191, s32[32768]{0:T(1024)S(1)} %bitcast.31), kind=kOutput, calls=%fused_computation.1.clone.1 | convolution fusion | flops 71696384 | bytes 2754560 | tf_op jit(solution)/shard_map/while/body/eval_jaxpr/dot_general | solution.py:59
  43.4 0.9 bitcast_dynamic-update-slice_fusion.2
  45.4 2.5 %multiply_reduce_fusion.3 = f32[4,32768]{1,0:T(4,128)S(1)} fusion(f32[16,32768]{1,0:T(8,128)S(1)} %fusion.25, bf16[64,16]{0,1:T(8,128)(2,1)S(1)} %get-tuple-element.191, s32[32768]{0:T(1024)S(1)} %bitcast.31), kind=kOutput, calls=%fused_computation.1.clone.1 | convolution fusion | flops 71696384 | bytes 2754560 | tf_op jit(solution)/shard_map/while/body/eval_jaxpr/dot_general | solution.py:59
  49.9 2.5 %multiply_reduce_fusion.3 = f32[4,32768]{1,0:T(4,128)S(1)} fusion(f32[16,32768]{1,0:T(8,128)S(1)} %fusion.25, bf16[64,16]{0,1:T(8,128)(2,1)S(1)} %get-tuple-element.191, s32[32768]{0:T(1024)S(1)} %bitcast.31), kind=kOutput, calls=%fused_computation.1.clone.1 | convolution fusion | flops 71696384 | bytes 2754560 | tf_op jit(solution)/shard_map/while/body/eval_jaxpr/dot_general | solution.py:59
  54.4 2.5 %multiply_reduce_fusion.3 = f32[4,32768]{1,0:T(4,128)S(1)} fusion(f32[16,32768]{1,0:T(8,128)S(1)} %fusion.25, bf16[64,16]{0,1:T(8,128)(2,1)S(1)} %get-tuple-element.191, s32[32768]{0:T(1024)S(1)} %bitcast.31), kind=kOutput, calls=%fused_computation.1.clone.1 | convolution fusion | flops 71696384 | bytes 2754560 | tf_op jit(solution)/shard_map/while/body/eval_jaxpr/dot_general | solution.py:59
  58.8 2.5 %multiply_reduce_fusion.3 = f32[4,32768]{1,0:T(4,128)S(1)} fusion(f32[16,32768]{1,0:T(8,128)S(1)} %fusion.25, bf16[64,16]{0,1:T(8,128)(2,1)S(1)} %get-tuple-element.191, s32[32768]{0:T(1024)S(1)} %bitcast.31), kind=kOutput, calls=%fused_computation.1.clone.1 | convolution fusion | flops 71696384 | bytes 2754560 | tf_op jit(solution)/shard_map/while/body/eval_jaxpr/dot_general | solution.py:59
  61.3 0.9 bitcast_dynamic-update-slice_fusion.2
  63.4 2.5 %multiply_reduce_fusion.3 = f32[4,32768]{1,0:T(4,128)S(1)} fusion(f32[16,32768]{1,0:T(8,128)S(1)} %fusion.25, bf16[64,16]{0,1:T(8,128)(2,1)S(1)} %get-tuple-element.191, s32[32768]{0:T(1024)S(1)} %bitcast.31), kind=kOutput, calls=%fused_computation.1.clone.1 | convolution fusion | flops 71696384 | bytes 2754560 | tf_op jit(solution)/shard_map/while/body/eval_jaxpr/dot_general | solution.py:59
  67.8 2.5 %multiply_reduce_fusion.3 = f32[4,32768]{1,0:T(4,128)S(1)} fusion(f32[16,32768]{1,0:T(8,128)S(1)} %fusion.25, bf16[64,16]{0,1:T(8,128)(2,1)S(1)} %get-tuple-element.191, s32[32768]{0:T(1024)S(1)} %bitcast.31), kind=kOutput, calls=%fused_computation.1.clone.1 | convolution fusion | flops 71696384 | bytes 2754560 | tf_op jit(solution)/shard_map/while/body/eval_jaxpr/dot_general | solution.py:59
  72.3 2.5 %multiply_reduce_fusion.3 = f32[4,32768]{1,0:T(4,128)S(1)} fusion(f32[16,32768]{1,0:T(8,128)S(1)} %fusion.25, bf16[64,16]{0,1:T(8,128)(2,1)S(1)} %get-tuple-element.191, s32[32768]{0:T(1024)S(1)} %bitcast.31), kind=kOutput, calls=%fused_computation.1.clone.1 | convolution fusion | flops 71696384 | bytes 2754560 | tf_op jit(solution)/shard_map/while/body/eval_jaxpr/dot_general | solution.py:59
  76.8 2.5 %multiply_reduce_fusion.3 = f32[4,32768]{1,0:T(4,128)S(1)} fusion(f32[16,32768]{1,0:T(8,128)S(1)} %fusion.25, bf16[64,16]{0,1:T(8,128)(2,1)S(1)} %get-tuple-element.191, s32[32768]{0:T(1024)S(1)} %bitcast.31), kind=kOutput, calls=%fused_computation.1.clone.1 | convolution fusion | flops 71696384 | bytes 2754560 | tf_op jit(solution)/shard_map/while/body/eval_jaxpr/dot_general | solution.py:59
  81.2 2.5 %multiply_reduce_fusion.3 = f32[4,32768]{1,0:T(4,128)S(1)} fusion(f32[16,32768]{1,0:T(8,128)S(1)} %fusion.25, bf16[64,16]{0,1:T(8,128)(2,1)S(1)} %get-tuple-element.191, s32[32768]{0:T(1024)S(1)} %bitcast.31), kind=kOutput, calls=%fused_computation.1.clone.1 | convolution fusion | flops 71696384 | bytes 2754560 | tf_op jit(solution)/shard_map/while/body/eval_jaxpr/dot_general | solution.py:59
  83.7 0.9 bitcast_dynamic-update-slice_fusion.2
  84.6 11.6 %fusion.9 = f32[16,32768]{1,0:T(8,128)} fusion(f32[4,16,32768]{2,0,1:T(4,128)} %bitcast.29), kind=kLoop, calls=%fused_computation.28 | loop fusion | flops 524288 | bytes 4194304 | tf_op jit(solution)/shard_map/mul | solution.py:66
  96.2 1.7 mul.142
  97.9 1.3 fusion.19
  99.2 2.6 %negate_exponential_fusion = (f32[2,128,2048]{2,1,0:T(8,128)}, f32[2,128,2048]{2,1,0:T(8,128)}) fusion(f32[2,128,2048]{2,1,0:T(8,128)S(1)} %fusion.19, f32[2,128,2048]{2,1,0:T(8,128)S(1)} %mul.142), kind=kLoop, calls=%fused_computation.33 | loop fusion | flops 2097152 | bytes 8388608 | tf_op jit(solution)/shard_map/exp | solution.py:69
  101.8 1.4 constant_dynamic-update-slice_fusion.2
  104.0 1.3 collective-permute-start.2
  105.3 3.0 %collective-permute-start.3 = (f32[4,1,2048]{2,1,0:T(1,128)S(1)}, f32[4,1,2048]{2,1,0:T(1,128)S(1)}, u32[]{:S(2)}, u32[]{:S(2)}) collective-permute-start(f32[4,1,2048]{2,1,0:T(1,128)S(1)} %get-tuple-element.134), channel_id=1, source_target_pairs={{0,1},{1,2},{2,3},{4,5},{5,6},{6,7},{8,9},{9,10},{10,11},{12,13},{... | collective-permute-start | bytes 98312 | tf_op jit(solution)/shard_map/ppermute | solution.py:17
  108.4 1.2 fusion.12
  109.5 9.7 %copy.6 = f32[3,16,32768]{2,1,0:T(8,128)} copy(f32[3,16,32768]{2,0,1:T(4,128)} %bitcast.30) | data formatting | bytes 12582912 | tf_op jit(solution)/shard_map/slice | solution.py:67
  119.3 7.2 %slice.106 = f32[3,2,128,2048]{3,2,1,0:T(8,128)} reshape(f32[3,16,32768]{2,1,0:T(8,128)} %copy.6) | data formatting | bytes 12582912 | tf_op jit(solution)/shard_map/slice | solution.py:67
  126.4 4.1 %multiply_add_fusion = f32[2,128,2048]{2,1,0:T(8,128)S(1)} fusion(f32[2,128,2048]{2,1,0:T(8,128)S(1)} %copy-done.1, f32[4,128,2048]{2,1,0:T(8,128)} %copy-done.3, f32[4,1,2048]{2,1,0:T(1,128)S(1)} %collective-permute-done.3, f32[4,1,2048]{2,1,0:T(1,128)S(1)} %collective-permute-done.2, f32[1,128,2048]{2,1,0:T(8,128)} %collective-permute-done.1, ...), kind=kLoop, calls=%fused_computation.32 | loop fusion | flops 13107200 | bytes 10551296 | tf_op jit(solution)/shard_map/add | solution.py:44
  130.8 4.3 %multiply_reduce_fusion.1 = f32[3,128,2048]{2,1,0:T(8,128)S(1)} fusion(f32[3,2,128,2048]{3,2,1,0:T(8,128)S(1)} %copy-done, f32[2,128,2048]{2,1,0:T(8,128)} %get-tuple-element.140, f32[2,128,2048]{2,1,0:T(8,128)S(1)} %multiply_add_fusion, f32[2,128,2048]{2,1,0:T(8,128)} %get-tuple-element.139), kind=kLoop, calls=%fused_computation.13 | loop fusion | flops 5505024 | bytes 15728640 | tf_op jit(solution)/shard_map/reduce_sum | solution.py:69
  135.1 1.7 broadcast_select_fusion.3
  136.8 2.0 collective-permute-start.4
  138.8 46.3 %collective-permute-done.4 = f32[4,128,1024]{2,1,0:T(8,128)} collective-permute-done((f32[4,128,1024]{2,1,0:T(8,128)}, f32[4,128,1024]{2,1,0:T(8,128)}, u32[]{:S(2)}, u32[]{:S(2)}) %collective-permute-start.4) | collective-permute-done | bytes 2097184 | tf_op jit(solution)/shard_map/ppermute | solution.py:27
  185.1 2.8 %broadcast_select_fusion.1 = (f32[4,128,1024]{2,1,0:T(8,128)S(1)}, f32[4,128,1024]{2,1,0:T(8,128)S(1)}) fusion(f32[4,128,1024]{2,1,0:T(8,128)} %collective-permute-done.4, pred[]{:T(512)S(6)} %eq.88, f32[1,128,2048]{2,1,0:T(8,128)} %fusion.12, f32[3,128,2048]{2,1,0:T(8,128)S(1)} %multiply_reduce_fusion.1), kind=kLoop, calls=%fused_computation.43 | loop fusion | flops 3670016 | bytes 10485761 | tf_op jit(solution)/shard_map/jit(_where)/select_n | solution.py:81
  188.5 1.8 collective-permute-start.5
  190.3 23.8 %collective-permute-done.5 = f32[4,128,512]{2,1,0:T(8,128)} collective-permute-done((f32[4,128,512]{2,1,0:T(8,128)S(1)}, f32[4,128,512]{2,1,0:T(8,128)}, u32[]{:S(2)}, u32[]{:S(2)}) %collective-permute-start.5) | collective-permute-done | bytes 1048608 | tf_op jit(solution)/shard_map/ppermute | solution.py:27
  214.2 1.6 broadcast_select_fusion.5
  216.1 2.6 %collective-permute-start.6 = (f32[4,128,256]{2,1,0:T(8,128)S(1)}, f32[4,128,256]{2,1,0:T(8,128)S(1)}, u32[]{:S(2)}, u32[]{:S(2)}) collective-permute-start(f32[4,128,256]{2,1,0:T(8,128)S(1)} %broadcast_select_fusion.11), channel_id=1, source_target_pairs={{0,16},{4,20},{8,24},{12,28},{16,0},{20,4},{24,8},{28,12},{1,17},{... | collective-permute-start | bytes 1572872 | tf_op jit(solution)/shard_map/ppermute | solution.py:27
  218.6 23.1 %collective-permute-done.6 = f32[4,128,256]{2,1,0:T(8,128)S(1)} collective-permute-done((f32[4,128,256]{2,1,0:T(8,128)S(1)}, f32[4,128,256]{2,1,0:T(8,128)S(1)}, u32[]{:S(2)}, u32[]{:S(2)}) %collective-permute-start.6) | collective-permute-done | bytes 524320 | tf_op jit(solution)/shard_map/ppermute | solution.py:27
  (92 shorter events, 29.8 us)
Async XLA Ops:
  0.0 10.9 %copy-start.5 = (bf16[256]{0:T(256)(128)(2,1)S(1)}, bf16[256]{0:T(256)(128)(2,1)}, u32[]{:S(2)}) copy-start(bf16[256]{0:T(256)(128)(2,1)} %param.9) | copy-start | bytes 1540
  0.0 10.9 %copy-start.4 = (bf16[3,256]{1,0:T(4,128)(2,1)S(1)}, bf16[3,256]{1,0:T(4,128)(2,1)}, u32[]{:S(2)}) copy-start(bf16[3,256]{1,0:T(4,128)(2,1)} %param.8) | copy-start | bytes 4612
  3.1 100.8 %collective-permute-start = (f32[1,128,2048]{2,1,0:T(8,128)}, f32[1,128,2048]{2,1,0:T(8,128)S(1)}, u32[]{:S(2)}, u32[]{:S(2)}) collective-permute-start(f32[1,128,2048]{2,1,0:T(8,128)} %get-tuple-element.141), channel_id=1, source_target_pairs={{4,0},{8,4},{12,8},{16,12},{20,16},{24,20},{28,24},{5,1},{9,5},{13... | collective-permute-start | bytes 3145736 | tf_op jit(solution)/shard_map/ppermute | solution.py:19
  4.4 97.4 %collective-permute-start.1 = (f32[1,128,2048]{2,1,0:T(8,128)}, f32[1,128,2048]{2,1,0:T(8,128)}, u32[]{:S(2)}, u32[]{:S(2)}) collective-permute-start(f32[1,128,2048]{2,1,0:T(8,128)} %get-tuple-element.142), channel_id=1, source_target_pairs={{0,4},{4,8},{8,12},{12,16},{16,20},{20,24},{24,28},{1,5},{5,9},{9,... | collective-permute-start | bytes 3145736 | tf_op jit(solution)/shard_map/ppermute | solution.py:17
  101.8 1.9 copy-start.1
  104.0 5.6 %copy-start.3 = (f32[4,128,2048]{2,1,0:T(8,128)}, f32[4,128,2048]{2,1,0:T(8,128)S(1)}, u32[]{:S(2)}) copy-start(f32[4,128,2048]{2,1,0:T(8,128)S(1)} %constant_dynamic-update-slice_fusion) | copy-start | bytes 12582916
  104.0 22.4 %collective-permute-start.2 = (f32[4,1,2048]{2,1,0:T(1,128)S(1)}, f32[4,1,2048]{2,1,0:T(1,128)S(1)}, u32[]{:S(2)}, u32[]{:S(2)}) collective-permute-start(f32[4,1,2048]{2,1,0:T(1,128)S(1)} %get-tuple-element.133), channel_id=1, source_target_pairs={{1,0},{2,1},{3,2},{5,4},{6,5},{7,6},{9,8},{10,9},{11,10},{13,12},{... | collective-permute-start | bytes 98312 | tf_op jit(solution)/shard_map/ppermute | solution.py:19
  105.3 21.1 %collective-permute-start.3 = (f32[4,1,2048]{2,1,0:T(1,128)S(1)}, f32[4,1,2048]{2,1,0:T(1,128)S(1)}, u32[]{:S(2)}, u32[]{:S(2)}) collective-permute-start(f32[4,1,2048]{2,1,0:T(1,128)S(1)} %get-tuple-element.134), channel_id=1, source_target_pairs={{0,1},{1,2},{2,3},{4,5},{5,6},{6,7},{8,9},{9,10},{10,11},{12,13},{... | collective-permute-start | bytes 98312 | tf_op jit(solution)/shard_map/ppermute | solution.py:17
  126.4 4.4 %copy-start = (f32[3,2,128,2048]{3,2,1,0:T(8,128)S(1)}, f32[3,2,128,2048]{3,2,1,0:T(8,128)}, u32[]{:S(2)}) copy-start(f32[3,2,128,2048]{3,2,1,0:T(8,128)} %slice.106) | copy-start | bytes 18874372
  130.8 4.3 %copy-start.2 = (f32[1,128,2048]{2,1,0:T(8,128)S(1)}, f32[1,128,2048]{2,1,0:T(8,128)}, u32[]{:S(2)}) copy-start(f32[1,128,2048]{2,1,0:T(8,128)} %fusion.12) | copy-start | bytes 3145732
  136.8 48.2 %collective-permute-start.4 = (f32[4,128,1024]{2,1,0:T(8,128)}, f32[4,128,1024]{2,1,0:T(8,128)}, u32[]{:S(2)}, u32[]{:S(2)}) collective-permute-start(f32[4,128,1024]{2,1,0:T(8,128)} %broadcast_select_fusion.3), channel_id=1, source_target_pairs={{0,4},{4,0},{8,12},{12,8},{16,20},{20,16},{24,28},{28,24},{1,5},{5... | collective-permute-start | bytes 6291464 | tf_op jit(solution)/shard_map/ppermute | solution.py:27
  188.5 25.7 %collective-permute-start.5 = (f32[4,128,512]{2,1,0:T(8,128)S(1)}, f32[4,128,512]{2,1,0:T(8,128)}, u32[]{:S(2)}, u32[]{:S(2)}) collective-permute-start(f32[4,128,512]{2,1,0:T(8,128)S(1)} %broadcast_select_fusion.7), channel_id=1, source_target_pairs={{0,8},{4,12},{8,0},{12,4},{16,24},{20,28},{24,16},{28,20},{1,9},{5... | collective-permute-start | bytes 3145736 | tf_op jit(solution)/shard_map/ppermute | solution.py:27
  216.1 25.7 %collective-permute-start.6 = (f32[4,128,256]{2,1,0:T(8,128)S(1)}, f32[4,128,256]{2,1,0:T(8,128)S(1)}, u32[]{:S(2)}, u32[]{:S(2)}) collective-permute-start(f32[4,128,256]{2,1,0:T(8,128)S(1)} %broadcast_select_fusion.11), channel_id=1, source_target_pairs={{0,16},{4,20},{8,24},{12,28},{16,0},{20,4},{24,8},{28,12},{1,17},{... | collective-permute-start | bytes 1572872 | tf_op jit(solution)/shard_map/ppermute | solution.py:27
where the time goes:
time: 243 us
  waiting for transfers between devices  93.2 us (38%)
  other arithmetic  51.2 us (21%)
  local copies, waits for them, and re-layouts  39.7 us (16%)
  matrix products  39.6 us (16%)
  starting transfers between devices  18.5 us (8%)
    ppermute x3, waiting for transfers between devices, partner(): lax.ppermute(value, axis, [(i, i ^ 1 << stride) for i in range(lax.axis_s...  93.2 us
    dot_general x16, matrix products, look_block(): jnp.dot(table_rows, onehot_low, preferred_element_type=jnp.float32)  39.6 us
    slice x2, local copies, waits for them, and re-layouts, per_device(): emitted = entries[:3] * shade * (1.0 - jnp.exp(-optical))  16.9 us
    dynamic_update_slice x16, local copies, waits for them, and re-layouts, per_device(): entries = lax.map(look_block, bins.reshape(-1, block_size))  13.5 us
    mul x1, other arithmetic, per_device(): optical = entries[3] * depth_scale  11.6 us
    ppermute x2, starting transfers between devices, padded_2(): lax.ppermute(tail, axis, [(i, (i + 1) % count) for i in range(ends)])  9.52 us
    select_n x16, other arithmetic, look_block(): high_digit = bin_block // low_count  8.83 us
    select_n x16, other arithmetic, look_block(): low_digit = bin_block % low_count  7.15 us
  transfers between devices with their start and end apart: 7, of which 3 were waited for; matrix products, arithmetic and copies ran while one was open for 45% of the time, Pallas kernels for 0%

commit v1 on v0

v1 whole, which is shorter than its diff:
```python
import functools

import jax
import jax.numpy as jnp
from jax import lax
from jax.experimental import pallas as pl
from jax.experimental.pallas import tpu as pltpu
from jax.sharding import PartitionSpec as P

LANES = 128
VMEM_LIMIT = 24 * 1024 * 1024


def params():
    return pltpu.CompilerParams(vmem_limit_bytes=VMEM_LIMIT)


def pack_body(layers, rows, top_row, bottom_row, side_ref, dens, top, bottom, column, bins, out):
    side = side_ref[0]
    for layer in range(layers):
        out[layer * rows : (layer + 1) * rows, :] = dens[layer]
        out[(layers + layer) * rows : (layers + layer + 1) * rows, :] = bins[layer].astype(jnp.float32)
    base = 2 * layers * rows
    for layer in range(layers):
        out[base + 2 * layer : base + 2 * layer + 1, :] = top[layer, top_row : top_row + 1, :]
        out[base + 2 * layer + 1 : base + 2 * layer + 2, :] = bottom[layer, bottom_row : bottom_row + 1, :]
    lane = lax.broadcasted_iota(jnp.int32, (8, LANES), 1)
    edges = jnp.zeros((8, LANES), jnp.float32)
    for layer in range(layers):
        for step in range(rows // 8):
            block = column[layer, step * 8 : step * 8 + 8, :]
            edge = jnp.where(side == 0, block[:, LANES - 1 :], block[:, :1])
            edges = jnp.where(lane == layer * (rows // 8) + step, edge, edges)
    out[base + 4 : base + 8, :] = jnp.zeros((4, out.shape[1]), jnp.float32)
    out[base + 4 : base + 8, :LANES] = edges[:4]
    out[base + 4 : base + 8, LANES : 2 * LANES] = edges[4:]


def render_body(layers, rows, scale, top_row, bottom_row, side_ref, table, dens, top, bottom, column, bins, message, direct, passed, kept, sent, cells, ends, entry, rgbt, lookup):
    side = side_ref[0]
    bit = side_ref[1]
    half = dens.shape[2]
    tiles = half // LANES
    deep = 2 * layers
    mine = side * layers
    other = (1 - side) * layers
    base = 2 * layers * rows
    transmit = jnp.exp(table[3:4, :] * (-scale))
    for channel in range(4):
        value = table[channel : channel + 1, :] * (1.0 - transmit) if channel < 3 else transmit
        for part in range(2):
            lookup[2 * channel + part] = jnp.broadcast_to(value[:, part * LANES : (part + 1) * LANES], (8, LANES))
    body = pl.ds(8, rows)
    cells[(1 - side) * (deep + 1), body, :] = direct[...]
    cells[side * (deep + 1), body, :] = passed[...]
    low = message[base : base + 8, :LANES]
    high = message[base : base + 8, LANES : 2 * LANES]
    edges = jnp.concatenate([low[4:], high[4:]], 0)
    ends[side] = jnp.zeros_like(ends[side])
    for layer in range(layers):
        cells[1 + mine + layer, body, :] = dens[layer]
        cells[1 + mine + layer, 7:8, :] = top[layer, top_row : top_row + 1, :]
        cells[1 + mine + layer, 8 + rows : 9 + rows, :] = bottom[layer, bottom_row : bottom_row + 1, :]
        cells[1 + other + layer, body, :] = message[layer * rows : (layer + 1) * rows, :]
        cells[1 + other + layer, 7:8, :] = message[base + 2 * layer : base + 2 * layer + 1, :]
        cells[1 + other + layer, 8 + rows : 9 + rows, :] = message[base + 2 * layer + 1 : base + 2 * layer + 2, :]
        entry[mine + layer] = bins[layer]
        entry[other + layer] = message[(layers + layer) * rows : (layers + layer + 1) * rows, :].astype(jnp.int32)
        ends[1 - side, mine + layer] = column[layer]
        for step in range(rows // 8):
            place = layer * (rows // 8) + step
            ends[1 - side, other + layer, step * 8 : step * 8 + 8, :] = jnp.broadcast_to(edges[:, place : place + 1], (8, LANES))
    lane = lax.broadcasted_iota(jnp.int32, (8, LANES), 1)
    line = lax.broadcasted_iota(jnp.int32, (8, LANES), 0)

    def strip(step, carry):
        row = pl.multiple_of(step * 8, 8)
        here = pl.ds(row, 8)

        def tile_of(layer, tile):
            if tile < 0:
                return ends[0, layer, here, :]
            if tile == tiles:
                return ends[1, layer, here, :]
            return cells[1 + layer, pl.ds(row + 8, 8), tile * LANES : (tile + 1) * LANES]

        for tile in range(tiles):
            span = slice(tile * LANES, (tile + 1) * LANES)
            through = None
            total = None
            for layer in range(deep):
                before = cells[layer, pl.ds(row + 8, 8), span]
                after = cells[layer + 2, pl.ds(row + 8, 8), span]
                cell = tile_of(layer, tile)
                above = pltpu.roll(jnp.where(line == 7, cells[1 + layer, here, span], cell), 1, 0)
                below = pltpu.roll(jnp.where(line == 0, cells[1 + layer, pl.ds(row + 16, 8), span], cell), 7, 0)
                left = pltpu.roll(jnp.where(lane == LANES - 1, tile_of(layer, tile - 1), cell), 1, 1)
                right = pltpu.roll(jnp.where(lane == 0, tile_of(layer, tile + 1), cell), LANES - 1, 1)
                gx = after - before
                gy = below - above
                gz = right - left
                lit = jnp.abs(0.336 * gx + 0.42 * gy + 0.448 * gz)
                shade = 0.3 + lit * lax.rsqrt(gx * gx + gy * gy + gz * gz + 4.0)
                index = entry[layer, here, span]
                low_index = index & (LANES - 1)
                upper = index >= LANES
                looked = []
                for channel in range(4):
                    first = jnp.take_along_axis(lookup[2 * channel], low_index, axis=1, mode="promise_in_bounds")
                    second = jnp.take_along_axis(lookup[2 * channel + 1], low_index, axis=1, mode="promise_in_bounds")
                    looked.append(jnp.where(upper, second, first))
                if layer == 0:
                    total = [shade * looked[c] for c in range(3)]
                    through = looked[3]
                else:
                    weight = through * shade
                    total = [total[c] + weight * looked[c] for c in range(3)]
                    through = through * looked[3]
            which = jnp.where(bit == 0, tile // (tiles // 2), 1 - tile // (tiles // 2))
            place = slice((tile % (tiles // 2)) * LANES, (tile % (tiles // 2) + 1) * LANES)
            for c, value in enumerate(total + [through]):
                rgbt[which, c, here, place] = value
        return carry

    lax.fori_loop(0, rows // 8, strip, 0)
    kept[...] = rgbt[0]
    sent[...] = rgbt[1]


def merged_of(behind, held, got):
    mine = [held[c] for c in range(4)]
    theirs = [got[c] for c in range(4)]
    front = [jnp.where(behind, b, a) for a, b in zip(mine, theirs)]
    back = [jnp.where(behind, a, b) for a, b in zip(mine, theirs)]
    return [front[c] + front[3] * back[c] for c in range(3)] + [front[3] * back[3]]


def swap_body(bit_ref, held, got, kept, sent):
    width = kept.shape[2]
    values = merged_of(bit_ref[0] == 1, held, got)
    upper = bit_ref[1] == 1
    for c, value in enumerate(values):
        kept[c] = jnp.where(upper, value[:, width:], value[:, :width])
        sent[c] = jnp.where(upper, value[:, :width], value[:, width:])


def last_body(bit_ref, held, got, *rest):
    out = rest[-1]
    values = merged_of(bit_ref[0] == 1, held, got)
    for c in range(3):
        out[c] = values[c]
    out[3] = 1.0 - values[3]


def split_off(cells, bit):
    width = cells.shape[2] // 2
    low, high = cells[:, :, :width], cells[:, :, width:]
    return jnp.where(bit == 1, high, low), jnp.where(bit == 1, low, high)


def per_device(density, bins, colors, extinction, *, chunk_order, rows):
    layers, height, width = density.shape
    slabs = lax.axis_size("depth")
    tile_count = lax.axis_size("tile")
    scale = 0.6 / (layers * slabs)
    half = width // 2
    half_tiles = half // LANES
    slab = lax.axis_index("depth")
    rounds = slabs.bit_length() - 1
    bits = [jnp.right_shift(slab, r) & 1 for r in range(rounds)]
    side = bits[0]
    table = jnp.concatenate([colors, extinction[None, :]], 0).astype(jnp.float32)
    chunks = height // rows

    def along(array, axis, pairs):
        return lax.ppermute(array, axis, pairs)

    from_above = along(density[:, height - 1 :, :], "tile", [(i, i + 1) for i in range(tile_count - 1)])
    from_below = along(density[:, :1, :], "tile", [(i + 1, i) for i in range(tile_count - 1)])
    onward = [(i, i + 2) if i % 2 else (i, i - 2) for i in range(slabs)]
    onward = [(i, j) for i, j in onward if 0 <= j < slabs]
    backward = [(i, i - 2) if i % 2 else (i, i + 2) for i in range(slabs)]
    backward = [(i, j) for i, j in backward if 0 <= j < slabs]
    face = lax.dynamic_slice(density, (side * (layers - 1), 0, side * half), (1, height, half))[0]
    direct = along(face, "depth", onward)

    scalars = jnp.stack(bits[:2]).astype(jnp.int32)

    def whole(shape):
        return pl.BlockSpec(shape, lambda i, s: (0,) * len(shape))

    def edge_specs(chunk, half_of):
        if chunk == 0:
            first = (from_above, pl.BlockSpec((layers, 1, half), lambda i, s: (0, 0, half_of(s))), 0)
        else:
            first = (density, pl.BlockSpec((layers, 8, half), lambda i, s: (0, chunk * rows // 8 - 1, half_of(s))), 7)
        if chunk == chunks - 1:
            second = (from_below, pl.BlockSpec((layers, 1, half), lambda i, s: (0, 0, half_of(s))), 0)
        else:
            second = (density, pl.BlockSpec((layers, 8, half), lambda i, s: (0, (chunk + 1) * rows // 8, half_of(s))), 0)
        return first, second

    def pack(chunk):
        first, second = edge_specs(chunk, lambda s: 1 - s[0])
        block = pl.BlockSpec((layers, rows, half), lambda i, s: (0, chunk, 1 - s[0]))
        shape = (2 * layers * rows + 8, half)
        return pl.pallas_call(
            functools.partial(pack_body, layers, rows, first[2], second[2]),
            out_shape=jax.ShapeDtypeStruct(shape, jnp.float32),
            grid_spec=pltpu.PrefetchScalarGridSpec(
                num_scalar_prefetch=1,
                grid=(1,),
                in_specs=[
                    block,
                    first[1],
                    second[1],
                    pl.BlockSpec((layers, rows, LANES), lambda i, s: (0, chunk, half_tiles - 1 + s[0])),
                    block,
                ],
                out_specs=whole(shape),
            ),
            compiler_params=params(),
            cost_estimate=pl.CostEstimate(flops=0, bytes_accessed=4 * 4 * layers * rows * half, transcendentals=0),
            name="pack",
        )(scalars, density, first[0], second[0], density, bins)

    def render(chunk, message, passed):
        first, second = edge_specs(chunk, lambda s: s[0])
        block = pl.BlockSpec((layers, rows, half), lambda i, s: (0, chunk, s[0]))
        shape = (4, rows, half // 2)
        out = jax.ShapeDtypeStruct(shape, jnp.float32)
        deep = 2 * layers
        return pl.pallas_call(
            functools.partial(render_body, layers, rows, scale, first[2], second[2]),
            out_shape=(out, out),
            grid_spec=pltpu.PrefetchScalarGridSpec(
                num_scalar_prefetch=1,
                grid=(1,),
                in_specs=[
                    whole(table.shape),
                    block,
                    first[1],
                    second[1],
                    pl.BlockSpec((layers, rows, LANES), lambda i, s: (0, chunk, half_tiles - s[0])),
                    block,
                    whole(message.shape),
                    pl.BlockSpec((rows, half), lambda i, s: (chunk, 0)),
                    whole(passed.shape),
                ],
                out_specs=(whole(shape), whole(shape)),
                scratch_shapes=[
                    pltpu.VMEM((deep + 2, rows + 16, half), jnp.float32),
                    pltpu.VMEM((2, deep, rows, LANES), jnp.float32),
                    pltpu.VMEM((deep, rows, half), jnp.int32),
                    pltpu.VMEM((2, 4, rows, half // 2), jnp.float32),
                    pltpu.VMEM((8, 8, LANES), jnp.float32),
                ],
            ),
            compiler_params=params(),
            cost_estimate=pl.CostEstimate(flops=60 * deep * rows * half, bytes_accessed=40 * rows * half, transcendentals=deep * rows * half),
            name="render",
        )(scalars, table, density, first[0], second[0], density, bins, message, direct, passed)

    def small(body, scalars, ins, outs, out_spec=None, aliases=None, alias=None):
        specs = [whole(a.shape) for a in ins]
        operands = list(ins)
        if alias is not None:
            specs.append(pl.BlockSpec(memory_space=pl.ANY))
            operands.append(alias)
        return pl.pallas_call(
            body,
            out_shape=outs,
            grid_spec=pltpu.PrefetchScalarGridSpec(num_scalar_prefetch=1, grid=(1,), in_specs=specs, out_specs=out_spec),
            compiler_params=params(),
            input_output_aliases=aliases or {},
            cost_estimate=pl.CostEstimate(flops=8 * ins[0].size, bytes_accessed=16 * ins[0].size, transcendentals=0),
            name="merge",
        )(scalars, *operands)

    image = None
    parts = {}
    for chunk in chunk_order:
        message = along(pack(chunk), "depth", [(i, i ^ 1) for i in range(slabs)])
        layer = lax.dynamic_slice(message, ((1 - side) * (layers - 1) * rows, 0), (rows, half))
        passed = along(layer, "depth", backward)
        kept, sent = render(chunk, message, passed)
        for r in range(1, rounds):
            got = along(sent, "depth", [(i, i ^ (1 << r)) for i in range(slabs)])
            cols = kept.shape[2]
            if r == rounds - 1 and cols % LANES == 0:
                shape = (4, height, cols)
                image = small(
                    last_body,
                    bits[r][None],
                    [kept, got],
                    jax.ShapeDtypeStruct(shape, jnp.float32),
                    pl.BlockSpec((4, rows, cols), lambda i, s, chunk=chunk: (0, chunk, 0)),
                    {3: 0} if image is not None else None,
                    image,
                )
            elif r < rounds - 1 and cols % (2 * LANES) == 0:
                shape = (4, rows, cols // 2)
                out = jax.ShapeDtypeStruct(shape, jnp.float32)
                kept, sent = small(swap_body, jnp.stack([bits[r], bits[r + 1]]), [kept, got], (out, out), (whole(shape), whole(shape)))
            else:
                values = jnp.stack(merged_of(bits[r] == 1, kept, got))
                if r < rounds - 1:
                    kept, sent = split_off(values, bits[r + 1])
                else:
                    parts[chunk] = jnp.concatenate([values[:3], 1.0 - values[3:]], 0)
    if image is None:
        image = jnp.concatenate([parts[c] for c in range(chunks)], 1)
    return image


def solution(mesh):
    return jax.shard_map(
        functools.partial(per_device, chunk_order=(1, 2, 0, 3), rows=32),
        mesh=mesh,
        in_specs=(P("depth", "tile", None), P("depth", "tile", None), P(), P()),
        out_specs=P(None, "tile", "depth"),
        check_vma=False,
    )
```

time: 243 us -> 114 us (0.47)
  waiting for transfers between devices: 93.2 us -> 36 us
  other arithmetic: 51.2 us -> 0.16 us
  matrix products: 39.6 us -> 0 us
  Pallas kernels: 0 us -> 31.7 us
  local copies, waits for them, and re-layouts: 39.7 us -> 9.35 us
  starting transfers between devices: 18.5 us -> 36.1 us
    ppermute x7 -> x19, waiting for transfers between devices: 93.2 us -> 36 us  [along(): return lax.ppermute(array, axis, pairs)]
    dot_general x16 -> x0, matrix products: 39.6 us -> none  [look_block(): jnp.dot(table_rows, onehot_low, preferred_element_type=jnp.float32)]
    pallas_call x0 -> x16, Pallas kernels: none -> 31.7 us  [the longest x4 17.8 us: render(): pl.pallas_call(functools.partial(render_body, layers, rows, scale, first[...]
    select_n x38 -> x0, other arithmetic: 22.4 us -> none  [the longest x16 8.83 us: look_block(): high_digit = bin_block // low_count]
    slice x4 -> x1, local copies, waits for them, and re-layouts: 20 us -> 0.02 us  [per_device(): density[:, height - 1:, :]]
    ppermute x7 -> x19, starting transfers between devices: 18.5 us -> 36.1 us  [along(): return lax.ppermute(array, axis, pairs)]
    dynamic_update_slice x16 -> x0, local copies, waits for them, and re-layouts: 13.5 us -> none  [per_device(): entries = lax.map(look_block, bins.reshape(-1, block_size))]
    mul x4 -> x0, other arithmetic: 11.7 us -> none  [the longest x1 11.6 us: per_device(): optical = entries[3] * depth_scale]
  transfers between devices with their start and end apart: 7 -> 19, of which waited for: 3 -> 9; matrix products, arithmetic and copies ran while one was open for 45% -> 3% of each run, Pallas kernels for 0% -> 26%
where the time goes in v1:
time: 114 us; the launch traced here: 113 us
  starting transfers between devices  36.1 us (32%)
  waiting for transfers between devices  36 us (32%)
  Pallas kernels  31.7 us (28%)
  local copies, waits for them, and re-layouts  9.35 us (8%)
    ppermute x19, starting transfers between devices, along(): return lax.ppermute(array, axis, pairs)  36.1 us
    ppermute x19, waiting for transfers between devices, along(): return lax.ppermute(array, axis, pairs)  36 us
    pallas_call x4, Pallas kernels, render(): pl.pallas_call(functools.partial(render_body, layers, rows, scale, first[...  17.8 us
    pallas_call x8, Pallas kernels, small(): pl.pallas_call(body, out_shape=outs, grid_spec=pltpu.PrefetchScalarGridSp...  7.93 us
    pallas_call x4, Pallas kernels, pack(): pl.pallas_call(functools.partial(pack_body, layers, rows, first[2], secon...  6 us
    unnamed x18, local copies, waits for them, and re-layouts  5.74 us
    dynamic_slice x4, local copies, waits for them, and re-layouts, per_device(): lax.dynamic_slice(message, ((1 - side) * (layers - 1) * rows, 0), (rows,...  2.76 us
  transfers between devices with their start and end apart: 19, of which 9 were waited for; matrix products, arithmetic and copies ran while one was open for 3% of the time, Pallas kernels for 26%

profile of v1, /device:TPU:0, one launch (start us, length us, event | category | flops | bytes accessed | tf_op | source)
XLA Modules:
  0.0 113.5 jit_solution(11187583765047794960)
XLA Ops:
  0.1 1.6 %copy-done = f32[2,128,2048]{2,1,0:T(8,128)S(1)} copy-done((f32[2,128,2048]{2,1,0:T(8,128)S(1)}, f32[2,128,2048]{2,1,0:T(8,128)}, u32[]{:S(2)}) %copy-start) | copy-done | bytes 2097176
  1.7 1.6 %copy-done.2 = s32[2,128,2048]{2,1,0:T(8,128)S(1)} copy-done((s32[2,128,2048]{2,1,0:T(8,128)S(1)}, s32[2,128,2048]{2,1,0:T(8,128)}, u32[]{:S(2)}) %copy-start.2) | copy-done | bytes 2097176
  3.3 1.5 %pack.7 = f32[136,1024]{1,0:T(8,128)} custom-call(s32[2]{0:T(128)S(1)} %pad_add_fusion.1.side_ref, f32[2,128,2048]{2,1,0:T(8,128)S(1)} %copy-done, f32[2,128,2048]{2,1,0:T(8,128)S(1)} %copy-done, f32[2,128,2048]{2,1,0:T(8,128)S(1)} %copy-done, f32[2,128,2048]{2,1,0:T(8,128)S(1)} %copy-done, s32[2,128,2048]{2,1,0:T(8,128)S(1)} %copy-done.2), custom_call_target="tpu_custom_call" | custom-call | bytes 1048576 | tf_op jit(solution)/shard_map/pack/pallas_call | solution.py:207
  4.8 3.0 %collective-permute-start.15 = (f32[136,1024]{1,0:T(8,128)}, f32[136,1024]{1,0:T(8,128)}, u32[]{:S(2)}, u32[]{:S(2)}) collective-permute-start(f32[136,1024]{1,0:T(8,128)} %pack.7), channel_id=1, source_target_pairs={{0,4},{4,0},{8,12},{12,8},{16,20},{20,16},{24,28},{28,24},{1,5},{5... | collective-permute-start | bytes 1671176 | tf_op jit(solution)/shard_map/ppermute | solution.py:176
  7.7 1.5 %pack.6 = f32[136,1024]{1,0:T(8,128)} custom-call(s32[2]{0:T(128)S(1)} %pad_add_fusion.1.side_ref, f32[2,128,2048]{2,1,0:T(8,128)S(1)} %copy-done, f32[2,128,2048]{2,1,0:T(8,128)S(1)} %copy-done, f32[2,128,2048]{2,1,0:T(8,128)S(1)} %copy-done, f32[2,128,2048]{2,1,0:T(8,128)S(1)} %copy-done, s32[2,128,2048]{2,1,0:T(8,128)S(1)} %copy-done.2), custom_call_target="tpu_custom_call" | custom-call | bytes 1048576 | tf_op jit(solution)/shard_map/pack/pallas_call | solution.py:207
  9.3 1.6 %collective-permute-start.6 = (f32[2,1,2048]{2,1,0:T(1,128)S(1)}, f32[2,1,2048]{2,1,0:T(1,128)S(1)}, u32[]{:S(2)}, u32[]{:S(2)}) collective-permute-start(f32[2,1,2048]{2,1,0:T(1,128)S(1)} %get-tuple-element.37), channel_id=1, source_target_pairs={{0,1},{1,2},{2,3},{4,5},{5,6},{6,7},{8,9},{9,10},{10,11},{12,13},{... | collective-permute-start | bytes 49160 | tf_op jit(solution)/shard_map/ppermute | solution.py:176
  10.9 0.8 collective-permute-done.6.top
  11.7 1.5 %pack.5 = f32[136,1024]{1,0:T(8,128)} custom-call(s32[2]{0:T(128)S(1)} %pad_add_fusion.1.side_ref, f32[2,128,2048]{2,1,0:T(8,128)S(1)} %copy-done, f32[2,1,2048]{2,1,0:T(1,128)S(1)} %collective-permute-done.6.top, f32[2,128,2048]{2,1,0:T(8,128)S(1)} %copy-done, f32[2,128,2048]{2,1,0:T(8,128)S(1)} %copy-done, s32[2,128,2048]{2,1,0:T(8,128)S(1)} %copy-done.2), custom_call_target="tpu_custom_call" | custom-call | bytes 1048576 | tf_op jit(solution)/shard_map/pack/pallas_call | solution.py:207
  13.2 1.9 %collective-permute-start.7 = (f32[136,1024]{1,0:T(8,128)}, f32[136,1024]{1,0:T(8,128)}, u32[]{:S(2)}, u32[]{:S(2)}) collective-permute-start(f32[136,1024]{1,0:T(8,128)} %pack.5), channel_id=1, source_target_pairs={{0,4},{4,0},{8,12},{12,8},{16,20},{20,16},{24,28},{28,24},{1,5},{5... | collective-permute-start | bytes 1671176 | tf_op jit(solution)/shard_map/ppermute | solution.py:176
  15.1 1.4 %collective-permute-start = (f32[2,1,2048]{2,1,0:T(1,128)S(1)}, f32[2,1,2048]{2,1,0:T(1,128)S(1)}, u32[]{:S(2)}, u32[]{:S(2)}) collective-permute-start(f32[2,1,2048]{2,1,0:T(1,128)S(1)} %get-tuple-element.38), channel_id=1, source_target_pairs={{1,0},{2,1},{3,2},{5,4},{6,5},{7,6},{9,8},{10,9},{11,10},{13,12},{... | collective-permute-start | bytes 49160 | tf_op jit(solution)/shard_map/ppermute | solution.py:176
  16.5 3.3 %collective-permute-done.bottom = f32[2,1,2048]{2,1,0:T(1,128)S(1)} collective-permute-done((f32[2,1,2048]{2,1,0:T(1,128)S(1)}, f32[2,1,2048]{2,1,0:T(1,128)S(1)}, u32[]{:S(2)}, u32[]{:S(2)}) %collective-permute-start) | collective-permute-done | bytes 16416 | tf_op jit(solution)/shard_map/ppermute | solution.py:176
  19.7 1.5 %pack.4 = f32[136,1024]{1,0:T(8,128)} custom-call(s32[2]{0:T(128)S(1)} %pad_add_fusion.1.side_ref, f32[2,128,2048]{2,1,0:T(8,128)S(1)} %copy-done, f32[2,128,2048]{2,1,0:T(8,128)S(1)} %copy-done, f32[2,1,2048]{2,1,0:T(1,128)S(1)} %collective-permute-done.bottom, f32[2,128,2048]{2,1,0:T(8,128)S(1)} %copy-done, s32[2,128,2048]{2,1,0:T(8,128)S(1)} %copy-done.3), custom_call_target="tpu_custom_call" | custom-call | bytes 1048576 | tf_op jit(solution)/shard_map/pack/pallas_call | solution.py:207
  21.2 0.5 collective-permute-start.1
  21.7 0.8 dynamic-slice_bitcast_fusion
  22.6 1.3 %collective-permute-start.2 = (f32[128,1024]{1,0:T(8,128)}, f32[128,1024]{1,0:T(8,128)S(1)}, u32[]{:S(2)}, u32[]{:S(2)}) collective-permute-start(f32[128,1024]{1,0:T(8,128)} %dynamic-slice_bitcast_fusion), channel_id=1, source_target_pairs={{4,12},{8,0},{12,20},{16,8},{20,28},{24,16},{5,13},{9,1},{13,21},{... | collective-permute-start | bytes 1572872 | tf_op jit(solution)/shard_map/ppermute | solution.py:176
  23.9 0.9 constant_dynamic-slice_fusion
  24.8 4.6 %collective-permute-start.16 = (f32[32,1024]{1,0:T(8,128)S(1)}, f32[32,1024]{1,0:T(8,128)S(1)}, u32[]{:S(2)}, u32[]{:S(2)}) collective-permute-start(f32[32,1024]{1,0:T(8,128)S(1)} %constant_dynamic-slice_fusion), channel_id=1, source_target_pairs={{0,8},{8,16},{12,4},{16,24},{20,12},{28,20},{1,9},{9,17},{13,5},{1... | collective-permute-start | bytes 393224 | tf_op jit(solution)/shard_map/ppermute | solution.py:176
  29.4 4.0 %collective-permute-done.11.message = f32[136,1024]{1,0:T(8,128)S(1)} collective-permute-done((f32[136,1024]{1,0:T(8,128)}, f32[136,1024]{1,0:T(8,128)S(1)}, u32[]{:S(2)}, u32[]{:S(2)}) %collective-permute-start.11) | collective-permute-done | bytes 557088 | tf_op jit(solution)/shard_map/ppermute | solution.py:176
  33.3 4.0 %collective-permute-start.12 = (f32[32,1024]{1,0:T(8,128)S(1)}, f32[32,1024]{1,0:T(8,128)S(1)}, u32[]{:S(2)}, u32[]{:S(2)}) collective-permute-start(f32[32,1024]{1,0:T(8,128)S(1)} %constant_dynamic-slice_fusion.1), channel_id=1, source_target_pairs={{0,8},{8,16},{12,4},{16,24},{20,12},{28,20},{1,9},{9,17},{13,5},{1... | collective-permute-start | bytes 393224 | tf_op jit(solution)/shard_map/ppermute | solution.py:176
  37.4 8.0 %collective-permute-done.7.message = f32[136,1024]{1,0:T(8,128)} collective-permute-done((f32[136,1024]{1,0:T(8,128)}, f32[136,1024]{1,0:T(8,128)}, u32[]{:S(2)}, u32[]{:S(2)}) %collective-permute-start.7) | collective-permute-done | bytes 557088 | tf_op jit(solution)/shard_map/ppermute | solution.py:176
  45.4 0.9 constant_dynamic-slice_fusion.2
  46.3 4.0 %collective-permute-start.8 = (f32[32,1024]{1,0:T(8,128)S(1)}, f32[32,1024]{1,0:T(8,128)S(1)}, u32[]{:S(2)}, u32[]{:S(2)}) collective-permute-start(f32[32,1024]{1,0:T(8,128)S(1)} %constant_dynamic-slice_fusion.2), channel_id=1, source_target_pairs={{0,8},{8,16},{12,4},{16,24},{20,12},{28,20},{1,9},{9,17},{13,5},{1... | collective-permute-start | bytes 393224 | tf_op jit(solution)/shard_map/ppermute | solution.py:176
  50.3 6.2 %collective-permute-done.1.message = f32[136,1024]{1,0:T(8,128)} collective-permute-done((f32[136,1024]{1,0:T(8,128)}, f32[136,1024]{1,0:T(8,128)}, u32[]{:S(2)}, u32[]{:S(2)}) %collective-permute-start.1) | collective-permute-done | bytes 557088 | tf_op jit(solution)/shard_map/ppermute | solution.py:176
  56.5 0.9 constant_dynamic-slice_fusion.3
  57.4 3.7 %collective-permute-start.3 = (f32[32,1024]{1,0:T(8,128)S(1)}, f32[32,1024]{1,0:T(8,128)S(1)}, u32[]{:S(2)}, u32[]{:S(2)}) collective-permute-start(f32[32,1024]{1,0:T(8,128)S(1)} %constant_dynamic-slice_fusion.3), channel_id=1, source_target_pairs={{0,8},{8,16},{12,4},{16,24},{20,12},{28,20},{1,9},{9,17},{13,5},{1... | collective-permute-start | bytes 393224 | tf_op jit(solution)/shard_map/ppermute | solution.py:176
  61.2 1.6 %copy-done.4 = s32[2,128,2048]{2,1,0:T(8,128)S(1)} copy-done((s32[2,128,2048]{2,1,0:T(8,128)S(1)}, s32[2,128,2048]{2,1,0:T(8,128)}, u32[]{:S(2)}) %copy-start.4) | copy-done | bytes 2097176
  62.8 4.7 %render.7 = (f32[4,32,512]{2,1,0:T(8,128)S(1)}, f32[4,32,512]{2,1,0:T(8,128)}) custom-call(s32[2]{0:T(128)S(1)} %pad_add_fusion.1.side_ref, f32[4,256]{1,0:T(4,128)S(1)} %maximum_convert_fusion.table, f32[2,128,2048]{2,1,0:T(8,128)S(1)} %copy-done.1, f32[2,128,2048]{2,1,0:T(8,128)S(1)} %copy-done.1, f32[2,128,2048]{2,1,0:T(8,128)S(1)} %copy-done.1, ...), custom_call_target="tpu_custom_call" | custom-call | flops 7864320 | bytes 1310720 | tf_op jit(solution)/shard_map/render/pallas_call | solution.py:233
  67.5 1.6 %collective-permute-start.17 = (f32[4,32,512]{2,1,0:T(8,128)}, f32[4,32,512]{2,1,0:T(8,128)}, u32[]{:S(2)}, u32[]{:S(2)}) collective-permute-start(f32[4,32,512]{2,1,0:T(8,128)} %get-tuple-element.34), channel_id=1, source_target_pairs={{0,8},{4,12},{8,0},{12,4},{16,24},{20,28},{24,16},{28,20},{1,9},{5... | collective-permute-start | bytes 786440 | tf_op jit(solution)/shard_map/ppermute | solution.py:176
  69.1 3.6 %render.6 = (f32[4,32,512]{2,1,0:T(8,128)S(1)}, f32[4,32,512]{2,1,0:T(8,128)}) custom-call(s32[2]{0:T(128)S(1)} %pad_add_fusion.1.side_ref, f32[4,256]{1,0:T(4,128)S(1)} %maximum_convert_fusion.table, f32[2,128,2048]{2,1,0:T(8,128)S(1)} %copy-done.1, f32[2,128,2048]{2,1,0:T(8,128)S(1)} %copy-done.1, f32[2,128,2048]{2,1,0:T(8,128)S(1)} %copy-done.1, ...), custom_call_target="tpu_custom_call" | custom-call | flops 7864320 | bytes 1310720 | tf_op jit(solution)/shard_map/render/pallas_call | solution.py:233
  72.7 0.5 collective-permute-start.13
  73.2 4.7 %render.5 = (f32[4,32,512]{2,1,0:T(8,128)S(1)}, f32[4,32,512]{2,1,0:T(8,128)}) custom-call(s32[2]{0:T(128)S(1)} %pad_add_fusion.1.side_ref, f32[4,256]{1,0:T(4,128)S(1)} %maximum_convert_fusion.table, f32[2,128,2048]{2,1,0:T(8,128)S(1)} %copy-done.1, f32[2,1,2048]{2,1,0:T(1,128)S(1)} %collective-permute-done.6.top, f32[2,128,2048]{2,1,0:T(8,128)S(1)} %copy-done.1, ...), custom_call_target="tpu_custom_call" | custom-call | flops 7864320 | bytes 1310720 | tf_op jit(solution)/shard_map/render/pallas_call | solution.py:233
  77.9 1.6 %collective-permute-start.9 = (f32[4,32,512]{2,1,0:T(8,128)}, f32[4,32,512]{2,1,0:T(8,128)}, u32[]{:S(2)}, u32[]{:S(2)}) collective-permute-start(f32[4,32,512]{2,1,0:T(8,128)} %get-tuple-element.26), channel_id=1, source_target_pairs={{0,8},{4,12},{8,0},{12,4},{16,24},{20,28},{24,16},{28,20},{1,9},{5... | collective-permute-start | bytes 786440 | tf_op jit(solution)/shard_map/ppermute | solution.py:176
  79.4 4.7 %render.4 = (f32[4,32,512]{2,1,0:T(8,128)S(1)}, f32[4,32,512]{2,1,0:T(8,128)}) custom-call(s32[2]{0:T(128)S(1)} %pad_add_fusion.1.side_ref, f32[4,256]{1,0:T(4,128)S(1)} %maximum_convert_fusion.table, f32[2,128,2048]{2,1,0:T(8,128)S(1)} %copy-done.1, f32[2,128,2048]{2,1,0:T(8,128)S(1)} %copy-done.1, f32[2,1,2048]{2,1,0:T(1,128)S(1)} %collective-permute-done.bottom, ...), custom_call_target="tpu_custom_call" | custom-call | flops 7864320 | bytes 1310720 | tf_op jit(solution)/shard_map/render/pallas_call | solution.py:233
  84.7 0.9 copy-done.6
  85.6 1.5 %merge.11 = (f32[4,32,256]{2,1,0:T(8,128)S(1)}, f32[4,32,256]{2,1,0:T(8,128)S(1)}) custom-call(s32[2]{0:T(128)S(1)} %pad_add_fusion.bit_ref, f32[4,32,512]{2,1,0:T(8,128)S(1)} %copy-done.6, f32[4,32,512]{2,1,0:T(8,128)} %collective-permute-done.17.got), custom_call_target="tpu_custom_call" | custom-call | flops 524288 | bytes 1048576 | tf_op jit(solution)/shard_map/merge/pallas_call | solution.py:270
  87.2 2.7 %collective-permute-start.18 = (f32[4,32,256]{2,1,0:T(8,128)S(1)}, f32[4,32,256]{2,1,0:T(8,128)S(1)}, u32[]{:S(2)}, u32[]{:S(2)}) collective-permute-start(f32[4,32,256]{2,1,0:T(8,128)S(1)} %get-tuple-element.36), channel_id=1, source_target_pairs={{0,16},{4,20},{8,24},{12,28},{16,0},{20,4},{24,8},{28,12},{1,17},{... | collective-permute-start | bytes 393224 | tf_op jit(solution)/shard_map/ppermute | solution.py:176
  89.8 1.5 %merge.10 = (f32[4,32,256]{2,1,0:T(8,128)S(1)}, f32[4,32,256]{2,1,0:T(8,128)S(1)}) custom-call(s32[2]{0:T(128)S(1)} %pad_add_fusion.bit_ref, f32[4,32,512]{2,1,0:T(8,128)S(1)} %get-tuple-element.29.held, f32[4,32,512]{2,1,0:T(8,128)} %collective-permute-done.13.got), custom_call_target="tpu_custom_call" | custom-call | flops 524288 | bytes 1048576 | tf_op jit(solution)/shard_map/merge/pallas_call | solution.py:270
  91.8 1.5 %merge.9 = (f32[4,32,256]{2,1,0:T(8,128)S(1)}, f32[4,32,256]{2,1,0:T(8,128)S(1)}) custom-call(s32[2]{0:T(128)S(1)} %pad_add_fusion.bit_ref, f32[4,32,512]{2,1,0:T(8,128)S(1)} %get-tuple-element.25.held, f32[4,32,512]{2,1,0:T(8,128)} %collective-permute-done.9.got), custom_call_target="tpu_custom_call" | custom-call | flops 524288 | bytes 1048576 | tf_op jit(solution)/shard_map/merge/pallas_call | solution.py:270
  93.3 2.7 %collective-permute-start.10 = (f32[4,32,256]{2,1,0:T(8,128)S(1)}, f32[4,32,256]{2,1,0:T(8,128)S(1)}, u32[]{:S(2)}, u32[]{:S(2)}) collective-permute-start(f32[4,32,256]{2,1,0:T(8,128)S(1)} %get-tuple-element.28), channel_id=1, source_target_pairs={{0,16},{4,20},{8,24},{12,28},{16,0},{20,4},{24,8},{28,12},{1,17},{... | collective-permute-start | bytes 393224 | tf_op jit(solution)/shard_map/ppermute | solution.py:176
  96.0 0.6 merge.8
  97.0 8.4 %collective-permute-done.18.got = f32[4,32,256]{2,1,0:T(8,128)S(1)} collective-permute-done((f32[4,32,256]{2,1,0:T(8,128)S(1)}, f32[4,32,256]{2,1,0:T(8,128)S(1)}, u32[]{:S(2)}, u32[]{:S(2)}) %collective-permute-start.18) | collective-permute-done | bytes 131104 | tf_op jit(solution)/shard_map/ppermute | solution.py:176
  105.4 0.7 merge.12.rest_0_
  106.1 2.1 %collective-permute-done.14.got = f32[4,32,256]{2,1,0:T(8,128)S(1)} collective-permute-done((f32[4,32,256]{2,1,0:T(8,128)S(1)}, f32[4,32,256]{2,1,0:T(8,128)S(1)}, u32[]{:S(2)}, u32[]{:S(2)}) %collective-permute-start.14) | collective-permute-done | bytes 131104 | tf_op jit(solution)/shard_map/ppermute | solution.py:176
  108.2 0.7 merge.13.rest_0_
  108.9 2.1 %collective-permute-done.10.got = f32[4,32,256]{2,1,0:T(8,128)S(1)} collective-permute-done((f32[4,32,256]{2,1,0:T(8,128)S(1)}, f32[4,32,256]{2,1,0:T(8,128)S(1)}, u32[]{:S(2)}, u32[]{:S(2)}) %collective-permute-start.10) | collective-permute-done | bytes 131104 | tf_op jit(solution)/shard_map/ppermute | solution.py:176
  111.1 0.7 merge.14.rest_0_
  111.7 1.0 collective-permute-done.5.got
  112.8 0.7 merge.15
  (34 shorter events, 1.5 us)
Async XLA Ops:
  0.1 1.6 %copy-start = (f32[2,128,2048]{2,1,0:T(8,128)S(1)}, f32[2,128,2048]{2,1,0:T(8,128)}, u32[]{:S(2)}) copy-start(f32[2,128,2048]{2,1,0:T(8,128)} %column.15) | copy-start | bytes 6291460
  1.7 1.6 %copy-start.2 = (s32[2,128,2048]{2,1,0:T(8,128)S(1)}, s32[2,128,2048]{2,1,0:T(8,128)}, u32[]{:S(2)}) copy-start(s32[2,128,2048]{2,1,0:T(8,128)} %bins.15) | copy-start | bytes 6291460
  4.8 19.1 %collective-permute-start.15 = (f32[136,1024]{1,0:T(8,128)}, f32[136,1024]{1,0:T(8,128)}, u32[]{:S(2)}, u32[]{:S(2)}) collective-permute-start(f32[136,1024]{1,0:T(8,128)} %pack.7), channel_id=1, source_target_pairs={{0,4},{4,0},{8,12},{12,8},{16,20},{20,16},{24,28},{28,24},{1,5},{5... | collective-permute-start | bytes 1671176 | tf_op jit(solution)/shard_map/ppermute | solution.py:176
  9.2 24.1 %collective-permute-start.11 = (f32[136,1024]{1,0:T(8,128)}, f32[136,1024]{1,0:T(8,128)S(1)}, u32[]{:S(2)}, u32[]{:S(2)}) collective-permute-start(f32[136,1024]{1,0:T(8,128)} %pack.6), channel_id=1, source_target_pairs={{0,4},{4,0},{8,12},{12,8},{16,20},{20,16},{24,28},{28,24},{1,5},{5... | collective-permute-start | bytes 1671176 | tf_op jit(solution)/shard_map/ppermute | solution.py:176
  9.3 10.5 %copy-start.3 = (s32[2,128,2048]{2,1,0:T(8,128)S(1)}, s32[2,128,2048]{2,1,0:T(8,128)}, u32[]{:S(2)}) copy-start(s32[2,128,2048]{2,1,0:T(8,128)} %bins.15) | copy-start | bytes 6291460
  9.3 2.4 %collective-permute-start.6 = (f32[2,1,2048]{2,1,0:T(1,128)S(1)}, f32[2,1,2048]{2,1,0:T(1,128)S(1)}, u32[]{:S(2)}, u32[]{:S(2)}) collective-permute-start(f32[2,1,2048]{2,1,0:T(1,128)S(1)} %get-tuple-element.37), channel_id=1, source_target_pairs={{0,1},{1,2},{2,3},{4,5},{5,6},{6,7},{8,9},{9,10},{10,11},{12,13},{... | collective-permute-start | bytes 49160 | tf_op jit(solution)/shard_map/ppermute | solution.py:176
  13.2 32.2 %collective-permute-start.7 = (f32[136,1024]{1,0:T(8,128)}, f32[136,1024]{1,0:T(8,128)}, u32[]{:S(2)}, u32[]{:S(2)}) collective-permute-start(f32[136,1024]{1,0:T(8,128)} %pack.5), channel_id=1, source_target_pairs={{0,4},{4,0},{8,12},{12,8},{16,20},{20,16},{24,28},{28,24},{1,5},{5... | collective-permute-start | bytes 1671176 | tf_op jit(solution)/shard_map/ppermute | solution.py:176
  15.0 6.7 %copy-start.1 = (f32[2,128,2048]{2,1,0:T(8,128)S(1)}, f32[2,128,2048]{2,1,0:T(8,128)}, u32[]{:S(2)}) copy-start(f32[2,128,2048]{2,1,0:T(8,128)} %column.15) | copy-start | bytes 6291460
  15.1 4.7 %collective-permute-start = (f32[2,1,2048]{2,1,0:T(1,128)S(1)}, f32[2,1,2048]{2,1,0:T(1,128)S(1)}, u32[]{:S(2)}, u32[]{:S(2)}) collective-permute-start(f32[2,1,2048]{2,1,0:T(1,128)S(1)} %get-tuple-element.38), channel_id=1, source_target_pairs={{1,0},{2,1},{3,2},{5,4},{6,5},{7,6},{9,8},{10,9},{11,10},{13,12},{... | collective-permute-start | bytes 49160 | tf_op jit(solution)/shard_map/ppermute | solution.py:176
  21.2 39.9 %copy-start.8 = (bf16[256]{0:T(256)(128)(2,1)S(1)}, bf16[256]{0:T(256)(128)(2,1)}, u32[]{:S(2)}) copy-start(bf16[256]{0:T(256)(128)(2,1)} %param.7) | copy-start | bytes 1540
  21.2 39.9 %copy-start.7 = (bf16[3,256]{1,0:T(4,128)(2,1)S(1)}, bf16[3,256]{1,0:T(4,128)(2,1)}, u32[]{:S(2)}) copy-start(bf16[3,256]{1,0:T(4,128)(2,1)} %param.6) | copy-start | bytes 4612
  21.2 35.3 %collective-permute-start.1 = (f32[136,1024]{1,0:T(8,128)}, f32[136,1024]{1,0:T(8,128)}, u32[]{:S(2)}, u32[]{:S(2)}) collective-permute-start(f32[136,1024]{1,0:T(8,128)} %pack.4), channel_id=1, source_target_pairs={{0,4},{4,0},{8,12},{12,8},{16,20},{20,16},{24,28},{28,24},{1,5},{5... | collective-permute-start | bytes 1671176 | tf_op jit(solution)/shard_map/ppermute | solution.py:176
  22.6 38.6 %collective-permute-start.2 = (f32[128,1024]{1,0:T(8,128)}, f32[128,1024]{1,0:T(8,128)S(1)}, u32[]{:S(2)}, u32[]{:S(2)}) collective-permute-start(f32[128,1024]{1,0:T(8,128)} %dynamic-slice_bitcast_fusion), channel_id=1, source_target_pairs={{4,12},{8,0},{12,20},{16,8},{20,28},{24,16},{5,13},{9,1},{13,21},{... | collective-permute-start | bytes 1572872 | tf_op jit(solution)/shard_map/ppermute | solution.py:176
  24.8 36.4 %collective-permute-start.16 = (f32[32,1024]{1,0:T(8,128)S(1)}, f32[32,1024]{1,0:T(8,128)S(1)}, u32[]{:S(2)}, u32[]{:S(2)}) collective-permute-start(f32[32,1024]{1,0:T(8,128)S(1)} %constant_dynamic-slice_fusion), channel_id=1, source_target_pairs={{0,8},{8,16},{12,4},{16,24},{20,12},{28,20},{1,9},{9,17},{13,5},{1... | collective-permute-start | bytes 393224 | tf_op jit(solution)/shard_map/ppermute | solution.py:176
  33.3 35.7 %collective-permute-start.12 = (f32[32,1024]{1,0:T(8,128)S(1)}, f32[32,1024]{1,0:T(8,128)S(1)}, u32[]{:S(2)}, u32[]{:S(2)}) collective-permute-start(f32[32,1024]{1,0:T(8,128)S(1)} %constant_dynamic-slice_fusion.1), channel_id=1, source_target_pairs={{0,8},{8,16},{12,4},{16,24},{20,12},{28,20},{1,9},{9,17},{13,5},{1... | collective-permute-start | bytes 393224 | tf_op jit(solution)/shard_map/ppermute | solution.py:176
  46.3 26.9 %collective-permute-start.8 = (f32[32,1024]{1,0:T(8,128)S(1)}, f32[32,1024]{1,0:T(8,128)S(1)}, u32[]{:S(2)}, u32[]{:S(2)}) collective-permute-start(f32[32,1024]{1,0:T(8,128)S(1)} %constant_dynamic-slice_fusion.2), channel_id=1, source_target_pairs={{0,8},{8,16},{12,4},{16,24},{20,12},{28,20},{1,9},{9,17},{13,5},{1... | collective-permute-start | bytes 393224 | tf_op jit(solution)/shard_map/ppermute | solution.py:176
  57.4 22.0 %collective-permute-start.3 = (f32[32,1024]{1,0:T(8,128)S(1)}, f32[32,1024]{1,0:T(8,128)S(1)}, u32[]{:S(2)}, u32[]{:S(2)}) collective-permute-start(f32[32,1024]{1,0:T(8,128)S(1)} %constant_dynamic-slice_fusion.3), channel_id=1, source_target_pairs={{0,8},{8,16},{12,4},{16,24},{20,12},{28,20},{1,9},{9,17},{13,5},{1... | collective-permute-start | bytes 393224 | tf_op jit(solution)/shard_map/ppermute | solution.py:176
  61.2 1.6 %copy-start.4 = (s32[2,128,2048]{2,1,0:T(8,128)S(1)}, s32[2,128,2048]{2,1,0:T(8,128)}, u32[]{:S(2)}) copy-start(s32[2,128,2048]{2,1,0:T(8,128)} %bins.15) | copy-start | bytes 6291460
  67.5 5.2 %copy-start.5 = (f32[4,32,512]{2,1,0:T(8,128)}, f32[4,32,512]{2,1,0:T(8,128)S(1)}, u32[]{:S(2)}) copy-start(f32[4,32,512]{2,1,0:T(8,128)S(1)} %get-tuple-element.33.held) | copy-start | bytes 786436
  67.5 17.2 %collective-permute-start.17 = (f32[4,32,512]{2,1,0:T(8,128)}, f32[4,32,512]{2,1,0:T(8,128)}, u32[]{:S(2)}, u32[]{:S(2)}) collective-permute-start(f32[4,32,512]{2,1,0:T(8,128)} %get-tuple-element.34), channel_id=1, source_target_pairs={{0,8},{4,12},{8,0},{12,4},{16,24},{20,28},{24,16},{28,20},{1,9},{5... | collective-permute-start | bytes 786440 | tf_op jit(solution)/shard_map/ppermute | solution.py:176
  72.7 17.1 %collective-permute-start.13 = (f32[4,32,512]{2,1,0:T(8,128)}, f32[4,32,512]{2,1,0:T(8,128)}, u32[]{:S(2)}, u32[]{:S(2)}) collective-permute-start(f32[4,32,512]{2,1,0:T(8,128)} %get-tuple-element.30), channel_id=1, source_target_pairs={{0,8},{4,12},{8,0},{12,4},{16,24},{20,28},{24,16},{28,20},{1,9},{5... | collective-permute-start | bytes 786440 | tf_op jit(solution)/shard_map/ppermute | solution.py:176
  77.9 13.9 %collective-permute-start.9 = (f32[4,32,512]{2,1,0:T(8,128)}, f32[4,32,512]{2,1,0:T(8,128)}, u32[]{:S(2)}, u32[]{:S(2)}) collective-permute-start(f32[4,32,512]{2,1,0:T(8,128)} %get-tuple-element.26), channel_id=1, source_target_pairs={{0,8},{4,12},{8,0},{12,4},{16,24},{20,28},{24,16},{28,20},{1,9},{5... | collective-permute-start | bytes 786440 | tf_op jit(solution)/shard_map/ppermute | solution.py:176
  84.2 11.8 %collective-permute-start.4 = (f32[4,32,512]{2,1,0:T(8,128)}, f32[4,32,512]{2,1,0:T(8,128)S(1)}, u32[]{:S(2)}, u32[]{:S(2)}) collective-permute-start(f32[4,32,512]{2,1,0:T(8,128)} %get-tuple-element.22), channel_id=1, source_target_pairs={{0,8},{4,12},{8,0},{12,4},{16,24},{20,28},{24,16},{28,20},{1,9},{5... | collective-permute-start | bytes 786440 | tf_op jit(solution)/shard_map/ppermute | solution.py:176
  84.7 1.0 copy-start.6
  87.2 18.2 %collective-permute-start.18 = (f32[4,32,256]{2,1,0:T(8,128)S(1)}, f32[4,32,256]{2,1,0:T(8,128)S(1)}, u32[]{:S(2)}, u32[]{:S(2)}) collective-permute-start(f32[4,32,256]{2,1,0:T(8,128)S(1)} %get-tuple-element.36), channel_id=1, source_target_pairs={{0,16},{4,20},{8,24},{12,28},{16,0},{20,4},{24,8},{28,12},{1,17},{... | collective-permute-start | bytes 393224 | tf_op jit(solution)/shard_map/ppermute | solution.py:176
  91.4 16.9 %collective-permute-start.14 = (f32[4,32,256]{2,1,0:T(8,128)S(1)}, f32[4,32,256]{2,1,0:T(8,128)S(1)}, u32[]{:S(2)}, u32[]{:S(2)}) collective-permute-start(f32[4,32,256]{2,1,0:T(8,128)S(1)} %get-tuple-element.32), channel_id=1, source_target_pairs={{0,16},{4,20},{8,24},{12,28},{16,0},{20,4},{24,8},{28,12},{1,17},{... | collective-permute-start | bytes 393224 | tf_op jit(solution)/shard_map/ppermute | solution.py:176
  93.3 17.7 %collective-permute-start.10 = (f32[4,32,256]{2,1,0:T(8,128)S(1)}, f32[4,32,256]{2,1,0:T(8,128)S(1)}, u32[]{:S(2)}, u32[]{:S(2)}) collective-permute-start(f32[4,32,256]{2,1,0:T(8,128)S(1)} %get-tuple-element.28), channel_id=1, source_target_pairs={{0,16},{4,20},{8,24},{12,28},{16,0},{20,4},{24,8},{28,12},{1,17},{... | collective-permute-start | bytes 393224 | tf_op jit(solution)/shard_map/ppermute | solution.py:176
  96.6 16.2 %collective-permute-start.5 = (f32[4,32,256]{2,1,0:T(8,128)S(1)}, f32[4,32,256]{2,1,0:T(8,128)S(1)}, u32[]{:S(2)}, u32[]{:S(2)}) collective-permute-start(f32[4,32,256]{2,1,0:T(8,128)S(1)} %get-tuple-element.24), channel_id=1, source_target_pairs={{0,16},{4,20},{8,24},{12,28},{16,0},{20,4},{24,8},{28,12},{1,17},{... | collective-permute-start | bytes 393224 | tf_op jit(solution)/shard_map/ppermute | solution.py:176

commit v2 on v0

v2 whole, which is shorter than its diff:
```python
import functools

import jax
import jax.numpy as jnp
from jax import lax
from jax.experimental import pallas as pl
from jax.experimental.pallas import tpu as pltpu
from jax.sharding import PartitionSpec as P

LANES = 128
VMEM_LIMIT = 12 * 1024 * 1024
FLOPS_PER_US = 1.15e9


def seed_token(token):
    token[...] = jnp.zeros_like(token)


def edge_column(side, column, layers, rows):
    lane = lax.broadcasted_iota(jnp.int32, (8, LANES), 1)
    edges = jnp.zeros((8, LANES), jnp.float32)
    for layer in range(layers):
        for step in range(rows // 8):
            block = column(layer, step * 8)
            edge = jnp.where(side == 0, block[:, LANES - 1 :], block[:, :1])
            edges = jnp.where(lane == layer * (rows // 8) + step, edge, edges)
    return edges


def store_edges(out, base, edges):
    out[base + 4 : base + 8, :] = jnp.zeros((4, out.shape[1]), jnp.float32)
    out[base + 4 : base + 8, :LANES] = edges[:4]
    out[base + 4 : base + 8, LANES : 2 * LANES] = edges[4:]


def position():
    slab = lax.axis_index("depth")
    return lambda r: jnp.right_shift(slab, r) & 1


def start_all(pairs, sems):
    copies = [pltpu.make_async_copy(source, target, sems.at[n]) for n, (source, target) in enumerate(pairs)]
    for copy in copies:
        copy.start()
    return copies


def pack_body(start, rows, ranges, density, bins, *rest):
    out, token, entry, column, above, below, sems = rest[-7:]
    seed_token(token)
    side = position()(0)
    layers, height, width = density.shape
    half = width // 2
    theirs = pl.ds(pl.multiple_of((1 - side) * half, LANES), half)
    border = pl.ds(pl.multiple_of(half - LANES + side * LANES, LANES), LANES)
    pairs = [(bins.at[:, start : start + rows, theirs], entry)]
    base = 0
    for begin, size in ranges:
        pairs.append((density.at[side * (layers - 1), begin : begin + size, theirs], out.at[base : base + size, :]))
        base += size
    for layer in range(layers - 1):
        pairs.append((density.at[1 - side + layer, start : start + rows, theirs], out.at[base : base + rows, :]))
        base += rows
    pairs.append((density.at[:, start : start + rows, border], column))
    if start > 0:
        pairs.append((density.at[:, start - 8 : start, theirs], above))
    if start + rows < height:
        pairs.append((density.at[:, start + rows : start + rows + 8, theirs], below))
    copies = start_all(pairs, sems)
    for copy in copies:
        copy.wait()
    for layer in range(layers):
        out[base : base + rows, :] = entry[layer].astype(jnp.float32)
        base += rows
    for layer in range(layers):
        before = above[layer, 7:8, :] if start > 0 else rest[0][layer, 0:1, theirs]
        after = below[layer, 0:1, :] if start + rows < height else rest[1][layer, 0:1, theirs]
        out[base + 2 * layer : base + 2 * layer + 1, :] = before
        out[base + 2 * layer + 1 : base + 2 * layer + 2, :] = after
    store_edges(out, base, edge_column(side, lambda layer, row: column[layer, row : row + 8, :], layers, rows))


def packed_table(table, lookup):
    red, green, blue = ((table[c : c + 1, :] * 2048.0).astype(jnp.int32) for c in range(3))
    absorbed = (table[3:4, :] * 4096.0).astype(jnp.int32)
    for word, value in enumerate((red * 4096 + green, blue * 131072 + absorbed)):
        for part in range(2):
            lookup[2 * word + part] = jnp.broadcast_to(value[:, part * LANES : (part + 1) * LANES], (8, LANES))


def render_body(start, rows, skip, offset, scale, table, density, bins, direct, face, message, passed, *rest):
    kept, sent, token, cells, ends, entry, rgbt, lookup, sems = rest[-9:]
    seed_token(token)
    bits = position()
    side, bit = bits(0), bits(1)
    layers, height, width = density.shape
    half = width // 2
    tiles = half // LANES
    deep = 2 * layers
    inner = layers - 1
    mine = side * layers
    other = (1 - side) * layers
    ours = pl.ds(pl.multiple_of(side * half, LANES), half)
    border = pl.ds(pl.multiple_of(half - side * LANES, LANES), LANES)
    body = pl.ds(8, rows)
    top = max(start - 8, 0)
    bottom = min(start + rows + 8, height)
    copies = start_all(
        [
            (density.at[:, top:bottom, ours], cells.at[pl.ds(1 + mine, layers), pl.ds(8 + top - start, bottom - top), :]),
            (bins.at[:, start : start + rows, ours], entry.at[pl.ds(mine, layers)]),
            (density.at[:, start : start + rows, border], ends.at[1 - side, pl.ds(mine, layers)]),
            (direct.at[start : start + rows, :], cells.at[(1 - side) * (deep + 1), body, :]),
        ],
        sems,
    )
    packed_table(table, lookup)
    base = skip + (inner + layers) * rows
    cells[side * (deep + 1), body, :] = passed[offset : offset + rows, :]
    edges = jnp.concatenate([message[base + 4 : base + 8, :LANES], message[base + 4 : base + 8, LANES : 2 * LANES]], 0)
    ends[side] = jnp.zeros_like(ends[side])
    cells[1 + other + (1 - side) * inner, body, :] = face[offset : offset + rows, :]
    for layer in range(inner):
        cells[1 + other + side + layer, body, :] = message[skip + layer * rows : skip + (layer + 1) * rows, :]
    for layer in range(layers):
        if start == 0:
            cells[1 + mine + layer, 7:8, :] = rest[0][layer, 0:1, ours]
        if start + rows == height:
            cells[1 + mine + layer, 8 + rows : 9 + rows, :] = rest[1][layer, 0:1, ours]
        cells[1 + other + layer, 7:8, :] = message[base + 2 * layer : base + 2 * layer + 1, :]
        cells[1 + other + layer, 8 + rows : 9 + rows, :] = message[base + 2 * layer + 1 : base + 2 * layer + 2, :]
        entry[other + layer] = message[skip + (inner + layer) * rows : skip + (inner + layer + 1) * rows, :].astype(jnp.int32)
        for step in range(rows // 8):
            place = layer * (rows // 8) + step
            ends[1 - side, other + layer, step * 8 : step * 8 + 8, :] = jnp.broadcast_to(edges[:, place : place + 1], (8, LANES))
    for copy in copies:
        copy.wait()
    lane = lax.broadcasted_iota(jnp.int32, (8, LANES), 1)
    line = lax.broadcasted_iota(jnp.int32, (8, LANES), 0)

    def strip(step, carry):
        row = pl.multiple_of(step * 8, 8)
        here = pl.ds(row, 8)

        def tile_of(layer, tile):
            if tile < 0:
                return ends[0, layer, here, :]
            if tile == tiles:
                return ends[1, layer, here, :]
            return cells[1 + layer, pl.ds(row + 8, 8), tile * LANES : (tile + 1) * LANES]

        for tile in range(tiles):
            span = slice(tile * LANES, (tile + 1) * LANES)
            through = None
            total = None
            for layer in range(deep):
                before = cells[layer, pl.ds(row + 8, 8), span]
                after = cells[layer + 2, pl.ds(row + 8, 8), span]
                cell = tile_of(layer, tile)
                up = pltpu.roll(jnp.where(line == 7, cells[1 + layer, here, span], cell), 1, 0)
                down = pltpu.roll(jnp.where(line == 0, cells[1 + layer, pl.ds(row + 16, 8), span], cell), 7, 0)
                left = pltpu.roll(jnp.where(lane == LANES - 1, tile_of(layer, tile - 1), cell), 1, 1)
                right = pltpu.roll(jnp.where(lane == 0, tile_of(layer, tile + 1), cell), LANES - 1, 1)
                gx = after - before
                gy = down - up
                gz = right - left
                lit = jnp.abs((0.336 / 2048) * gx + (0.42 / 2048) * gy + (0.448 / 2048) * gz)
                shade = 0.3 / 2048 + lit * lax.rsqrt(gx * gx + gy * gy + gz * gz + 4.0)
                index = entry[layer, here, span]
                low_index = index & (LANES - 1)
                upper = index >= LANES
                words = []
                for word in range(2):
                    first = jnp.take_along_axis(lookup[2 * word], low_index, axis=1, mode="promise_in_bounds")
                    second = jnp.take_along_axis(lookup[2 * word + 1], low_index, axis=1, mode="promise_in_bounds")
                    words.append(jnp.where(upper, second, first))
                colour = [(words[0] >> 12).astype(jnp.float32), (words[0] & 4095).astype(jnp.float32), (words[1] >> 17).astype(jnp.float32)]
                passing = jnp.exp2((words[1] & 131071).astype(jnp.float32) * (-scale * 1.4426950408889634 / 4096))
                if layer == 0:
                    weight = shade * (1.0 - passing)
                    total = [weight * colour[c] for c in range(3)]
                    through = passing
                else:
                    weight = shade * (through * (1.0 - passing))
                    total = [total[c] + weight * colour[c] for c in range(3)]
                    through = through * passing
            which = jnp.where(bit == 0, tile // (tiles // 2), 1 - tile // (tiles // 2))
            place = slice((tile % (tiles // 2)) * LANES, (tile % (tiles // 2) + 1) * LANES)
            for c, value in enumerate(total + [through]):
                rgbt[which, c, here, place] = value
        return carry

    lax.fori_loop(0, rows // 8, strip, 0)
    kept[...] = rgbt[0]
    sent[...] = rgbt[1]


def merged_of(behind, held, got):
    mine = [held[c] for c in range(4)]
    theirs = [got[c] for c in range(4)]
    front = [jnp.where(behind, b, a) for a, b in zip(mine, theirs)]
    back = [jnp.where(behind, a, b) for a, b in zip(mine, theirs)]
    return [front[c] + front[3] * back[c] for c in range(3)] + [front[3] * back[3]]


def swap_body(count, joined, r, *rest):
    kept, sent, token = rest[-3:]
    seed_token(token)
    width = kept.shape[2]
    bits = position()
    upper = bits(r + 1) == 1
    row = 0
    for held, got in zip(rest[2 * count : 2 * count + joined], rest[2 * count + joined : 2 * count + 2 * joined]):
        rows = held.shape[1]
        kept[:, row : row + rows, :] = held[...]
        sent[:, row : row + rows, :] = got[...]
        row += rows
    for held, got in zip(rest[:count], rest[count : 2 * count]):
        rows = held.shape[1]
        for c, value in enumerate(merged_of(bits(r) == 1, held, got)):
            kept[c, row : row + rows, :] = jnp.where(upper, value[:, width:], value[:, :width])
            sent[c, row : row + rows, :] = jnp.where(upper, value[:, :width], value[:, width:])
        row += rows


def last_body(ranges, r, held, got, *rest):
    out, token, done, sems = rest[-4:]
    seed_token(token)
    values = merged_of(position()(r) == 1, held, got)
    for c in range(3):
        done[c] = values[c]
    done[3] = 1.0 - values[3]
    row = 0
    copies = []
    for number, (start, rows) in enumerate(ranges):
        copies.append(pltpu.make_async_copy(done.at[:, row : row + rows, :], out.at[:, start : start + rows, :], sems.at[number]))
        copies[-1].start()
        row += rows
    for copy in copies:
        copy.wait()


def split_off(cells, bit):
    width = cells.shape[2] // 2
    low, high = cells[:, :, :width], cells[:, :, width:]
    return jnp.where(bit == 1, high, low), jnp.where(bit == 1, low, high)


def per_device(density, bins, colors, extinction, *, chunks, steps, costs, far):
    volume = pltpu.with_memory_space_constraint(density, pltpu.HBM)
    entries = pltpu.with_memory_space_constraint(bins, pltpu.HBM)
    layers, height, width = density.shape
    slabs = lax.axis_size("depth")
    tile_count = lax.axis_size("tile")
    scale = 0.6 / (layers * slabs)
    half = width // 2
    deep = 2 * layers
    rounds = slabs.bit_length() - 1
    slab = lax.axis_index("depth")
    bits = [jnp.right_shift(slab, r) & 1 for r in range(rounds)]
    side = bits[0]
    table = jnp.concatenate([colors, extinction[None, :]], 0).astype(jnp.float32)
    swaps = [[(i, i ^ (1 << r)) for i in range(slabs)] for r in range(rounds)]
    onward = [(i, i + 2) if i % 2 else (i, i - 2) for i in range(slabs)]
    onward = [(i, j) for i, j in onward if 0 <= j < slabs]
    backward = [(i, i - 2) if i % 2 else (i, i + 2) for i in range(slabs)]
    backward = [(i, j) for i, j in backward if 0 <= j < slabs]
    vmem = pl.BlockSpec(memory_space=pltpu.VMEM)
    hbm = pl.BlockSpec(memory_space=pltpu.HBM)
    anywhere = pl.BlockSpec(memory_space=pl.ANY)
    last = []

    def call(body, operands, specs, outs, out_specs, name, micros, scratch=(), aliases=None):
        results = pl.pallas_call(
            body,
            out_shape=[*outs, jax.ShapeDtypeStruct((8, LANES), jnp.float32)],
            in_specs=[*specs, *[anywhere] * len(last)],
            out_specs=[*out_specs, vmem],
            scratch_shapes=scratch,
            compiler_params=pltpu.CompilerParams(vmem_limit_bytes=VMEM_LIMIT),
            input_output_aliases=aliases or {},
            cost_estimate=pl.CostEstimate(flops=int(micros * FLOPS_PER_US), bytes_accessed=1024, transcendentals=0),
            name=name,
        )(*operands, *last)
        last[:] = [results[-1]]
        return results[:-1]

    def after_last(array):
        return lax.optimization_barrier((array, *last))[0] if last else array

    messages = []
    faces = {}

    def send_message(number):
        start, rows, ranges = chunks[number]
        count = sum(size for _, size in ranges)
        shape = jax.ShapeDtypeStruct((count + (2 * layers - 1) * rows + 8, half), jnp.float32)
        scratch = [
            pltpu.VMEM((layers, rows, half), jnp.int32),
            pltpu.VMEM((layers, rows, LANES), jnp.float32),
            pltpu.VMEM((layers, 8, half), jnp.float32),
            pltpu.VMEM((layers, 8, half), jnp.float32),
            pltpu.SemaphoreType.DMA((len(ranges) + layers + 3,)),
        ]
        beyond = [from_above, from_below] if start == 0 or start + rows == height else []
        last.extend([from_above, from_below] if number == 2 else [])
        body = functools.partial(pack_body, start, rows, ranges)
        specs = [hbm, hbm] + [vmem] * len(beyond)
        packed = call(body, [*((volume, entries) if number < far else (density, bins)), *beyond], specs, [shape], [vmem], "pack", costs[0], scratch)[0]
        message = lax.ppermute(packed, "depth", swaps[0])
        messages.append(message)
        if ranges:
            passed = lax.ppermute(message[:count], "depth", backward)
            offset = 0
            for begin, size in ranges:
                faces[begin] = (offset, message, passed)
                offset += size

    def render(number):
        start, rows, ranges = chunks[number]
        offset, face, passed = faces[start]
        skip = sum(size for _, size in ranges)
        out = jax.ShapeDtypeStruct((4, rows, half // 2), jnp.float32)
        beyond = [from_above, from_below] if start == 0 or start + rows == height else []
        return call(
            functools.partial(render_body, start, rows, skip, offset, scale),
            [table, *((volume, entries) if far > 9 else (density, bins)), direct, face, messages[number], passed, *beyond],
            [vmem, hbm, hbm, anywhere, vmem, vmem, vmem] + [vmem] * len(beyond),
            [out, out],
            [vmem, vmem],
            "render",
            costs[1] * (0.3 + rows / 21),
            [
                pltpu.VMEM((deep + 2, rows + 16, half), jnp.float32),
                pltpu.VMEM((2, deep, rows, LANES), jnp.float32),
                pltpu.VMEM((deep, rows, half), jnp.int32),
                pltpu.VMEM((2, 4, rows, half // 2), jnp.float32),
                pltpu.VMEM((4, 8, LANES), jnp.int32),
                pltpu.SemaphoreType.DMA((4,)),
            ],
        )

    image = None
    parts = {}

    def land(entries, send=True, ready=()):
        nonlocal image
        r = entries[0][1]
        ranges = sum((entry[0] for entry in entries), [])
        kepts = [entry[2] for entry in entries]
        gots = [entry[3] for entry in entries]
        ranges = sum((entry[0] for entry in ready), []) + ranges
        rows = sum(size for _, size in ranges)
        cols = kepts[0].shape[2]
        if r == rounds - 1 and cols % LANES == 0:
            image = call(
                functools.partial(last_body, ranges, r),
                [kepts[0], gots[0]] + ([image] if image is not None else []),
                [vmem, vmem] + ([hbm] if image is not None else []),
                [jax.ShapeDtypeStruct((4, height, cols), jnp.float32)],
                [hbm],
                "finish",
                costs[3],
                [pltpu.VMEM((4, rows, cols), jnp.float32), pltpu.SemaphoreType.DMA((len(ranges),))],
                aliases={2: 0} if image is not None else None,
            )[0]
            return None
        if r < rounds - 1 and cols % (2 * LANES) == 0:
            out = jax.ShapeDtypeStruct((4, rows, cols // 2), jnp.float32)
            kept, sent = call(
                functools.partial(swap_body, len(entries), len(ready), r),
                [*kepts, *gots, *[entry[2] for entry in ready], *[entry[3] for entry in ready]],
                [vmem] * (2 * len(entries) + 2 * len(ready)),
                [out, out],
                [vmem, vmem],
                "merge",
                costs[2],
            )
        else:
            values = jnp.stack(merged_of(bits[r] == 1, jnp.concatenate(kepts, 1), jnp.concatenate(gots, 1)))
            if r == rounds - 1:
                values = jnp.concatenate([values[:3], 1.0 - values[3:]], 0)
                for start, size in ranges:
                    parts[start] = values[:, :size]
                    values = values[:, size:]
                return None
            kept, sent = split_off(values, bits[r + 1])
            kept, sent = (jnp.concatenate([*[entry[n] for entry in ready], part], 1) for n, part in ((2, kept), (3, sent)))
        if not send:
            return (ranges, r + 1, kept, sent)
        return (ranges, r + 1, kept, lax.ppermute(sent, "depth", swaps[r + 1]))

    flying = {}
    held = []
    for kind, number in steps:
        if kind == "pack":
            send_message(number)
        elif kind == "edges":
            near = after_last(density)
            from_above = lax.ppermute(near[:, height - 1 :, :], "tile", [(i, i + 1) for i in range(tile_count - 1)])
            from_below = lax.ppermute(near[:, :1, :], "tile", [(i + 1, i) for i in range(tile_count - 1)])
        elif kind == "outer":
            outer = lax.dynamic_slice(after_last(density), (side * (layers - 1), 0, side * half), (1, height, half))[0]
            direct = lax.ppermute(outer, "depth", onward)
        elif kind == "wait":
            last.extend([from_above, from_below])
        elif kind == "render":
            start, rows, _ = chunks[number]
            kept, sent = render(number)
            flying[number] = ([(start, rows)], 1, kept, lax.ppermute(sent, "depth", swaps[1]))
        elif kind == "keep":
            held.append(land([flying.pop(number)], send=False))
        else:
            flying[number] = land([flying[number]], ready=held if flying[number][1] < rounds - 1 else ())
            held = held if flying[number] is None else []
    while any(flying.values()):
        for number in list(flying):
            if flying[number]:
                flying[number] = land([flying[number]])
    if image is None:
        image = jnp.concatenate([parts[start] for start in sorted(parts)], 1)
    return image


def plan(height):
    unit = height // 16
    chunks = [(start * unit, rows * unit, [(s * unit, r * unit) for s, r in ranges]) for start, rows, ranges in [(2, 2, [(4, 4), (2, 2)]), (4, 4, [(8, 4), (12, 4), (0, 2)]), (8, 4, []), (12, 4, []), (0, 2, [])]]
    steps = ['p0', 'o0', 'p1', 'e0', 'p2', 'r0', 'p3', 'k0', 'r1', 'p4', 'r2', 'l1', 'r3', 'l2', 'r4', 'l1', 'l3', 'l2', 'l4', 'l3', 'l4']
    names = {"p": "pack", "r": "render", "l": "land", "e": "edges", "o": "outer", "w": "wait", "k": "keep"}
    return dict(far=1, costs=(0.4, 1.0, 0.1, 0.7), chunks=chunks, steps=[(names[s[0]], int(s[1:])) for s in steps])


def solution(mesh):
    def device(density, bins, colors, extinction):
        return per_device(density, bins, colors, extinction, **plan(density.shape[1]))

    return jax.shard_map(
        device,
        mesh=mesh,
        in_specs=(P("depth", "tile", None), P("depth", "tile", None), P(), P()),
        out_specs=P(None, "tile", "depth"),
        check_vma=False,
    )
```

time: 243 us -> 76.9 us (0.32)
  waiting for transfers between devices: 93.2 us -> 15.9 us
  other arithmetic: 51.2 us -> 0.01 us
  matrix products: 39.6 us -> 0 us
  local copies, waits for them, and re-layouts: 39.7 us -> 2.8 us
  starting transfers between devices: 18.5 us -> 42.3 us
  Pallas kernels: 0 us -> 15.3 us
    ppermute x7 -> x19, waiting for transfers between devices: 93.2 us -> 15.9 us  [the longest x5 7.65 us: send_message(): message = lax.ppermute(packed, 'depth', swaps[0])]
    dot_general x16 -> x0, matrix products: 39.6 us -> none  [look_block(): jnp.dot(table_rows, onehot_low, preferred_element_type=jnp.float32)]
    ppermute x7 -> x19, starting transfers between devices: 18.5 us -> 42.3 us  [the longest x5 11.8 us: per_device(): lax.ppermute(sent, 'depth', swaps[1])]
    select_n x38 -> x0, other arithmetic: 22.4 us -> none  [the longest x16 8.83 us: look_block(): high_digit = bin_block // low_count]
    slice x4 -> x3, local copies, waits for them, and re-layouts: 20 us -> 0.06 us  [the longest x2 0.04 us: send_message(): passed = lax.ppermute(message[:count], 'depth', backward)]
    pallas_call x0 -> x19, Pallas kernels: none -> 15.3 us  [call(): pl.pallas_call(body, out_shape=[*outs, jax.ShapeDtypeStruct((8, LANES), j...]
    dynamic_update_slice x16 -> x0, local copies, waits for them, and re-layouts: 13.5 us -> none  [per_device(): entries = lax.map(look_block, bins.reshape(-1, block_size))]
    mul x4 -> x0, other arithmetic: 11.7 us -> none  [the longest x1 11.6 us: per_device(): optical = entries[3] * depth_scale]
  transfers between devices with their start and end apart: 7 -> 19, of which waited for: 3 -> 7; matrix products, arithmetic and copies ran while one was open for 45% -> 0% of each run, Pallas kernels for 0% -> 16%
where the time goes in v2:
time: 76.9 us; the launch traced here: 76.6 us
  starting transfers between devices  42.3 us (55%)
  waiting for transfers between devices  15.9 us (21%)
  Pallas kernels  15.3 us (20%)
  local copies, waits for them, and re-layouts  2.8 us (4%)
    pallas_call x19, Pallas kernels, call(): pl.pallas_call(body, out_shape=[*outs, jax.ShapeDtypeStruct((8, LANES), j...  15.3 us
    ppermute x5, starting transfers between devices, per_device(): lax.ppermute(sent, 'depth', swaps[1])  11.8 us
    ppermute x4, starting transfers between devices, land(): return (ranges, r + 1, kept, lax.ppermute(sent, 'depth', swaps[r + 1]))  9.94 us
    ppermute x2, starting transfers between devices, send_message(): passed = lax.ppermute(message[:count], 'depth', backward)  8.07 us
    ppermute x5, waiting for transfers between devices, send_message(): message = lax.ppermute(packed, 'depth', swaps[0])  7.65 us
    ppermute x5, starting transfers between devices, send_message(): message = lax.ppermute(packed, 'depth', swaps[0])  6.97 us
    ppermute x5, waiting for transfers between devices, per_device(): lax.ppermute(sent, 'depth', swaps[1])  3.99 us
    ppermute x4, waiting for transfers between devices, land(): return (ranges, r + 1, kept, lax.ppermute(sent, 'depth', swaps[r + 1]))  3.41 us
  transfers between devices with their start and end apart: 19, of which 7 were waited for; matrix products, arithmetic and copies ran while one was open for 0% of the time, Pallas kernels for 16%

profile of v2, /device:TPU:0, one launch (start us, length us, event | category | flops | bytes accessed | tf_op | source)
XLA Modules:
  0.0 76.6 jit_solution(8695911212312128256)
XLA Ops:
  0.0 1.4 %pack.5 = (f32[104,1024]{1,0:T(8,128)S(1)}, f32[8,128]{1,0:T(8,128)S(1)}) custom-call(f32[2,128,2048]{2,1,0:T(8,128)} %density.19, s32[2,128,2048]{2,1,0:T(8,128)} %bins.19), custom_call_target="tpu_custom_call" | custom-call | flops 460000000 | bytes 1024 | tf_op jit(solution)/shard_map/pack/pallas_call | solution.py:274
  1.4 3.0 %collective-permute-start.4 = (f32[104,1024]{1,0:T(8,128)S(1)}, f32[104,1024]{1,0:T(8,128)S(1)}, u32[]{:S(2)}, u32[]{:S(2)}) collective-permute-start(f32[104,1024]{1,0:T(8,128)S(1)} %get-tuple-element.59), channel_id=1, source_target_pairs={{0,4},{4,0},{8,12},{12,8},{16,20},{20,16},{24,28},{28,24},{1,5},{5... | collective-permute-start | bytes 1277960 | tf_op jit(solution)/shard_map/ppermute | solution.py:310
  4.5 1.3 %collective-permute-start = (f32[128,1024]{1,0:T(8,128)S(1)}, f32[128,1024]{1,0:T(8,128)S(1)}, u32[]{:S(2)}, u32[]{:S(2)}) collective-permute-start(f32[128,1024]{1,0:T(8,128)S(1)} %dynamic-slice_bitcast_fusion), channel_id=1, source_target_pairs={{4,12},{8,0},{12,20},{16,8},{20,28},{24,16},{5,13},{9,1},{13,21},{... | collective-permute-start | bytes 1572872 | tf_op jit(solution)/shard_map/ppermute | solution.py:404
  5.8 0.0 copy-start.1
  5.8 1.6 %copy-done.1 = s32[2,128,2048]{2,1,0:T(8,128)S(1)} copy-done((s32[2,128,2048]{2,1,0:T(8,128)S(1)}, s32[2,128,2048]{2,1,0:T(8,128)}, u32[]{:S(2)}) %copy-start.1) | copy-done | bytes 2097176
  7.4 0.5 pack.6
  8.0 2.8 %collective-permute-start.1 = (f32[184,1024]{1,0:T(8,128)S(1)}, f32[184,1024]{1,0:T(8,128)S(1)}, u32[]{:S(2)}, u32[]{:S(2)}) collective-permute-start(f32[184,1024]{1,0:T(8,128)S(1)} %get-tuple-element.56), channel_id=1, source_target_pairs={{0,4},{4,0},{8,12},{12,8},{16,20},{20,16},{24,28},{28,24},{1,5},{5... | collective-permute-start | bytes 2261000 | tf_op jit(solution)/shard_map/ppermute | solution.py:310
  10.8 4.4 %collective-permute-done.4.face.message = f32[104,1024]{1,0:T(8,128)S(1)} collective-permute-done((f32[104,1024]{1,0:T(8,128)S(1)}, f32[104,1024]{1,0:T(8,128)S(1)}, u32[]{:S(2)}, u32[]{:S(2)}) %collective-permute-start.4) | collective-permute-done | bytes 426016 | tf_op jit(solution)/shard_map/ppermute | solution.py:310
  15.1 4.0 %collective-permute-start.5 = (f32[48,1024]{1,0:T(8,128)S(1)}, f32[48,1024]{1,0:T(8,128)S(1)}, u32[]{:S(2)}, u32[]{:S(2)}) collective-permute-start(f32[48,1024]{1,0:T(8,128)S(1)} %slice.16), channel_id=1, source_target_pairs={{0,8},{8,16},{12,4},{16,24},{20,12},{28,20},{1,9},{9,17},{13,5},{1... | collective-permute-start | bytes 589832 | tf_op jit(solution)/shard_map/ppermute | solution.py:313
  19.2 1.3 %collective-permute-start.3 = (f32[2,1,2048]{2,1,0:T(1,128)S(1)}, f32[2,1,2048]{2,1,0:T(1,128)S(1)}, u32[]{:S(2)}, u32[]{:S(2)}) collective-permute-start(f32[2,1,2048]{2,1,0:T(1,128)S(1)} %get-tuple-element.103), channel_id=1, source_target_pairs={{1,0},{2,1},{3,2},{5,4},{6,5},{7,6},{9,8},{10,9},{11,10},{13,12},{... | collective-permute-start | bytes 49160 | tf_op jit(solution)/shard_map/ppermute | solution.py:401
  20.5 3.0 %collective-permute-start.2 = (f32[2,1,2048]{2,1,0:T(1,128)S(1)}, f32[2,1,2048]{2,1,0:T(1,128)S(1)}, u32[]{:S(2)}, u32[]{:S(2)}) collective-permute-start(f32[2,1,2048]{2,1,0:T(1,128)S(1)} %get-tuple-element.104), channel_id=1, source_target_pairs={{0,1},{1,2},{2,3},{4,5},{5,6},{6,7},{8,9},{9,10},{10,11},{12,13},{... | collective-permute-start | bytes 49160 | tf_op jit(solution)/shard_map/ppermute | solution.py:400
  23.6 0.8 collective-permute-done.2.rest_1_.rest_0_
  24.4 0.4 pack.7
  24.8 0.1 collective-permute-start.9
  24.9 1.2 %render.5 = (f32[4,16,512]{2,1,0:T(8,128)S(1)}, f32[4,16,512]{2,1,0:T(8,128)S(1)}, f32[8,128]{1,0:T(8,128)S(1)}) custom-call(f32[4,256]{1,0:T(4,128)S(1)} %maximum_convert_fusion.table, f32[2,128,2048]{2,1,0:T(8,128)S(1)} %copy-done, s32[2,128,2048]{2,1,0:T(8,128)S(1)} %copy-done.1, f32[128,1024]{1,0:T(8,128)S(1)} %collective-permute-done.direct, ...), custom_call_target="tpu_custom_call" | custom-call | flops 1221190528 | bytes 1024 | tf_op jit(solution)/shard_map/render/pallas_call | solution.py:274
  26.0 2.0 %collective-permute-start.6 = (f32[4,16,512]{2,1,0:T(8,128)S(1)}, f32[4,16,512]{2,1,0:T(8,128)S(1)}, u32[]{:S(2)}, u32[]{:S(2)}) collective-permute-start(f32[4,16,512]{2,1,0:T(8,128)S(1)} %get-tuple-element.62), channel_id=1, source_target_pairs={{0,8},{4,12},{8,0},{12,4},{16,24},{20,28},{24,16},{28,20},{1,9},{5... | collective-permute-start | bytes 393224 | tf_op jit(solution)/shard_map/ppermute | solution.py:410
  28.0 3.3 %collective-permute-done.1.message.face = f32[184,1024]{1,0:T(8,128)S(1)} collective-permute-done((f32[184,1024]{1,0:T(8,128)S(1)}, f32[184,1024]{1,0:T(8,128)S(1)}, u32[]{:S(2)}, u32[]{:S(2)}) %collective-permute-start.1) | collective-permute-done | bytes 753696 | tf_op jit(solution)/shard_map/ppermute | solution.py:310
  31.3 4.0 %collective-permute-start.8 = (f32[80,1024]{1,0:T(8,128)S(1)}, f32[80,1024]{1,0:T(8,128)S(1)}, u32[]{:S(2)}, u32[]{:S(2)}) collective-permute-start(f32[80,1024]{1,0:T(8,128)S(1)} %slice.17), channel_id=1, source_target_pairs={{0,8},{8,16},{12,4},{16,24},{20,12},{28,20},{1,9},{9,17},{13,5},{1... | collective-permute-start | bytes 983048 | tf_op jit(solution)/shard_map/ppermute | solution.py:313
  35.4 0.0 copy-start.2
  35.4 0.3 pack.8
  35.7 0.1 collective-permute-start.11
  35.8 1.1 %copy-done.2 = s32[2,128,2048]{2,1,0:T(8,128)S(1)} copy-done((s32[2,128,2048]{2,1,0:T(8,128)S(1)}, s32[2,128,2048]{2,1,0:T(8,128)}, u32[]{:S(2)}) %copy-start.2) | copy-done | bytes 2097176
  36.9 2.1 %render.6 = (f32[4,32,512]{2,1,0:T(8,128)S(1)}, f32[4,32,512]{2,1,0:T(8,128)S(1)}, f32[8,128]{1,0:T(8,128)S(1)}) custom-call(f32[4,256]{1,0:T(4,128)S(1)} %maximum_convert_fusion.table, f32[2,128,2048]{2,1,0:T(8,128)S(1)} %copy-done, s32[2,128,2048]{2,1,0:T(8,128)S(1)} %copy-done.2, f32[128,1024]{1,0:T(8,128)S(1)} %collective-permute-done.direct, ...), custom_call_target="tpu_custom_call" | custom-call | flops 2097380992 | bytes 1024 | tf_op jit(solution)/shard_map/render/pallas_call | solution.py:274
  39.1 1.6 %collective-permute-start.12 = (f32[4,32,512]{2,1,0:T(8,128)S(1)}, f32[4,32,512]{2,1,0:T(8,128)S(1)}, u32[]{:S(2)}, u32[]{:S(2)}) collective-permute-start(f32[4,32,512]{2,1,0:T(8,128)S(1)} %get-tuple-element.74), channel_id=1, source_target_pairs={{0,8},{4,12},{8,0},{12,4},{16,24},{20,28},{24,16},{28,20},{1,9},{5... | collective-permute-start | bytes 786440 | tf_op jit(solution)/shard_map/ppermute | solution.py:410
  40.7 0.3 pack.9
  41.0 1.0 %collective-permute-start.7 = (f32[56,1024]{1,0:T(8,128)S(1)}, f32[56,1024]{1,0:T(8,128)S(1)}, u32[]{:S(2)}, u32[]{:S(2)}) collective-permute-start(f32[56,1024]{1,0:T(8,128)S(1)} %get-tuple-element.67), channel_id=1, source_target_pairs={{0,4},{4,0},{8,12},{12,8},{16,20},{20,16},{24,28},{28,24},{1,5},{5... | collective-permute-start | bytes 688136 | tf_op jit(solution)/shard_map/ppermute | solution.py:310
  42.0 0.1 collective-permute-done.8.passed
  42.1 2.1 %render.7 = (f32[4,32,512]{2,1,0:T(8,128)S(1)}, f32[4,32,512]{2,1,0:T(8,128)S(1)}, f32[8,128]{1,0:T(8,128)S(1)}) custom-call(f32[4,256]{1,0:T(4,128)S(1)} %maximum_convert_fusion.table, f32[2,128,2048]{2,1,0:T(8,128)S(1)} %copy-done, s32[2,128,2048]{2,1,0:T(8,128)S(1)} %copy-done.2, f32[128,1024]{1,0:T(8,128)S(1)} %collective-permute-done.direct, ...), custom_call_target="tpu_custom_call" | custom-call | flops 2097380992 | bytes 1024 | tf_op jit(solution)/shard_map/render/pallas_call | solution.py:274
  44.2 2.5 %collective-permute-start.10 = (f32[4,32,512]{2,1,0:T(8,128)S(1)}, f32[4,32,512]{2,1,0:T(8,128)S(1)}, u32[]{:S(2)}, u32[]{:S(2)}) collective-permute-start(f32[4,32,512]{2,1,0:T(8,128)S(1)} %get-tuple-element.71), channel_id=1, source_target_pairs={{0,8},{4,12},{8,0},{12,4},{16,24},{20,28},{24,16},{28,20},{1,9},{5... | collective-permute-start | bytes 786440 | tf_op jit(solution)/shard_map/ppermute | solution.py:410
  46.8 1.0 %collective-permute-done.12.rest_1_ = f32[4,32,512]{2,1,0:T(8,128)S(1)} collective-permute-done((f32[4,32,512]{2,1,0:T(8,128)S(1)}, f32[4,32,512]{2,1,0:T(8,128)S(1)}, u32[]{:S(2)}, u32[]{:S(2)}) %collective-permute-start.12) | collective-permute-done | bytes 262176 | tf_op jit(solution)/shard_map/ppermute | solution.py:410
  47.7 0.1 merge.6
  47.8 5.7 %collective-permute-start.15 = (f32[4,48,256]{2,1,0:T(8,128)S(1)}, f32[4,48,256]{2,1,0:T(8,128)S(1)}, u32[]{:S(2)}, u32[]{:S(2)}) collective-permute-start(f32[4,48,256]{2,1,0:T(8,128)S(1)} %get-tuple-element.86), channel_id=1, source_target_pairs={{0,16},{4,20},{8,24},{12,28},{16,0},{20,4},{24,8},{28,12},{1,17},{... | collective-permute-start | bytes 589832 | tf_op jit(solution)/shard_map/ppermute | solution.py:391
  53.5 2.1 %render.8 = (f32[4,32,512]{2,1,0:T(8,128)S(1)}, f32[4,32,512]{2,1,0:T(8,128)S(1)}, f32[8,128]{1,0:T(8,128)S(1)}) custom-call(f32[4,256]{1,0:T(4,128)S(1)} %maximum_convert_fusion.table, f32[2,128,2048]{2,1,0:T(8,128)S(1)} %copy-done, s32[2,128,2048]{2,1,0:T(8,128)S(1)} %copy-done.2, f32[128,1024]{1,0:T(8,128)S(1)} %collective-permute-done.direct, ...), custom_call_target="tpu_custom_call" | custom-call | flops 2097380992 | bytes 1024 | tf_op jit(solution)/shard_map/render/pallas_call | solution.py:274
  55.6 2.5 %collective-permute-start.16 = (f32[4,32,512]{2,1,0:T(8,128)S(1)}, f32[4,32,512]{2,1,0:T(8,128)S(1)}, u32[]{:S(2)}, u32[]{:S(2)}) collective-permute-start(f32[4,32,512]{2,1,0:T(8,128)S(1)} %get-tuple-element.90), channel_id=1, source_target_pairs={{0,8},{4,12},{8,0},{12,4},{16,24},{20,28},{24,16},{28,20},{1,9},{5... | collective-permute-start | bytes 786440 | tf_op jit(solution)/shard_map/ppermute | solution.py:410
  58.2 0.1 merge.7
  58.2 0.3 collective-permute-start.14
  58.6 1.2 %render.9 = (f32[4,16,512]{2,1,0:T(8,128)S(1)}, f32[4,16,512]{2,1,0:T(8,128)S(1)}, f32[8,128]{1,0:T(8,128)S(1)}) custom-call(f32[4,256]{1,0:T(4,128)S(1)} %maximum_convert_fusion.table, f32[2,128,2048]{2,1,0:T(8,128)S(1)} %copy-done, s32[2,128,2048]{2,1,0:T(8,128)S(1)} %copy-done.2, f32[128,1024]{1,0:T(8,128)S(1)} %collective-permute-done.direct, ...), custom_call_target="tpu_custom_call" | custom-call | flops 1221190528 | bytes 1024 | tf_op jit(solution)/shard_map/render/pallas_call | solution.py:274
  59.7 3.0 %collective-permute-start.13 = (f32[4,16,512]{2,1,0:T(8,128)S(1)}, f32[4,16,512]{2,1,0:T(8,128)S(1)}, u32[]{:S(2)}, u32[]{:S(2)}) collective-permute-start(f32[4,16,512]{2,1,0:T(8,128)S(1)} %get-tuple-element.82), channel_id=1, source_target_pairs={{0,8},{4,12},{8,0},{12,4},{16,24},{20,28},{24,16},{28,20},{1,9},{5... | collective-permute-start | bytes 393224 | tf_op jit(solution)/shard_map/ppermute | solution.py:410
  62.8 0.7 finish.4
  63.5 3.0 %collective-permute-done.16.rest_1_ = f32[4,32,512]{2,1,0:T(8,128)S(1)} collective-permute-done((f32[4,32,512]{2,1,0:T(8,128)S(1)}, f32[4,32,512]{2,1,0:T(8,128)S(1)}, u32[]{:S(2)}, u32[]{:S(2)}) %collective-permute-start.16) | collective-permute-done | bytes 262176 | tf_op jit(solution)/shard_map/ppermute | solution.py:410
  66.6 0.1 merge.8
  66.6 2.8 %collective-permute-start.18 = (f32[4,32,256]{2,1,0:T(8,128)S(1)}, f32[4,32,256]{2,1,0:T(8,128)S(1)}, u32[]{:S(2)}, u32[]{:S(2)}) collective-permute-start(f32[4,32,256]{2,1,0:T(8,128)S(1)} %get-tuple-element.97), channel_id=1, source_target_pairs={{0,16},{4,20},{8,24},{12,28},{16,0},{20,4},{24,8},{28,12},{1,17},{... | collective-permute-start | bytes 393224 | tf_op jit(solution)/shard_map/ppermute | solution.py:391
  69.4 0.7 finish.5
  70.2 1.1 %collective-permute-start.17 = (f32[4,16,256]{2,1,0:T(8,128)S(1)}, f32[4,16,256]{2,1,0:T(8,128)S(1)}, u32[]{:S(2)}, u32[]{:S(2)}) collective-permute-start(f32[4,16,256]{2,1,0:T(8,128)S(1)} %get-tuple-element.95), channel_id=1, source_target_pairs={{0,16},{4,20},{8,24},{12,28},{16,0},{20,4},{24,8},{28,12},{1,17},{... | collective-permute-start | bytes 196616 | tf_op jit(solution)/shard_map/ppermute | solution.py:391
  71.3 3.4 %collective-permute-done.18.got = f32[4,32,256]{2,1,0:T(8,128)S(1)} collective-permute-done((f32[4,32,256]{2,1,0:T(8,128)S(1)}, f32[4,32,256]{2,1,0:T(8,128)S(1)}, u32[]{:S(2)}, u32[]{:S(2)}) %collective-permute-start.18) | collective-permute-done | bytes 131104 | tf_op jit(solution)/shard_map/ppermute | solution.py:391
  74.7 0.7 finish.6
  75.4 0.0 collective-permute-done.17.got
  75.4 1.2 %finish.7 = (f32[4,128,256]{2,1,0:T(8,128)}, f32[8,128]{1,0:T(8,128)}) custom-call(f32[4,16,256]{2,1,0:T(8,128)S(1)} %get-tuple-element.94.held, f32[4,16,256]{2,1,0:T(8,128)S(1)} %collective-permute-done.17.got, f32[4,128,256]{2,1,0:T(8,128)} %get-tuple-element.100.rest_0_, f32[8,128]{1,0:T(8,128)S(1)} %get-tuple-element.101.rest_1_), custom_call_target="tpu_custom_call", output_to_operand_aliasing={{0}: (2, {})} | custom-call | flops 805000000 | bytes 1024 | tf_op jit(solution)/shard_map/finish/pallas_call | solution.py:274
  (25 shorter events, 0.2 us)
Async XLA Ops:
  0.0 4.5 %copy-start = (f32[2,128,2048]{2,1,0:T(8,128)S(1)}, f32[2,128,2048]{2,1,0:T(8,128)}, u32[]{:S(2)}) copy-start(f32[2,128,2048]{2,1,0:T(8,128)} %density.19) | copy-start | bytes 6291460
  1.4 13.7 %collective-permute-start.4 = (f32[104,1024]{1,0:T(8,128)S(1)}, f32[104,1024]{1,0:T(8,128)S(1)}, u32[]{:S(2)}, u32[]{:S(2)}) collective-permute-start(f32[104,1024]{1,0:T(8,128)S(1)} %get-tuple-element.59), channel_id=1, source_target_pairs={{0,4},{4,0},{8,12},{12,8},{16,20},{20,16},{24,28},{28,24},{1,5},{5... | collective-permute-start | bytes 1277960 | tf_op jit(solution)/shard_map/ppermute | solution.py:310
  4.5 20.3 %collective-permute-start = (f32[128,1024]{1,0:T(8,128)S(1)}, f32[128,1024]{1,0:T(8,128)S(1)}, u32[]{:S(2)}, u32[]{:S(2)}) collective-permute-start(f32[128,1024]{1,0:T(8,128)S(1)} %dynamic-slice_bitcast_fusion), channel_id=1, source_target_pairs={{4,12},{8,0},{12,20},{16,8},{20,28},{24,16},{5,13},{9,1},{13,21},{... | collective-permute-start | bytes 1572872 | tf_op jit(solution)/shard_map/ppermute | solution.py:404
  5.8 1.6 %copy-start.1 = (s32[2,128,2048]{2,1,0:T(8,128)S(1)}, s32[2,128,2048]{2,1,0:T(8,128)}, u32[]{:S(2)}) copy-start(s32[2,128,2048]{2,1,0:T(8,128)} %bins.19) | copy-start | bytes 6291460
  7.4 16.1 %copy-start.4 = (bf16[256]{0:T(256)(128)(2,1)S(1)}, bf16[256]{0:T(256)(128)(2,1)}, u32[]{:S(2)}) copy-start(bf16[256]{0:T(256)(128)(2,1)} %param.7) | copy-start | bytes 1540
  7.4 16.2 %copy-start.3 = (bf16[3,256]{1,0:T(4,128)(2,1)S(1)}, bf16[3,256]{1,0:T(4,128)(2,1)}, u32[]{:S(2)}) copy-start(bf16[3,256]{1,0:T(4,128)(2,1)} %param.6) | copy-start | bytes 4612
  8.0 23.3 %collective-permute-start.1 = (f32[184,1024]{1,0:T(8,128)S(1)}, f32[184,1024]{1,0:T(8,128)S(1)}, u32[]{:S(2)}, u32[]{:S(2)}) collective-permute-start(f32[184,1024]{1,0:T(8,128)S(1)} %get-tuple-element.56), channel_id=1, source_target_pairs={{0,4},{4,0},{8,12},{12,8},{16,20},{20,16},{24,28},{28,24},{1,5},{5... | collective-permute-start | bytes 2261000 | tf_op jit(solution)/shard_map/ppermute | solution.py:310
  15.1 9.7 %collective-permute-start.5 = (f32[48,1024]{1,0:T(8,128)S(1)}, f32[48,1024]{1,0:T(8,128)S(1)}, u32[]{:S(2)}, u32[]{:S(2)}) collective-permute-start(f32[48,1024]{1,0:T(8,128)S(1)} %slice.16), channel_id=1, source_target_pairs={{0,8},{8,16},{12,4},{16,24},{20,12},{28,20},{1,9},{9,17},{13,5},{1... | collective-permute-start | bytes 589832 | tf_op jit(solution)/shard_map/ppermute | solution.py:313
  19.2 4.4 %collective-permute-start.3 = (f32[2,1,2048]{2,1,0:T(1,128)S(1)}, f32[2,1,2048]{2,1,0:T(1,128)S(1)}, u32[]{:S(2)}, u32[]{:S(2)}) collective-permute-start(f32[2,1,2048]{2,1,0:T(1,128)S(1)} %get-tuple-element.103), channel_id=1, source_target_pairs={{1,0},{2,1},{3,2},{5,4},{6,5},{7,6},{9,8},{10,9},{11,10},{13,12},{... | collective-permute-start | bytes 49160 | tf_op jit(solution)/shard_map/ppermute | solution.py:401
  20.5 3.9 %collective-permute-start.2 = (f32[2,1,2048]{2,1,0:T(1,128)S(1)}, f32[2,1,2048]{2,1,0:T(1,128)S(1)}, u32[]{:S(2)}, u32[]{:S(2)}) collective-permute-start(f32[2,1,2048]{2,1,0:T(1,128)S(1)} %get-tuple-element.104), channel_id=1, source_target_pairs={{0,1},{1,2},{2,3},{4,5},{5,6},{6,7},{8,9},{9,10},{10,11},{12,13},{... | collective-permute-start | bytes 49160 | tf_op jit(solution)/shard_map/ppermute | solution.py:400
  24.8 17.3 %collective-permute-start.9 = (f32[104,1024]{1,0:T(8,128)S(1)}, f32[104,1024]{1,0:T(8,128)S(1)}, u32[]{:S(2)}, u32[]{:S(2)}) collective-permute-start(f32[104,1024]{1,0:T(8,128)S(1)} %get-tuple-element.68), channel_id=1, source_target_pairs={{0,4},{4,0},{8,12},{12,8},{16,20},{20,16},{24,28},{28,24},{1,5},{5... | collective-permute-start | bytes 1277960 | tf_op jit(solution)/shard_map/ppermute | solution.py:310
  26.0 9.8 %collective-permute-start.6 = (f32[4,16,512]{2,1,0:T(8,128)S(1)}, f32[4,16,512]{2,1,0:T(8,128)S(1)}, u32[]{:S(2)}, u32[]{:S(2)}) collective-permute-start(f32[4,16,512]{2,1,0:T(8,128)S(1)} %get-tuple-element.62), channel_id=1, source_target_pairs={{0,8},{4,12},{8,0},{12,4},{16,24},{20,28},{24,16},{28,20},{1,9},{5... | collective-permute-start | bytes 393224 | tf_op jit(solution)/shard_map/ppermute | solution.py:410
  31.3 10.8 %collective-permute-start.8 = (f32[80,1024]{1,0:T(8,128)S(1)}, f32[80,1024]{1,0:T(8,128)S(1)}, u32[]{:S(2)}, u32[]{:S(2)}) collective-permute-start(f32[80,1024]{1,0:T(8,128)S(1)} %slice.17), channel_id=1, source_target_pairs={{0,8},{8,16},{12,4},{16,24},{20,12},{28,20},{1,9},{9,17},{13,5},{1... | collective-permute-start | bytes 983048 | tf_op jit(solution)/shard_map/ppermute | solution.py:313
  35.4 1.6 %copy-start.2 = (s32[2,128,2048]{2,1,0:T(8,128)S(1)}, s32[2,128,2048]{2,1,0:T(8,128)}, u32[]{:S(2)}) copy-start(s32[2,128,2048]{2,1,0:T(8,128)} %bins.19) | copy-start | bytes 6291460
  35.7 17.8 %collective-permute-start.11 = (f32[104,1024]{1,0:T(8,128)S(1)}, f32[104,1024]{1,0:T(8,128)S(1)}, u32[]{:S(2)}, u32[]{:S(2)}) collective-permute-start(f32[104,1024]{1,0:T(8,128)S(1)} %get-tuple-element.72), channel_id=1, source_target_pairs={{0,4},{4,0},{8,12},{12,8},{16,20},{20,16},{24,28},{28,24},{1,5},{5... | collective-permute-start | bytes 1277960 | tf_op jit(solution)/shard_map/ppermute | solution.py:310
  39.1 8.7 %collective-permute-start.12 = (f32[4,32,512]{2,1,0:T(8,128)S(1)}, f32[4,32,512]{2,1,0:T(8,128)S(1)}, u32[]{:S(2)}, u32[]{:S(2)}) collective-permute-start(f32[4,32,512]{2,1,0:T(8,128)S(1)} %get-tuple-element.74), channel_id=1, source_target_pairs={{0,8},{4,12},{8,0},{12,4},{16,24},{20,28},{24,16},{28,20},{1,9},{5... | collective-permute-start | bytes 786440 | tf_op jit(solution)/shard_map/ppermute | solution.py:410
  41.0 17.5 %collective-permute-start.7 = (f32[56,1024]{1,0:T(8,128)S(1)}, f32[56,1024]{1,0:T(8,128)S(1)}, u32[]{:S(2)}, u32[]{:S(2)}) collective-permute-start(f32[56,1024]{1,0:T(8,128)S(1)} %get-tuple-element.67), channel_id=1, source_target_pairs={{0,4},{4,0},{8,12},{12,8},{16,20},{20,16},{24,28},{28,24},{1,5},{5... | collective-permute-start | bytes 688136 | tf_op jit(solution)/shard_map/ppermute | solution.py:310
  44.2 13.9 %collective-permute-start.10 = (f32[4,32,512]{2,1,0:T(8,128)S(1)}, f32[4,32,512]{2,1,0:T(8,128)S(1)}, u32[]{:S(2)}, u32[]{:S(2)}) collective-permute-start(f32[4,32,512]{2,1,0:T(8,128)S(1)} %get-tuple-element.71), channel_id=1, source_target_pairs={{0,8},{4,12},{8,0},{12,4},{16,24},{20,28},{24,16},{28,20},{1,9},{5... | collective-permute-start | bytes 786440 | tf_op jit(solution)/shard_map/ppermute | solution.py:410
  47.8 15.0 %collective-permute-start.15 = (f32[4,48,256]{2,1,0:T(8,128)S(1)}, f32[4,48,256]{2,1,0:T(8,128)S(1)}, u32[]{:S(2)}, u32[]{:S(2)}) collective-permute-start(f32[4,48,256]{2,1,0:T(8,128)S(1)} %get-tuple-element.86), channel_id=1, source_target_pairs={{0,16},{4,20},{8,24},{12,28},{16,0},{20,4},{24,8},{28,12},{1,17},{... | collective-permute-start | bytes 589832 | tf_op jit(solution)/shard_map/ppermute | solution.py:391
  55.6 10.9 %collective-permute-start.16 = (f32[4,32,512]{2,1,0:T(8,128)S(1)}, f32[4,32,512]{2,1,0:T(8,128)S(1)}, u32[]{:S(2)}, u32[]{:S(2)}) collective-permute-start(f32[4,32,512]{2,1,0:T(8,128)S(1)} %get-tuple-element.90), channel_id=1, source_target_pairs={{0,8},{4,12},{8,0},{12,4},{16,24},{20,28},{24,16},{28,20},{1,9},{5... | collective-permute-start | bytes 786440 | tf_op jit(solution)/shard_map/ppermute | solution.py:410
  58.2 11.2 %collective-permute-start.14 = (f32[4,32,256]{2,1,0:T(8,128)S(1)}, f32[4,32,256]{2,1,0:T(8,128)S(1)}, u32[]{:S(2)}, u32[]{:S(2)}) collective-permute-start(f32[4,32,256]{2,1,0:T(8,128)S(1)} %get-tuple-element.84), channel_id=1, source_target_pairs={{0,16},{4,20},{8,24},{12,28},{16,0},{20,4},{24,8},{28,12},{1,17},{... | collective-permute-start | bytes 393224 | tf_op jit(solution)/shard_map/ppermute | solution.py:391
  59.7 10.4 %collective-permute-start.13 = (f32[4,16,512]{2,1,0:T(8,128)S(1)}, f32[4,16,512]{2,1,0:T(8,128)S(1)}, u32[]{:S(2)}, u32[]{:S(2)}) collective-permute-start(f32[4,16,512]{2,1,0:T(8,128)S(1)} %get-tuple-element.82), channel_id=1, source_target_pairs={{0,8},{4,12},{8,0},{12,4},{16,24},{20,28},{24,16},{28,20},{1,9},{5... | collective-permute-start | bytes 393224 | tf_op jit(solution)/shard_map/ppermute | solution.py:410
  66.6 8.0 %collective-permute-start.18 = (f32[4,32,256]{2,1,0:T(8,128)S(1)}, f32[4,32,256]{2,1,0:T(8,128)S(1)}, u32[]{:S(2)}, u32[]{:S(2)}) collective-permute-start(f32[4,32,256]{2,1,0:T(8,128)S(1)} %get-tuple-element.97), channel_id=1, source_target_pairs={{0,16},{4,20},{8,24},{12,28},{16,0},{20,4},{24,8},{28,12},{1,17},{... | collective-permute-start | bytes 393224 | tf_op jit(solution)/shard_map/ppermute | solution.py:391
  70.2 5.2 %collective-permute-start.17 = (f32[4,16,256]{2,1,0:T(8,128)S(1)}, f32[4,16,256]{2,1,0:T(8,128)S(1)}, u32[]{:S(2)}, u32[]{:S(2)}) collective-permute-start(f32[4,16,256]{2,1,0:T(8,128)S(1)} %get-tuple-element.95), channel_id=1, source_target_pairs={{0,16},{4,20},{8,24},{12,28},{16,0},{20,4},{24,8},{28,12},{1,17},{... | collective-permute-start | bytes 196616 | tf_op jit(solution)/shard_map/ppermute | solution.py:391

commit v3 on v2

--- a/solution.py
+++ b/solution.py
@@ -223,9 +223,10 @@
         row += rows
 
 
-def last_body(ranges, r, held, got, *rest):
-    out, token, done, sems = rest[-4:]
-    seed_token(token)
+def last_body(ranges, r, linked, held, got, *rest):
+    out, token, done, sems = rest[-4:] if linked else (rest[-3], None, *rest[-2:])
+    if linked:
+        seed_token(token)
     values = merged_of(position()(r) == 1, held, got)
     for c in range(3):
         done[c] = values[c]
@@ -270,18 +271,20 @@
     anywhere = pl.BlockSpec(memory_space=pl.ANY)
     last = []
 
-    def call(body, operands, specs, outs, out_specs, name, micros, scratch=(), aliases=None):
+    def call(body, operands, specs, outs, out_specs, name, micros, scratch=(), aliases=None, linked=True):
         results = pl.pallas_call(
             body,
-            out_shape=[*outs, jax.ShapeDtypeStruct((8, LANES), jnp.float32)],
+            out_shape=[*outs, *[jax.ShapeDtypeStruct((8, LANES), jnp.float32)] * linked],
             in_specs=[*specs, *[anywhere] * len(last)],
-            out_specs=[*out_specs, vmem],
+            out_specs=[*out_specs, *[vmem] * linked],
             scratch_shapes=scratch,
             compiler_params=pltpu.CompilerParams(vmem_limit_bytes=VMEM_LIMIT),
             input_output_aliases=aliases or {},
             cost_estimate=pl.CostEstimate(flops=int(micros * FLOPS_PER_US), bytes_accessed=1024, transcendentals=0),
             name=name,
         )(*operands, *last)
+        if not linked:
+            return results
         last[:] = [results[-1]]
         return results[:-1]
 
@@ -342,6 +345,7 @@
 
     image = None
     parts = {}
+    written = []
 
     def land(entries, send=True, ready=()):
         nonlocal image
@@ -353,8 +357,10 @@
         rows = sum(size for _, size in ranges)
         cols = kepts[0].shape[2]
         if r == rounds - 1 and cols % LANES == 0:
+            written.extend(ranges)
+            linked = len(written) < len(chunks)
             image = call(
-                functools.partial(last_body, ranges, r),
+                functools.partial(last_body, ranges, r, linked),
                 [kepts[0], gots[0]] + ([image] if image is not None else []),
                 [vmem, vmem] + ([hbm] if image is not None else []),
                 [jax.ShapeDtypeStruct((4, height, cols), jnp.float32)],
@@ -363,6 +369,7 @@
                 costs[3],
                 [pltpu.VMEM((4, rows, cols), jnp.float32), pltpu.SemaphoreType.DMA((len(ranges),))],
                 aliases={2: 0} if image is not None else None,
+                linked=linked,
             )[0]
             return None
         if r < rounds - 1 and cols % (2 * LANES) == 0:
@@ -424,10 +431,10 @@
 
 def plan(height):
     unit = height // 16
-    chunks = [(start * unit, rows * unit, [(s * unit, r * unit) for s, r in ranges]) for start, rows, ranges in [(2, 2, [(4, 4), (2, 2)]), (4, 4, [(8, 4), (12, 4), (0, 2)]), (8, 4, []), (12, 4, []), (0, 2, [])]]
-    steps = ['p0', 'o0', 'p1', 'e0', 'p2', 'r0', 'p3', 'k0', 'r1', 'p4', 'r2', 'l1', 'r3', 'l2', 'r4', 'l1', 'l3', 'l2', 'l4', 'l3', 'l4']
-    names = {"p": "pack", "r": "render", "l": "land", "e": "edges", "o": "outer", "w": "wait", "k": "keep"}
-    return dict(far=1, costs=(0.4, 1.0, 0.1, 0.7), chunks=chunks, steps=[(names[s[0]], int(s[1:])) for s in steps])
+    chunks = [(start * unit, rows * unit, [(s * unit, r * unit) for s, r in ranges]) for start, rows, ranges in [(2, 3, [(2, 3), (5, 3)]), (5, 3, [(8, 4), (12, 4), (0, 2)]), (8, 4, []), (12, 4, []), (0, 2, [])]]
+    steps = ['p0', 'o0', 'e0', 'p1', 'p2', 'p3', 'r0', 'k0', 'r1', 'p4', 'r2', 'l1', 'r3', 'l2', 'r4', 'l1', 'l3', 'l2', 'l4', 'l3', 'l4']
+    names = {"p": "pack", "r": "render", "l": "land", "e": "edges", "o": "outer", "g": "across", "k": "keep"}
+    return dict(far=1, costs=(0.52, 1.3, 0.13, 0.9099999999999999), chunks=chunks, steps=[(names[s[0]], int(s[1:])) for s in steps])
 
 
 def solution(mesh):

time: 76.9 us -> 75 us (0.975)
  local copies, waits for them, and re-layouts: 2.8 us -> 1.7 us
    ppermute x5, waiting for transfers between devices: 7.65 us -> 3.4 us  [send_message(): message = lax.ppermute(packed, 'depth', swaps[0])]
    ppermute x2, waiting for transfers between devices: 0.1 us -> 3.33 us  [send_message(): passed = lax.ppermute(message[:count], 'depth', backward)]
    ppermute x5, starting transfers between devices: 6.97 us -> 9.11 us  [send_message(): message = lax.ppermute(packed, 'depth', swaps[0])]
    ppermute x5, waiting for transfers between devices: 3.99 us -> 5.97 us  [per_device(): lax.ppermute(sent, 'depth', swaps[1])]
    ppermute x4, starting transfers between devices: 9.94 us -> 8.16 us  [land(): return (ranges, r + 1, kept, lax.ppermute(sent, 'depth', swaps[r + 1]))]
    unnamed x10, local copies, waits for them, and re-layouts: 2.7 us -> 1.6 us
    ppermute x5, starting transfers between devices: 11.8 us -> 10.9 us  [per_device(): lax.ppermute(sent, 'depth', swaps[1])]
  transfers between devices with their start and end apart: 19 -> 19, of which waited for: 7 -> 7; matrix products, arithmetic and copies ran while one was open for 0% -> 0% of each run, Pallas kernels for 16% -> 17%
where the time goes in v3:
time: 75 us; the launch traced here: 74.7 us
  starting transfers between devices  41.9 us (56%)
  waiting for transfers between devices  16 us (21%)
  Pallas kernels  14.8 us (20%)
  local copies, waits for them, and re-layouts  1.7 us (2%)
    pallas_call x19, Pallas kernels, call(): pl.pallas_call(body, out_shape=[*outs, *[jax.ShapeDtypeStruct((8, LANES),...  14.8 us
    ppermute x5, starting transfers between devices, per_device(): lax.ppermute(sent, 'depth', swaps[1])  10.9 us
    ppermute x5, starting transfers between devices, send_message(): message = lax.ppermute(packed, 'depth', swaps[0])  9.11 us
    ppermute x4, starting transfers between devices, land(): return (ranges, r + 1, kept, lax.ppermute(sent, 'depth', swaps[r + 1]))  8.16 us
    ppermute x2, starting transfers between devices, send_message(): passed = lax.ppermute(message[:count], 'depth', backward)  8.07 us
    ppermute x5, waiting for transfers between devices, per_device(): lax.ppermute(sent, 'depth', swaps[1])  5.97 us
    ppermute x5, waiting for transfers between devices, send_message(): message = lax.ppermute(packed, 'depth', swaps[0])  3.4 us
    ppermute x2, waiting for transfers between devices, send_message(): passed = lax.ppermute(message[:count], 'depth', backward)  3.33 us
  transfers between devices with their start and end apart: 19, of which 7 were waited for; matrix products, arithmetic and copies ran while one was open for 0% of the time, Pallas kernels for 17%

profile of v3, /device:TPU:0, one launch (start us, length us, event | category | flops | bytes accessed | tf_op | source)
XLA Modules:
  0.0 74.7 jit_solution(14796739783497631455)
XLA Ops:
  0.0 1.5 %pack.5 = (f32[128,1024]{1,0:T(8,128)S(1)}, f32[8,128]{1,0:T(8,128)S(1)}) custom-call(f32[2,128,2048]{2,1,0:T(8,128)} %density.19, s32[2,128,2048]{2,1,0:T(8,128)} %bins.19), custom_call_target="tpu_custom_call" | custom-call | flops 598000000 | bytes 1024 | tf_op jit(solution)/shard_map/pack/pallas_call | solution.py:275
  1.5 3.0 %collective-permute-start.4 = (f32[128,1024]{1,0:T(8,128)S(1)}, f32[128,1024]{1,0:T(8,128)S(1)}, u32[]{:S(2)}, u32[]{:S(2)}) collective-permute-start(f32[128,1024]{1,0:T(8,128)S(1)} %get-tuple-element.55), channel_id=1, source_target_pairs={{0,4},{4,0},{8,12},{12,8},{16,20},{20,16},{24,28},{28,24},{1,5},{5... | collective-permute-start | bytes 1572872 | tf_op jit(solution)/shard_map/ppermute | solution.py:313
  4.6 1.3 %collective-permute-start = (f32[128,1024]{1,0:T(8,128)S(1)}, f32[128,1024]{1,0:T(8,128)S(1)}, u32[]{:S(2)}, u32[]{:S(2)}) collective-permute-start(f32[128,1024]{1,0:T(8,128)S(1)} %dynamic-slice_bitcast_fusion), channel_id=1, source_target_pairs={{4,12},{8,0},{12,20},{16,8},{20,28},{24,16},{5,13},{9,1},{13,21},{... | collective-permute-start | bytes 1572872 | tf_op jit(solution)/shard_map/ppermute | solution.py:411
  5.9 0.0 copy-start.1
  5.9 1.6 %copy-done.1 = s32[2,128,2048]{2,1,0:T(8,128)S(1)} copy-done((s32[2,128,2048]{2,1,0:T(8,128)S(1)}, s32[2,128,2048]{2,1,0:T(8,128)}, u32[]{:S(2)}) %copy-start.1) | copy-done | bytes 2097176
  7.5 0.5 pack.6
  8.0 2.8 %collective-permute-start.1 = (f32[160,1024]{1,0:T(8,128)S(1)}, f32[160,1024]{1,0:T(8,128)S(1)}, u32[]{:S(2)}, u32[]{:S(2)}) collective-permute-start(f32[160,1024]{1,0:T(8,128)S(1)} %get-tuple-element.54), channel_id=1, source_target_pairs={{0,4},{4,0},{8,12},{12,8},{16,20},{20,16},{24,28},{28,24},{1,5},{5... | collective-permute-start | bytes 1966088 | tf_op jit(solution)/shard_map/ppermute | solution.py:313
  10.9 1.3 %collective-permute-start.3 = (f32[2,1,2048]{2,1,0:T(1,128)S(1)}, f32[2,1,2048]{2,1,0:T(1,128)S(1)}, u32[]{:S(2)}, u32[]{:S(2)}) collective-permute-start(f32[2,1,2048]{2,1,0:T(1,128)S(1)} %get-tuple-element.99), channel_id=1, source_target_pairs={{1,0},{2,1},{3,2},{5,4},{6,5},{7,6},{9,8},{10,9},{11,10},{13,12},{... | collective-permute-start | bytes 49160 | tf_op jit(solution)/shard_map/ppermute | solution.py:408
  12.2 3.0 %collective-permute-start.2 = (f32[2,1,2048]{2,1,0:T(1,128)S(1)}, f32[2,1,2048]{2,1,0:T(1,128)S(1)}, u32[]{:S(2)}, u32[]{:S(2)}) collective-permute-start(f32[2,1,2048]{2,1,0:T(1,128)S(1)} %get-tuple-element.100), channel_id=1, source_target_pairs={{0,1},{1,2},{2,3},{4,5},{5,6},{6,7},{8,9},{9,10},{10,11},{12,13},{... | collective-permute-start | bytes 49160 | tf_op jit(solution)/shard_map/ppermute | solution.py:407
  15.2 2.1 %collective-permute-done.4.face.message = f32[128,1024]{1,0:T(8,128)S(1)} collective-permute-done((f32[128,1024]{1,0:T(8,128)S(1)}, f32[128,1024]{1,0:T(8,128)S(1)}, u32[]{:S(2)}, u32[]{:S(2)}) %collective-permute-start.4) | collective-permute-done | bytes 524320 | tf_op jit(solution)/shard_map/ppermute | solution.py:313
  17.3 4.0 %collective-permute-start.5 = (f32[48,1024]{1,0:T(8,128)S(1)}, f32[48,1024]{1,0:T(8,128)S(1)}, u32[]{:S(2)}, u32[]{:S(2)}) collective-permute-start(f32[48,1024]{1,0:T(8,128)S(1)} %slice.16), channel_id=1, source_target_pairs={{0,8},{8,16},{12,4},{16,24},{20,12},{28,20},{1,9},{9,17},{13,5},{1... | collective-permute-start | bytes 589832 | tf_op jit(solution)/shard_map/ppermute | solution.py:316
  21.4 0.0 collective-permute-done.3.rest_2_.rest_1_
  21.4 0.4 pack.7
  21.8 0.3 pack.8
  22.1 0.0 collective-permute-done.direct
  22.2 2.4 %collective-permute-done.5.passed = f32[48,1024]{1,0:T(8,128)S(1)} collective-permute-done((f32[48,1024]{1,0:T(8,128)S(1)}, f32[48,1024]{1,0:T(8,128)S(1)}, u32[]{:S(2)}, u32[]{:S(2)}) %collective-permute-start.5) | collective-permute-done | bytes 196640 | tf_op jit(solution)/shard_map/ppermute | solution.py:316
  24.5 1.6 %render.5 = (f32[4,24,512]{2,1,0:T(8,128)S(1)}, f32[4,24,512]{2,1,0:T(8,128)S(1)}, f32[8,128]{1,0:T(8,128)S(1)}) custom-call(f32[4,256]{1,0:T(4,128)S(1)} %maximum_convert_fusion.table, f32[2,128,2048]{2,1,0:T(8,128)S(1)} %copy-done, s32[2,128,2048]{2,1,0:T(8,128)S(1)} %copy-done.1, f32[128,1024]{1,0:T(8,128)S(1)} %collective-permute-done.direct, ...), custom_call_target="tpu_custom_call" | custom-call | flops 2157071360 | bytes 1024 | tf_op jit(solution)/shard_map/render/pallas_call | solution.py:275
  26.1 2.5 %collective-permute-start.6 = (f32[4,24,512]{2,1,0:T(8,128)S(1)}, f32[4,24,512]{2,1,0:T(8,128)S(1)}, u32[]{:S(2)}, u32[]{:S(2)}) collective-permute-start(f32[4,24,512]{2,1,0:T(8,128)S(1)} %get-tuple-element.60), channel_id=1, source_target_pairs={{0,8},{4,12},{8,0},{12,4},{16,24},{20,28},{24,16},{28,20},{1,9},{5... | collective-permute-start | bytes 589832 | tf_op jit(solution)/shard_map/ppermute | solution.py:417
  28.7 1.5 %collective-permute-start.9 = (f32[104,1024]{1,0:T(8,128)S(1)}, f32[104,1024]{1,0:T(8,128)S(1)}, u32[]{:S(2)}, u32[]{:S(2)}) collective-permute-start(f32[104,1024]{1,0:T(8,128)S(1)} %get-tuple-element.65), channel_id=1, source_target_pairs={{0,4},{4,0},{8,12},{12,8},{16,20},{20,16},{24,28},{28,24},{1,5},{5... | collective-permute-start | bytes 1277960 | tf_op jit(solution)/shard_map/ppermute | solution.py:313
  30.2 1.1 %collective-permute-done.1.message.face = f32[160,1024]{1,0:T(8,128)S(1)} collective-permute-done((f32[160,1024]{1,0:T(8,128)S(1)}, f32[160,1024]{1,0:T(8,128)S(1)}, u32[]{:S(2)}, u32[]{:S(2)}) %collective-permute-start.1) | collective-permute-done | bytes 655392 | tf_op jit(solution)/shard_map/ppermute | solution.py:313
  31.4 4.0 %collective-permute-start.8 = (f32[80,1024]{1,0:T(8,128)S(1)}, f32[80,1024]{1,0:T(8,128)S(1)}, u32[]{:S(2)}, u32[]{:S(2)}) collective-permute-start(f32[80,1024]{1,0:T(8,128)S(1)} %slice.17), channel_id=1, source_target_pairs={{0,8},{8,16},{12,4},{16,24},{20,12},{28,20},{1,9},{9,17},{13,5},{1... | collective-permute-start | bytes 983048 | tf_op jit(solution)/shard_map/ppermute | solution.py:316
  35.4 0.1 collective-permute-start.11
  35.6 1.6 %render.6 = (f32[4,24,512]{2,1,0:T(8,128)S(1)}, f32[4,24,512]{2,1,0:T(8,128)S(1)}, f32[8,128]{1,0:T(8,128)S(1)}) custom-call(f32[4,256]{1,0:T(4,128)S(1)} %maximum_convert_fusion.table, f32[2,128,2048]{2,1,0:T(8,128)S(1)} %copy-done, s32[2,128,2048]{2,1,0:T(8,128)S(1)} %copy-done.2, f32[128,1024]{1,0:T(8,128)S(1)} %collective-permute-done.direct, ...), custom_call_target="tpu_custom_call" | custom-call | flops 2157071360 | bytes 1024 | tf_op jit(solution)/shard_map/render/pallas_call | solution.py:275
  37.2 2.0 %collective-permute-start.12 = (f32[4,24,512]{2,1,0:T(8,128)S(1)}, f32[4,24,512]{2,1,0:T(8,128)S(1)}, u32[]{:S(2)}, u32[]{:S(2)}) collective-permute-start(f32[4,24,512]{2,1,0:T(8,128)S(1)} %get-tuple-element.71), channel_id=1, source_target_pairs={{0,8},{4,12},{8,0},{12,4},{16,24},{20,28},{24,16},{28,20},{1,9},{5... | collective-permute-start | bytes 589832 | tf_op jit(solution)/shard_map/ppermute | solution.py:417
  39.2 0.3 pack.9
  39.5 1.7 %collective-permute-start.7 = (f32[56,1024]{1,0:T(8,128)S(1)}, f32[56,1024]{1,0:T(8,128)S(1)}, u32[]{:S(2)}, u32[]{:S(2)}) collective-permute-start(f32[56,1024]{1,0:T(8,128)S(1)} %get-tuple-element.64), channel_id=1, source_target_pairs={{0,4},{4,0},{8,12},{12,8},{16,20},{20,16},{24,28},{28,24},{1,5},{5... | collective-permute-start | bytes 688136 | tf_op jit(solution)/shard_map/ppermute | solution.py:313
  41.2 0.2 collective-permute-done.9.message
  41.5 1.0 %collective-permute-done.8.passed = f32[80,1024]{1,0:T(8,128)S(1)} collective-permute-done((f32[80,1024]{1,0:T(8,128)S(1)}, f32[80,1024]{1,0:T(8,128)S(1)}, u32[]{:S(2)}, u32[]{:S(2)}) %collective-permute-start.8) | collective-permute-done | bytes 327712 | tf_op jit(solution)/shard_map/ppermute | solution.py:316
  42.4 2.1 %render.7 = (f32[4,32,512]{2,1,0:T(8,128)S(1)}, f32[4,32,512]{2,1,0:T(8,128)S(1)}, f32[8,128]{1,0:T(8,128)S(1)}) custom-call(f32[4,256]{1,0:T(4,128)S(1)} %maximum_convert_fusion.table, f32[2,128,2048]{2,1,0:T(8,128)S(1)} %copy-done, s32[2,128,2048]{2,1,0:T(8,128)S(1)} %copy-done.2, f32[128,1024]{1,0:T(8,128)S(1)} %collective-permute-done.direct, ...), custom_call_target="tpu_custom_call" | custom-call | flops 2726595328 | bytes 1024 | tf_op jit(solution)/shard_map/render/pallas_call | solution.py:275
  44.5 2.5 %collective-permute-start.10 = (f32[4,32,512]{2,1,0:T(8,128)S(1)}, f32[4,32,512]{2,1,0:T(8,128)S(1)}, u32[]{:S(2)}, u32[]{:S(2)}) collective-permute-start(f32[4,32,512]{2,1,0:T(8,128)S(1)} %get-tuple-element.68), channel_id=1, source_target_pairs={{0,8},{4,12},{8,0},{12,4},{16,24},{20,28},{24,16},{28,20},{1,9},{5... | collective-permute-start | bytes 786440 | tf_op jit(solution)/shard_map/ppermute | solution.py:417
  47.1 0.1 merge.6
  47.1 4.0 %collective-permute-start.15 = (f32[4,48,256]{2,1,0:T(8,128)S(1)}, f32[4,48,256]{2,1,0:T(8,128)S(1)}, u32[]{:S(2)}, u32[]{:S(2)}) collective-permute-start(f32[4,48,256]{2,1,0:T(8,128)S(1)} %get-tuple-element.83), channel_id=1, source_target_pairs={{0,16},{4,20},{8,24},{12,28},{16,0},{20,4},{24,8},{28,12},{1,17},{... | collective-permute-start | bytes 589832 | tf_op jit(solution)/shard_map/ppermute | solution.py:398
  51.1 2.1 %render.8 = (f32[4,32,512]{2,1,0:T(8,128)S(1)}, f32[4,32,512]{2,1,0:T(8,128)S(1)}, f32[8,128]{1,0:T(8,128)S(1)}) custom-call(f32[4,256]{1,0:T(4,128)S(1)} %maximum_convert_fusion.table, f32[2,128,2048]{2,1,0:T(8,128)S(1)} %copy-done, s32[2,128,2048]{2,1,0:T(8,128)S(1)} %copy-done.2, f32[128,1024]{1,0:T(8,128)S(1)} %collective-permute-done.direct, ...), custom_call_target="tpu_custom_call" | custom-call | flops 2726595328 | bytes 1024 | tf_op jit(solution)/shard_map/render/pallas_call | solution.py:275
  53.2 2.5 %collective-permute-start.16 = (f32[4,32,512]{2,1,0:T(8,128)S(1)}, f32[4,32,512]{2,1,0:T(8,128)S(1)}, u32[]{:S(2)}, u32[]{:S(2)}) collective-permute-start(f32[4,32,512]{2,1,0:T(8,128)S(1)} %get-tuple-element.87), channel_id=1, source_target_pairs={{0,8},{4,12},{8,0},{12,4},{16,24},{20,28},{24,16},{28,20},{1,9},{5... | collective-permute-start | bytes 786440 | tf_op jit(solution)/shard_map/ppermute | solution.py:417
  55.8 0.1 merge.7
  55.9 0.7 collective-permute-start.14
  56.6 1.2 %render.9 = (f32[4,16,512]{2,1,0:T(8,128)S(1)}, f32[4,16,512]{2,1,0:T(8,128)S(1)}, f32[8,128]{1,0:T(8,128)S(1)}) custom-call(f32[4,256]{1,0:T(4,128)S(1)} %maximum_convert_fusion.table, f32[2,128,2048]{2,1,0:T(8,128)S(1)} %copy-done, s32[2,128,2048]{2,1,0:T(8,128)S(1)} %copy-done.2, f32[128,1024]{1,0:T(8,128)S(1)} %collective-permute-done.direct, ...), custom_call_target="tpu_custom_call" | custom-call | flops 1587547648 | bytes 1024 | tf_op jit(solution)/shard_map/render/pallas_call | solution.py:275
  57.8 1.3 %collective-permute-start.13 = (f32[4,16,512]{2,1,0:T(8,128)S(1)}, f32[4,16,512]{2,1,0:T(8,128)S(1)}, u32[]{:S(2)}, u32[]{:S(2)}) collective-permute-start(f32[4,16,512]{2,1,0:T(8,128)S(1)} %get-tuple-element.79), channel_id=1, source_target_pairs={{0,8},{4,12},{8,0},{12,4},{16,24},{20,28},{24,16},{28,20},{1,9},{5... | collective-permute-start | bytes 393224 | tf_op jit(solution)/shard_map/ppermute | solution.py:417
  59.1 0.7 finish.4
  59.8 6.0 %collective-permute-done.16.rest_1_ = f32[4,32,512]{2,1,0:T(8,128)S(1)} collective-permute-done((f32[4,32,512]{2,1,0:T(8,128)S(1)}, f32[4,32,512]{2,1,0:T(8,128)S(1)}, u32[]{:S(2)}, u32[]{:S(2)}) %collective-permute-start.16) | collective-permute-done | bytes 262176 | tf_op jit(solution)/shard_map/ppermute | solution.py:417
  65.8 0.1 merge.8
  65.8 1.2 %collective-permute-start.18 = (f32[4,32,256]{2,1,0:T(8,128)S(1)}, f32[4,32,256]{2,1,0:T(8,128)S(1)}, u32[]{:S(2)}, u32[]{:S(2)}) collective-permute-start(f32[4,32,256]{2,1,0:T(8,128)S(1)} %get-tuple-element.94), channel_id=1, source_target_pairs={{0,16},{4,20},{8,24},{12,28},{16,0},{20,4},{24,8},{28,12},{1,17},{... | collective-permute-start | bytes 393224 | tf_op jit(solution)/shard_map/ppermute | solution.py:398
  67.0 0.7 finish.5
  67.8 2.3 %collective-permute-start.17 = (f32[4,16,256]{2,1,0:T(8,128)S(1)}, f32[4,16,256]{2,1,0:T(8,128)S(1)}, u32[]{:S(2)}, u32[]{:S(2)}) collective-permute-start(f32[4,16,256]{2,1,0:T(8,128)S(1)} %get-tuple-element.92), channel_id=1, source_target_pairs={{0,16},{4,20},{8,24},{12,28},{16,0},{20,4},{24,8},{28,12},{1,17},{... | collective-permute-start | bytes 196616 | tf_op jit(solution)/shard_map/ppermute | solution.py:398
  70.0 3.3 %collective-permute-done.18.got = f32[4,32,256]{2,1,0:T(8,128)S(1)} collective-permute-done((f32[4,32,256]{2,1,0:T(8,128)S(1)}, f32[4,32,256]{2,1,0:T(8,128)S(1)}, u32[]{:S(2)}, u32[]{:S(2)}) %collective-permute-start.18) | collective-permute-done | bytes 131104 | tf_op jit(solution)/shard_map/ppermute | solution.py:398
  73.3 0.7 finish.6
  74.0 0.0 collective-permute-done.17.got
  74.0 0.7 finish.7
  (25 shorter events, 0.2 us)
Async XLA Ops:
  0.0 4.5 %copy-start = (f32[2,128,2048]{2,1,0:T(8,128)S(1)}, f32[2,128,2048]{2,1,0:T(8,128)}, u32[]{:S(2)}) copy-start(f32[2,128,2048]{2,1,0:T(8,128)} %density.19) | copy-start | bytes 6291460
  1.5 15.8 %collective-permute-start.4 = (f32[128,1024]{1,0:T(8,128)S(1)}, f32[128,1024]{1,0:T(8,128)S(1)}, u32[]{:S(2)}, u32[]{:S(2)}) collective-permute-start(f32[128,1024]{1,0:T(8,128)S(1)} %get-tuple-element.55), channel_id=1, source_target_pairs={{0,4},{4,0},{8,12},{12,8},{16,20},{20,16},{24,28},{28,24},{1,5},{5... | collective-permute-start | bytes 1572872 | tf_op jit(solution)/shard_map/ppermute | solution.py:313
  4.6 17.6 %collective-permute-start = (f32[128,1024]{1,0:T(8,128)S(1)}, f32[128,1024]{1,0:T(8,128)S(1)}, u32[]{:S(2)}, u32[]{:S(2)}) collective-permute-start(f32[128,1024]{1,0:T(8,128)S(1)} %dynamic-slice_bitcast_fusion), channel_id=1, source_target_pairs={{4,12},{8,0},{12,20},{16,8},{20,28},{24,16},{5,13},{9,1},{13,21},{... | collective-permute-start | bytes 1572872 | tf_op jit(solution)/shard_map/ppermute | solution.py:411
  5.9 1.6 %copy-start.1 = (s32[2,128,2048]{2,1,0:T(8,128)S(1)}, s32[2,128,2048]{2,1,0:T(8,128)}, u32[]{:S(2)}) copy-start(s32[2,128,2048]{2,1,0:T(8,128)} %bins.19) | copy-start | bytes 6291460
  7.5 7.7 %copy-start.4 = (bf16[256]{0:T(256)(128)(2,1)S(1)}, bf16[256]{0:T(256)(128)(2,1)}, u32[]{:S(2)}) copy-start(bf16[256]{0:T(256)(128)(2,1)} %param.7) | copy-start | bytes 1540
  7.5 13.9 %copy-start.3 = (bf16[3,256]{1,0:T(4,128)(2,1)S(1)}, bf16[3,256]{1,0:T(4,128)(2,1)}, u32[]{:S(2)}) copy-start(bf16[3,256]{1,0:T(4,128)(2,1)} %param.6) | copy-start | bytes 4612
  8.0 23.3 %collective-permute-start.1 = (f32[160,1024]{1,0:T(8,128)S(1)}, f32[160,1024]{1,0:T(8,128)S(1)}, u32[]{:S(2)}, u32[]{:S(2)}) collective-permute-start(f32[160,1024]{1,0:T(8,128)S(1)} %get-tuple-element.54), channel_id=1, source_target_pairs={{0,4},{4,0},{8,12},{12,8},{16,20},{20,16},{24,28},{28,24},{1,5},{5... | collective-permute-start | bytes 1966088 | tf_op jit(solution)/shard_map/ppermute | solution.py:313
  10.9 10.5 %collective-permute-start.3 = (f32[2,1,2048]{2,1,0:T(1,128)S(1)}, f32[2,1,2048]{2,1,0:T(1,128)S(1)}, u32[]{:S(2)}, u32[]{:S(2)}) collective-permute-start(f32[2,1,2048]{2,1,0:T(1,128)S(1)} %get-tuple-element.99), channel_id=1, source_target_pairs={{1,0},{2,1},{3,2},{5,4},{6,5},{7,6},{9,8},{10,9},{11,10},{13,12},{... | collective-permute-start | bytes 49160 | tf_op jit(solution)/shard_map/ppermute | solution.py:408
  12.2 9.2 %collective-permute-start.2 = (f32[2,1,2048]{2,1,0:T(1,128)S(1)}, f32[2,1,2048]{2,1,0:T(1,128)S(1)}, u32[]{:S(2)}, u32[]{:S(2)}) collective-permute-start(f32[2,1,2048]{2,1,0:T(1,128)S(1)} %get-tuple-element.100), channel_id=1, source_target_pairs={{0,1},{1,2},{2,3},{4,5},{5,6},{6,7},{8,9},{9,10},{10,11},{12,13},{... | collective-permute-start | bytes 49160 | tf_op jit(solution)/shard_map/ppermute | solution.py:407
  17.3 7.2 %collective-permute-start.5 = (f32[48,1024]{1,0:T(8,128)S(1)}, f32[48,1024]{1,0:T(8,128)S(1)}, u32[]{:S(2)}, u32[]{:S(2)}) collective-permute-start(f32[48,1024]{1,0:T(8,128)S(1)} %slice.16), channel_id=1, source_target_pairs={{0,8},{8,16},{12,4},{16,24},{20,12},{28,20},{1,9},{9,17},{13,5},{1... | collective-permute-start | bytes 589832 | tf_op jit(solution)/shard_map/ppermute | solution.py:316
  24.5 11.0 %copy-start.2 = (s32[2,128,2048]{2,1,0:T(8,128)S(1)}, s32[2,128,2048]{2,1,0:T(8,128)}, u32[]{:S(2)}) copy-start(s32[2,128,2048]{2,1,0:T(8,128)} %bins.19) | copy-start | bytes 6291460
  26.1 9.3 %collective-permute-start.6 = (f32[4,24,512]{2,1,0:T(8,128)S(1)}, f32[4,24,512]{2,1,0:T(8,128)S(1)}, u32[]{:S(2)}, u32[]{:S(2)}) collective-permute-start(f32[4,24,512]{2,1,0:T(8,128)S(1)} %get-tuple-element.60), channel_id=1, source_target_pairs={{0,8},{4,12},{8,0},{12,4},{16,24},{20,28},{24,16},{28,20},{1,9},{5... | collective-permute-start | bytes 589832 | tf_op jit(solution)/shard_map/ppermute | solution.py:417
  28.7 12.8 %collective-permute-start.9 = (f32[104,1024]{1,0:T(8,128)S(1)}, f32[104,1024]{1,0:T(8,128)S(1)}, u32[]{:S(2)}, u32[]{:S(2)}) collective-permute-start(f32[104,1024]{1,0:T(8,128)S(1)} %get-tuple-element.65), channel_id=1, source_target_pairs={{0,4},{4,0},{8,12},{12,8},{16,20},{20,16},{24,28},{28,24},{1,5},{5... | collective-permute-start | bytes 1277960 | tf_op jit(solution)/shard_map/ppermute | solution.py:313
  31.4 11.1 %collective-permute-start.8 = (f32[80,1024]{1,0:T(8,128)S(1)}, f32[80,1024]{1,0:T(8,128)S(1)}, u32[]{:S(2)}, u32[]{:S(2)}) collective-permute-start(f32[80,1024]{1,0:T(8,128)S(1)} %slice.17), channel_id=1, source_target_pairs={{0,8},{8,16},{12,4},{16,24},{20,12},{28,20},{1,9},{9,17},{13,5},{1... | collective-permute-start | bytes 983048 | tf_op jit(solution)/shard_map/ppermute | solution.py:316
  35.4 15.7 %collective-permute-start.11 = (f32[104,1024]{1,0:T(8,128)S(1)}, f32[104,1024]{1,0:T(8,128)S(1)}, u32[]{:S(2)}, u32[]{:S(2)}) collective-permute-start(f32[104,1024]{1,0:T(8,128)S(1)} %get-tuple-element.69), channel_id=1, source_target_pairs={{0,4},{4,0},{8,12},{12,8},{16,20},{20,16},{24,28},{28,24},{1,5},{5... | collective-permute-start | bytes 1277960 | tf_op jit(solution)/shard_map/ppermute | solution.py:313
  37.2 9.9 %collective-permute-start.12 = (f32[4,24,512]{2,1,0:T(8,128)S(1)}, f32[4,24,512]{2,1,0:T(8,128)S(1)}, u32[]{:S(2)}, u32[]{:S(2)}) collective-permute-start(f32[4,24,512]{2,1,0:T(8,128)S(1)} %get-tuple-element.71), channel_id=1, source_target_pairs={{0,8},{4,12},{8,0},{12,4},{16,24},{20,28},{24,16},{28,20},{1,9},{5... | collective-permute-start | bytes 589832 | tf_op jit(solution)/shard_map/ppermute | solution.py:417
  39.5 17.1 %collective-permute-start.7 = (f32[56,1024]{1,0:T(8,128)S(1)}, f32[56,1024]{1,0:T(8,128)S(1)}, u32[]{:S(2)}, u32[]{:S(2)}) collective-permute-start(f32[56,1024]{1,0:T(8,128)S(1)} %get-tuple-element.64), channel_id=1, source_target_pairs={{0,4},{4,0},{8,12},{12,8},{16,20},{20,16},{24,28},{28,24},{1,5},{5... | collective-permute-start | bytes 688136 | tf_op jit(solution)/shard_map/ppermute | solution.py:313
  44.5 11.3 %collective-permute-start.10 = (f32[4,32,512]{2,1,0:T(8,128)S(1)}, f32[4,32,512]{2,1,0:T(8,128)S(1)}, u32[]{:S(2)}, u32[]{:S(2)}) collective-permute-start(f32[4,32,512]{2,1,0:T(8,128)S(1)} %get-tuple-element.68), channel_id=1, source_target_pairs={{0,8},{4,12},{8,0},{12,4},{16,24},{20,28},{24,16},{28,20},{1,9},{5... | collective-permute-start | bytes 786440 | tf_op jit(solution)/shard_map/ppermute | solution.py:417
  47.1 11.9 %collective-permute-start.15 = (f32[4,48,256]{2,1,0:T(8,128)S(1)}, f32[4,48,256]{2,1,0:T(8,128)S(1)}, u32[]{:S(2)}, u32[]{:S(2)}) collective-permute-start(f32[4,48,256]{2,1,0:T(8,128)S(1)} %get-tuple-element.83), channel_id=1, source_target_pairs={{0,16},{4,20},{8,24},{12,28},{16,0},{20,4},{24,8},{28,12},{1,17},{... | collective-permute-start | bytes 589832 | tf_op jit(solution)/shard_map/ppermute | solution.py:398
  53.2 12.5 %collective-permute-start.16 = (f32[4,32,512]{2,1,0:T(8,128)S(1)}, f32[4,32,512]{2,1,0:T(8,128)S(1)}, u32[]{:S(2)}, u32[]{:S(2)}) collective-permute-start(f32[4,32,512]{2,1,0:T(8,128)S(1)} %get-tuple-element.87), channel_id=1, source_target_pairs={{0,8},{4,12},{8,0},{12,4},{16,24},{20,28},{24,16},{28,20},{1,9},{5... | collective-permute-start | bytes 786440 | tf_op jit(solution)/shard_map/ppermute | solution.py:417
  55.9 11.2 %collective-permute-start.14 = (f32[4,32,256]{2,1,0:T(8,128)S(1)}, f32[4,32,256]{2,1,0:T(8,128)S(1)}, u32[]{:S(2)}, u32[]{:S(2)}) collective-permute-start(f32[4,32,256]{2,1,0:T(8,128)S(1)} %get-tuple-element.81), channel_id=1, source_target_pairs={{0,16},{4,20},{8,24},{12,28},{16,0},{20,4},{24,8},{28,12},{1,17},{... | collective-permute-start | bytes 393224 | tf_op jit(solution)/shard_map/ppermute | solution.py:398
  57.8 9.9 %collective-permute-start.13 = (f32[4,16,512]{2,1,0:T(8,128)S(1)}, f32[4,16,512]{2,1,0:T(8,128)S(1)}, u32[]{:S(2)}, u32[]{:S(2)}) collective-permute-start(f32[4,16,512]{2,1,0:T(8,128)S(1)} %get-tuple-element.79), channel_id=1, source_target_pairs={{0,8},{4,12},{8,0},{12,4},{16,24},{20,28},{24,16},{28,20},{1,9},{5... | collective-permute-start | bytes 393224 | tf_op jit(solution)/shard_map/ppermute | solution.py:417
  65.8 7.5 %collective-permute-start.18 = (f32[4,32,256]{2,1,0:T(8,128)S(1)}, f32[4,32,256]{2,1,0:T(8,128)S(1)}, u32[]{:S(2)}, u32[]{:S(2)}) collective-permute-start(f32[4,32,256]{2,1,0:T(8,128)S(1)} %get-tuple-element.94), channel_id=1, source_target_pairs={{0,16},{4,20},{8,24},{12,28},{16,0},{20,4},{24,8},{28,12},{1,17},{... | collective-permute-start | bytes 393224 | tf_op jit(solution)/shard_map/ppermute | solution.py:398
  67.8 6.2 %collective-permute-start.17 = (f32[4,16,256]{2,1,0:T(8,128)S(1)}, f32[4,16,256]{2,1,0:T(8,128)S(1)}, u32[]{:S(2)}, u32[]{:S(2)}) collective-permute-start(f32[4,16,256]{2,1,0:T(8,128)S(1)} %get-tuple-element.92), channel_id=1, source_target_pairs={{0,16},{4,20},{8,24},{12,28},{16,0},{20,4},{24,8},{28,12},{1,17},{... | collective-permute-start | bytes 196616 | tf_op jit(solution)/shard_map/ppermute | solution.py:398

commit v4 on v3

--- a/solution.py
+++ b/solution.py
@@ -190,7 +190,7 @@
                 rgbt[which, c, here, place] = value
         return carry
 
-    lax.fori_loop(0, rows // 8, strip, 0)
+    lax.fori_loop(0, rows // 8, strip, 0, unroll=True)
     kept[...] = rgbt[0]
     sent[...] = rgbt[1]
 

time: 75 us -> 74.8 us (level)
  Pallas kernels: 14.8 us -> 13.6 us
  starting transfers between devices: 41.9 us -> 43 us
    pallas_call x19, Pallas kernels: 14.8 us -> 13.6 us  [call(): pl.pallas_call(body, out_shape=[*outs, *[jax.ShapeDtypeStruct((8, LANES),...]
  transfers between devices with their start and end apart: 19 -> 19, of which waited for: 7 -> 7; matrix products, arithmetic and copies ran while one was open for 0% -> 0% of each run, Pallas kernels for 17% -> 15%
where the time goes in v4:
time: 74.8 us; the launch traced here: 74.4 us
  starting transfers between devices  43 us (57%)
  waiting for transfers between devices  15.8 us (21%)
  Pallas kernels  13.6 us (18%)
  local copies, waits for them, and re-layouts  1.7 us (2%)
    pallas_call x19, Pallas kernels, call(): pl.pallas_call(body, out_shape=[*outs, *[jax.ShapeDtypeStruct((8, LANES),...  13.6 us
    ppermute x5, starting transfers between devices, per_device(): lax.ppermute(sent, 'depth', swaps[1])  11.6 us
    ppermute x5, starting transfers between devices, send_message(): message = lax.ppermute(packed, 'depth', swaps[0])  9.11 us
    ppermute x4, starting transfers between devices, land(): return (ranges, r + 1, kept, lax.ppermute(sent, 'depth', swaps[r + 1]))  8.54 us
    ppermute x2, starting transfers between devices, send_message(): passed = lax.ppermute(message[:count], 'depth', backward)  8.07 us
    ppermute x5, waiting for transfers between devices, per_device(): lax.ppermute(sent, 'depth', swaps[1])  5.56 us
    ppermute x5, waiting for transfers between devices, send_message(): message = lax.ppermute(packed, 'depth', swaps[0])  3.6 us
    ppermute x2, waiting for transfers between devices, send_message(): passed = lax.ppermute(message[:count], 'depth', backward)  3.54 us
  transfers between devices with their start and end apart: 19, of which 7 were waited for; matrix products, arithmetic and copies ran while one was open for 0% of the time, Pallas kernels for 15%

profile of v4, /device:TPU:0, one launch (start us, length us, event | category | flops | bytes accessed | tf_op | source)
XLA Modules:
  0.0 74.4 jit_solution(9289484141276596257)
XLA Ops:
  0.0 1.5 %pack.5 = (f32[128,1024]{1,0:T(8,128)S(1)}, f32[8,128]{1,0:T(8,128)S(1)}) custom-call(f32[2,128,2048]{2,1,0:T(8,128)} %density.19, s32[2,128,2048]{2,1,0:T(8,128)} %bins.19), custom_call_target="tpu_custom_call" | custom-call | flops 598000000 | bytes 1024 | tf_op jit(solution)/shard_map/pack/pallas_call | solution.py:275
  1.5 3.0 %collective-permute-start.4 = (f32[128,1024]{1,0:T(8,128)S(1)}, f32[128,1024]{1,0:T(8,128)S(1)}, u32[]{:S(2)}, u32[]{:S(2)}) collective-permute-start(f32[128,1024]{1,0:T(8,128)S(1)} %get-tuple-element.55), channel_id=1, source_target_pairs={{0,4},{4,0},{8,12},{12,8},{16,20},{20,16},{24,28},{28,24},{1,5},{5... | collective-permute-start | bytes 1572872 | tf_op jit(solution)/shard_map/ppermute | solution.py:313
  4.6 1.3 %collective-permute-start = (f32[128,1024]{1,0:T(8,128)S(1)}, f32[128,1024]{1,0:T(8,128)S(1)}, u32[]{:S(2)}, u32[]{:S(2)}) collective-permute-start(f32[128,1024]{1,0:T(8,128)S(1)} %dynamic-slice_bitcast_fusion), channel_id=1, source_target_pairs={{4,12},{8,0},{12,20},{16,8},{20,28},{24,16},{5,13},{9,1},{13,21},{... | collective-permute-start | bytes 1572872 | tf_op jit(solution)/shard_map/ppermute | solution.py:411
  5.9 0.0 copy-start.1
  5.9 1.6 %copy-done.1 = s32[2,128,2048]{2,1,0:T(8,128)S(1)} copy-done((s32[2,128,2048]{2,1,0:T(8,128)S(1)}, s32[2,128,2048]{2,1,0:T(8,128)}, u32[]{:S(2)}) %copy-start.1) | copy-done | bytes 2097176
  7.5 0.5 pack.6
  8.0 2.8 %collective-permute-start.1 = (f32[160,1024]{1,0:T(8,128)S(1)}, f32[160,1024]{1,0:T(8,128)S(1)}, u32[]{:S(2)}, u32[]{:S(2)}) collective-permute-start(f32[160,1024]{1,0:T(8,128)S(1)} %get-tuple-element.54), channel_id=1, source_target_pairs={{0,4},{4,0},{8,12},{12,8},{16,20},{20,16},{24,28},{28,24},{1,5},{5... | collective-permute-start | bytes 1966088 | tf_op jit(solution)/shard_map/ppermute | solution.py:313
  10.9 1.3 %collective-permute-start.3 = (f32[2,1,2048]{2,1,0:T(1,128)S(1)}, f32[2,1,2048]{2,1,0:T(1,128)S(1)}, u32[]{:S(2)}, u32[]{:S(2)}) collective-permute-start(f32[2,1,2048]{2,1,0:T(1,128)S(1)} %get-tuple-element.99), channel_id=1, source_target_pairs={{1,0},{2,1},{3,2},{5,4},{6,5},{7,6},{9,8},{10,9},{11,10},{13,12},{... | collective-permute-start | bytes 49160 | tf_op jit(solution)/shard_map/ppermute | solution.py:408
  12.2 3.0 %collective-permute-start.2 = (f32[2,1,2048]{2,1,0:T(1,128)S(1)}, f32[2,1,2048]{2,1,0:T(1,128)S(1)}, u32[]{:S(2)}, u32[]{:S(2)}) collective-permute-start(f32[2,1,2048]{2,1,0:T(1,128)S(1)} %get-tuple-element.100), channel_id=1, source_target_pairs={{0,1},{1,2},{2,3},{4,5},{5,6},{6,7},{8,9},{9,10},{10,11},{12,13},{... | collective-permute-start | bytes 49160 | tf_op jit(solution)/shard_map/ppermute | solution.py:407
  15.2 2.1 %collective-permute-done.4.face.message = f32[128,1024]{1,0:T(8,128)S(1)} collective-permute-done((f32[128,1024]{1,0:T(8,128)S(1)}, f32[128,1024]{1,0:T(8,128)S(1)}, u32[]{:S(2)}, u32[]{:S(2)}) %collective-permute-start.4) | collective-permute-done | bytes 524320 | tf_op jit(solution)/shard_map/ppermute | solution.py:313
  17.3 4.0 %collective-permute-start.5 = (f32[48,1024]{1,0:T(8,128)S(1)}, f32[48,1024]{1,0:T(8,128)S(1)}, u32[]{:S(2)}, u32[]{:S(2)}) collective-permute-start(f32[48,1024]{1,0:T(8,128)S(1)} %slice.16), channel_id=1, source_target_pairs={{0,8},{8,16},{12,4},{16,24},{20,12},{28,20},{1,9},{9,17},{13,5},{1... | collective-permute-start | bytes 589832 | tf_op jit(solution)/shard_map/ppermute | solution.py:316
  21.4 0.0 collective-permute-done.2.rest_1_.rest_0_
  21.4 0.4 pack.7
  21.8 0.3 pack.8
  22.2 2.4 %collective-permute-done.5.passed = f32[48,1024]{1,0:T(8,128)S(1)} collective-permute-done((f32[48,1024]{1,0:T(8,128)S(1)}, f32[48,1024]{1,0:T(8,128)S(1)}, u32[]{:S(2)}, u32[]{:S(2)}) %collective-permute-start.5) | collective-permute-done | bytes 196640 | tf_op jit(solution)/shard_map/ppermute | solution.py:316
  24.5 1.4 %render.5 = (f32[4,24,512]{2,1,0:T(8,128)S(1)}, f32[4,24,512]{2,1,0:T(8,128)S(1)}, f32[8,128]{1,0:T(8,128)S(1)}) custom-call(f32[4,256]{1,0:T(4,128)S(1)} %maximum_convert_fusion.table, f32[2,128,2048]{2,1,0:T(8,128)S(1)} %copy-done, s32[2,128,2048]{2,1,0:T(8,128)S(1)} %copy-done.1, f32[128,1024]{1,0:T(8,128)S(1)} %collective-permute-done.direct, ...), custom_call_target="tpu_custom_call" | custom-call | flops 2157071360 | bytes 1024 | tf_op jit(solution)/shard_map/render/pallas_call | solution.py:275
  25.9 2.6 %collective-permute-start.6 = (f32[4,24,512]{2,1,0:T(8,128)S(1)}, f32[4,24,512]{2,1,0:T(8,128)S(1)}, u32[]{:S(2)}, u32[]{:S(2)}) collective-permute-start(f32[4,24,512]{2,1,0:T(8,128)S(1)} %get-tuple-element.60), channel_id=1, source_target_pairs={{0,8},{4,12},{8,0},{12,4},{16,24},{20,28},{24,16},{28,20},{1,9},{5... | collective-permute-start | bytes 589832 | tf_op jit(solution)/shard_map/ppermute | solution.py:417
  28.5 1.5 %collective-permute-start.9 = (f32[104,1024]{1,0:T(8,128)S(1)}, f32[104,1024]{1,0:T(8,128)S(1)}, u32[]{:S(2)}, u32[]{:S(2)}) collective-permute-start(f32[104,1024]{1,0:T(8,128)S(1)} %get-tuple-element.65), channel_id=1, source_target_pairs={{0,4},{4,0},{8,12},{12,8},{16,20},{20,16},{24,28},{28,24},{1,5},{5... | collective-permute-start | bytes 1277960 | tf_op jit(solution)/shard_map/ppermute | solution.py:313
  30.0 1.3 %collective-permute-done.1.message.face = f32[160,1024]{1,0:T(8,128)S(1)} collective-permute-done((f32[160,1024]{1,0:T(8,128)S(1)}, f32[160,1024]{1,0:T(8,128)S(1)}, u32[]{:S(2)}, u32[]{:S(2)}) %collective-permute-start.1) | collective-permute-done | bytes 655392 | tf_op jit(solution)/shard_map/ppermute | solution.py:313
  31.4 4.0 %collective-permute-start.8 = (f32[80,1024]{1,0:T(8,128)S(1)}, f32[80,1024]{1,0:T(8,128)S(1)}, u32[]{:S(2)}, u32[]{:S(2)}) collective-permute-start(f32[80,1024]{1,0:T(8,128)S(1)} %slice.17), channel_id=1, source_target_pairs={{0,8},{8,16},{12,4},{16,24},{20,12},{28,20},{1,9},{9,17},{13,5},{1... | collective-permute-start | bytes 983048 | tf_op jit(solution)/shard_map/ppermute | solution.py:316
  35.4 0.1 collective-permute-start.11
  35.5 0.0 collective-permute-done.6.rest_1_
  35.6 1.4 %render.6 = (f32[4,24,512]{2,1,0:T(8,128)S(1)}, f32[4,24,512]{2,1,0:T(8,128)S(1)}, f32[8,128]{1,0:T(8,128)S(1)}) custom-call(f32[4,256]{1,0:T(4,128)S(1)} %maximum_convert_fusion.table, f32[2,128,2048]{2,1,0:T(8,128)S(1)} %copy-done, s32[2,128,2048]{2,1,0:T(8,128)S(1)} %copy-done.2, f32[128,1024]{1,0:T(8,128)S(1)} %collective-permute-done.direct, ...), custom_call_target="tpu_custom_call" | custom-call | flops 2157071360 | bytes 1024 | tf_op jit(solution)/shard_map/render/pallas_call | solution.py:275
  37.0 2.0 %collective-permute-start.12 = (f32[4,24,512]{2,1,0:T(8,128)S(1)}, f32[4,24,512]{2,1,0:T(8,128)S(1)}, u32[]{:S(2)}, u32[]{:S(2)}) collective-permute-start(f32[4,24,512]{2,1,0:T(8,128)S(1)} %get-tuple-element.71), channel_id=1, source_target_pairs={{0,8},{4,12},{8,0},{12,4},{16,24},{20,28},{24,16},{28,20},{1,9},{5... | collective-permute-start | bytes 589832 | tf_op jit(solution)/shard_map/ppermute | solution.py:417
  39.0 0.3 pack.9
  39.3 1.7 %collective-permute-start.7 = (f32[56,1024]{1,0:T(8,128)S(1)}, f32[56,1024]{1,0:T(8,128)S(1)}, u32[]{:S(2)}, u32[]{:S(2)}) collective-permute-start(f32[56,1024]{1,0:T(8,128)S(1)} %get-tuple-element.64), channel_id=1, source_target_pairs={{0,4},{4,0},{8,12},{12,8},{16,20},{20,16},{24,28},{28,24},{1,5},{5... | collective-permute-start | bytes 688136 | tf_op jit(solution)/shard_map/ppermute | solution.py:313
  41.0 0.2 collective-permute-done.9.message
  41.2 1.2 %collective-permute-done.8.passed = f32[80,1024]{1,0:T(8,128)S(1)} collective-permute-done((f32[80,1024]{1,0:T(8,128)S(1)}, f32[80,1024]{1,0:T(8,128)S(1)}, u32[]{:S(2)}, u32[]{:S(2)}) %collective-permute-start.8) | collective-permute-done | bytes 327712 | tf_op jit(solution)/shard_map/ppermute | solution.py:316
  42.4 1.8 %render.7 = (f32[4,32,512]{2,1,0:T(8,128)S(1)}, f32[4,32,512]{2,1,0:T(8,128)S(1)}, f32[8,128]{1,0:T(8,128)S(1)}) custom-call(f32[4,256]{1,0:T(4,128)S(1)} %maximum_convert_fusion.table, f32[2,128,2048]{2,1,0:T(8,128)S(1)} %copy-done, s32[2,128,2048]{2,1,0:T(8,128)S(1)} %copy-done.2, f32[128,1024]{1,0:T(8,128)S(1)} %collective-permute-done.direct, ...), custom_call_target="tpu_custom_call" | custom-call | flops 2726595328 | bytes 1024 | tf_op jit(solution)/shard_map/render/pallas_call | solution.py:275
  44.2 2.6 %collective-permute-start.10 = (f32[4,32,512]{2,1,0:T(8,128)S(1)}, f32[4,32,512]{2,1,0:T(8,128)S(1)}, u32[]{:S(2)}, u32[]{:S(2)}) collective-permute-start(f32[4,32,512]{2,1,0:T(8,128)S(1)} %get-tuple-element.68), channel_id=1, source_target_pairs={{0,8},{4,12},{8,0},{12,4},{16,24},{20,28},{24,16},{28,20},{1,9},{5... | collective-permute-start | bytes 786440 | tf_op jit(solution)/shard_map/ppermute | solution.py:417
  46.8 0.1 merge.6
  46.8 4.6 %collective-permute-start.15 = (f32[4,48,256]{2,1,0:T(8,128)S(1)}, f32[4,48,256]{2,1,0:T(8,128)S(1)}, u32[]{:S(2)}, u32[]{:S(2)}) collective-permute-start(f32[4,48,256]{2,1,0:T(8,128)S(1)} %get-tuple-element.83), channel_id=1, source_target_pairs={{0,16},{4,20},{8,24},{12,28},{16,0},{20,4},{24,8},{28,12},{1,17},{... | collective-permute-start | bytes 589832 | tf_op jit(solution)/shard_map/ppermute | solution.py:398
  51.4 1.8 %render.8 = (f32[4,32,512]{2,1,0:T(8,128)S(1)}, f32[4,32,512]{2,1,0:T(8,128)S(1)}, f32[8,128]{1,0:T(8,128)S(1)}) custom-call(f32[4,256]{1,0:T(4,128)S(1)} %maximum_convert_fusion.table, f32[2,128,2048]{2,1,0:T(8,128)S(1)} %copy-done, s32[2,128,2048]{2,1,0:T(8,128)S(1)} %copy-done.2, f32[128,1024]{1,0:T(8,128)S(1)} %collective-permute-done.direct, ...), custom_call_target="tpu_custom_call" | custom-call | flops 2726595328 | bytes 1024 | tf_op jit(solution)/shard_map/render/pallas_call | solution.py:275
  53.2 2.6 %collective-permute-start.16 = (f32[4,32,512]{2,1,0:T(8,128)S(1)}, f32[4,32,512]{2,1,0:T(8,128)S(1)}, u32[]{:S(2)}, u32[]{:S(2)}) collective-permute-start(f32[4,32,512]{2,1,0:T(8,128)S(1)} %get-tuple-element.87), channel_id=1, source_target_pairs={{0,8},{4,12},{8,0},{12,4},{16,24},{20,28},{24,16},{28,20},{1,9},{5... | collective-permute-start | bytes 786440 | tf_op jit(solution)/shard_map/ppermute | solution.py:417
  55.8 0.1 merge.7
  55.9 0.4 collective-permute-start.14
  56.3 1.1 %render.9 = (f32[4,16,512]{2,1,0:T(8,128)S(1)}, f32[4,16,512]{2,1,0:T(8,128)S(1)}, f32[8,128]{1,0:T(8,128)S(1)}) custom-call(f32[4,256]{1,0:T(4,128)S(1)} %maximum_convert_fusion.table, f32[2,128,2048]{2,1,0:T(8,128)S(1)} %copy-done, s32[2,128,2048]{2,1,0:T(8,128)S(1)} %copy-done.2, f32[128,1024]{1,0:T(8,128)S(1)} %collective-permute-done.direct, ...), custom_call_target="tpu_custom_call" | custom-call | flops 1587547648 | bytes 1024 | tf_op jit(solution)/shard_map/render/pallas_call | solution.py:275
  57.4 1.9 %collective-permute-start.13 = (f32[4,16,512]{2,1,0:T(8,128)S(1)}, f32[4,16,512]{2,1,0:T(8,128)S(1)}, u32[]{:S(2)}, u32[]{:S(2)}) collective-permute-start(f32[4,16,512]{2,1,0:T(8,128)S(1)} %get-tuple-element.79), channel_id=1, source_target_pairs={{0,8},{4,12},{8,0},{12,4},{16,24},{20,28},{24,16},{28,20},{1,9},{5... | collective-permute-start | bytes 393224 | tf_op jit(solution)/shard_map/ppermute | solution.py:417
  59.3 0.7 finish.4
  60.0 5.5 %collective-permute-done.16.rest_1_ = f32[4,32,512]{2,1,0:T(8,128)S(1)} collective-permute-done((f32[4,32,512]{2,1,0:T(8,128)S(1)}, f32[4,32,512]{2,1,0:T(8,128)S(1)}, u32[]{:S(2)}, u32[]{:S(2)}) %collective-permute-start.16) | collective-permute-done | bytes 262176 | tf_op jit(solution)/shard_map/ppermute | solution.py:417
  65.6 0.1 merge.8
  65.6 1.4 %collective-permute-start.18 = (f32[4,32,256]{2,1,0:T(8,128)S(1)}, f32[4,32,256]{2,1,0:T(8,128)S(1)}, u32[]{:S(2)}, u32[]{:S(2)}) collective-permute-start(f32[4,32,256]{2,1,0:T(8,128)S(1)} %get-tuple-element.94), channel_id=1, source_target_pairs={{0,16},{4,20},{8,24},{12,28},{16,0},{20,4},{24,8},{28,12},{1,17},{... | collective-permute-start | bytes 393224 | tf_op jit(solution)/shard_map/ppermute | solution.py:398
  67.0 0.7 finish.5
  67.8 2.1 %collective-permute-start.17 = (f32[4,16,256]{2,1,0:T(8,128)S(1)}, f32[4,16,256]{2,1,0:T(8,128)S(1)}, u32[]{:S(2)}, u32[]{:S(2)}) collective-permute-start(f32[4,16,256]{2,1,0:T(8,128)S(1)} %get-tuple-element.92), channel_id=1, source_target_pairs={{0,16},{4,20},{8,24},{12,28},{16,0},{20,4},{24,8},{28,12},{1,17},{... | collective-permute-start | bytes 196616 | tf_op jit(solution)/shard_map/ppermute | solution.py:398
  69.9 3.1 %collective-permute-done.18.got = f32[4,32,256]{2,1,0:T(8,128)S(1)} collective-permute-done((f32[4,32,256]{2,1,0:T(8,128)S(1)}, f32[4,32,256]{2,1,0:T(8,128)S(1)}, u32[]{:S(2)}, u32[]{:S(2)}) %collective-permute-start.18) | collective-permute-done | bytes 131104 | tf_op jit(solution)/shard_map/ppermute | solution.py:398
  73.0 0.7 finish.6
  73.7 0.0 collective-permute-done.17.got
  73.7 0.7 finish.7
  (25 shorter events, 0.2 us)
Async XLA Ops:
  0.0 4.5 %copy-start = (f32[2,128,2048]{2,1,0:T(8,128)S(1)}, f32[2,128,2048]{2,1,0:T(8,128)}, u32[]{:S(2)}) copy-start(f32[2,128,2048]{2,1,0:T(8,128)} %density.19) | copy-start | bytes 6291460
  1.5 15.8 %collective-permute-start.4 = (f32[128,1024]{1,0:T(8,128)S(1)}, f32[128,1024]{1,0:T(8,128)S(1)}, u32[]{:S(2)}, u32[]{:S(2)}) collective-permute-start(f32[128,1024]{1,0:T(8,128)S(1)} %get-tuple-element.55), channel_id=1, source_target_pairs={{0,4},{4,0},{8,12},{12,8},{16,20},{20,16},{24,28},{28,24},{1,5},{5... | collective-permute-start | bytes 1572872 | tf_op jit(solution)/shard_map/ppermute | solution.py:313
  4.6 17.6 %collective-permute-start = (f32[128,1024]{1,0:T(8,128)S(1)}, f32[128,1024]{1,0:T(8,128)S(1)}, u32[]{:S(2)}, u32[]{:S(2)}) collective-permute-start(f32[128,1024]{1,0:T(8,128)S(1)} %dynamic-slice_bitcast_fusion), channel_id=1, source_target_pairs={{4,12},{8,0},{12,20},{16,8},{20,28},{24,16},{5,13},{9,1},{13,21},{... | collective-permute-start | bytes 1572872 | tf_op jit(solution)/shard_map/ppermute | solution.py:411
  5.9 1.6 %copy-start.1 = (s32[2,128,2048]{2,1,0:T(8,128)S(1)}, s32[2,128,2048]{2,1,0:T(8,128)}, u32[]{:S(2)}) copy-start(s32[2,128,2048]{2,1,0:T(8,128)} %bins.19) | copy-start | bytes 6291460
  7.5 7.7 %copy-start.4 = (bf16[256]{0:T(256)(128)(2,1)S(1)}, bf16[256]{0:T(256)(128)(2,1)}, u32[]{:S(2)}) copy-start(bf16[256]{0:T(256)(128)(2,1)} %param.7) | copy-start | bytes 1540
  7.5 13.9 %copy-start.3 = (bf16[3,256]{1,0:T(4,128)(2,1)S(1)}, bf16[3,256]{1,0:T(4,128)(2,1)}, u32[]{:S(2)}) copy-start(bf16[3,256]{1,0:T(4,128)(2,1)} %param.6) | copy-start | bytes 4612
  8.0 23.3 %collective-permute-start.1 = (f32[160,1024]{1,0:T(8,128)S(1)}, f32[160,1024]{1,0:T(8,128)S(1)}, u32[]{:S(2)}, u32[]{:S(2)}) collective-permute-start(f32[160,1024]{1,0:T(8,128)S(1)} %get-tuple-element.54), channel_id=1, source_target_pairs={{0,4},{4,0},{8,12},{12,8},{16,20},{20,16},{24,28},{28,24},{1,5},{5... | collective-permute-start | bytes 1966088 | tf_op jit(solution)/shard_map/ppermute | solution.py:313
  10.9 10.5 %collective-permute-start.3 = (f32[2,1,2048]{2,1,0:T(1,128)S(1)}, f32[2,1,2048]{2,1,0:T(1,128)S(1)}, u32[]{:S(2)}, u32[]{:S(2)}) collective-permute-start(f32[2,1,2048]{2,1,0:T(1,128)S(1)} %get-tuple-element.99), channel_id=1, source_target_pairs={{1,0},{2,1},{3,2},{5,4},{6,5},{7,6},{9,8},{10,9},{11,10},{13,12},{... | collective-permute-start | bytes 49160 | tf_op jit(solution)/shard_map/ppermute | solution.py:408
  12.2 9.2 %collective-permute-start.2 = (f32[2,1,2048]{2,1,0:T(1,128)S(1)}, f32[2,1,2048]{2,1,0:T(1,128)S(1)}, u32[]{:S(2)}, u32[]{:S(2)}) collective-permute-start(f32[2,1,2048]{2,1,0:T(1,128)S(1)} %get-tuple-element.100), channel_id=1, source_target_pairs={{0,1},{1,2},{2,3},{4,5},{5,6},{6,7},{8,9},{9,10},{10,11},{12,13},{... | collective-permute-start | bytes 49160 | tf_op jit(solution)/shard_map/ppermute | solution.py:407
  17.3 7.2 %collective-permute-start.5 = (f32[48,1024]{1,0:T(8,128)S(1)}, f32[48,1024]{1,0:T(8,128)S(1)}, u32[]{:S(2)}, u32[]{:S(2)}) collective-permute-start(f32[48,1024]{1,0:T(8,128)S(1)} %slice.16), channel_id=1, source_target_pairs={{0,8},{8,16},{12,4},{16,24},{20,12},{28,20},{1,9},{9,17},{13,5},{1... | collective-permute-start | bytes 589832 | tf_op jit(solution)/shard_map/ppermute | solution.py:316
  24.5 11.0 %copy-start.2 = (s32[2,128,2048]{2,1,0:T(8,128)S(1)}, s32[2,128,2048]{2,1,0:T(8,128)}, u32[]{:S(2)}) copy-start(s32[2,128,2048]{2,1,0:T(8,128)} %bins.19) | copy-start | bytes 6291460
  25.9 9.6 %collective-permute-start.6 = (f32[4,24,512]{2,1,0:T(8,128)S(1)}, f32[4,24,512]{2,1,0:T(8,128)S(1)}, u32[]{:S(2)}, u32[]{:S(2)}) collective-permute-start(f32[4,24,512]{2,1,0:T(8,128)S(1)} %get-tuple-element.60), channel_id=1, source_target_pairs={{0,8},{4,12},{8,0},{12,4},{16,24},{20,28},{24,16},{28,20},{1,9},{5... | collective-permute-start | bytes 589832 | tf_op jit(solution)/shard_map/ppermute | solution.py:417
  28.5 12.8 %collective-permute-start.9 = (f32[104,1024]{1,0:T(8,128)S(1)}, f32[104,1024]{1,0:T(8,128)S(1)}, u32[]{:S(2)}, u32[]{:S(2)}) collective-permute-start(f32[104,1024]{1,0:T(8,128)S(1)} %get-tuple-element.65), channel_id=1, source_target_pairs={{0,4},{4,0},{8,12},{12,8},{16,20},{20,16},{24,28},{28,24},{1,5},{5... | collective-permute-start | bytes 1277960 | tf_op jit(solution)/shard_map/ppermute | solution.py:313
  31.4 11.1 %collective-permute-start.8 = (f32[80,1024]{1,0:T(8,128)S(1)}, f32[80,1024]{1,0:T(8,128)S(1)}, u32[]{:S(2)}, u32[]{:S(2)}) collective-permute-start(f32[80,1024]{1,0:T(8,128)S(1)} %slice.17), channel_id=1, source_target_pairs={{0,8},{8,16},{12,4},{16,24},{20,12},{28,20},{1,9},{9,17},{13,5},{1... | collective-permute-start | bytes 983048 | tf_op jit(solution)/shard_map/ppermute | solution.py:316
  35.4 16.0 %collective-permute-start.11 = (f32[104,1024]{1,0:T(8,128)S(1)}, f32[104,1024]{1,0:T(8,128)S(1)}, u32[]{:S(2)}, u32[]{:S(2)}) collective-permute-start(f32[104,1024]{1,0:T(8,128)S(1)} %get-tuple-element.69), channel_id=1, source_target_pairs={{0,4},{4,0},{8,12},{12,8},{16,20},{20,16},{24,28},{28,24},{1,5},{5... | collective-permute-start | bytes 1277960 | tf_op jit(solution)/shard_map/ppermute | solution.py:313
  37.0 9.8 %collective-permute-start.12 = (f32[4,24,512]{2,1,0:T(8,128)S(1)}, f32[4,24,512]{2,1,0:T(8,128)S(1)}, u32[]{:S(2)}, u32[]{:S(2)}) collective-permute-start(f32[4,24,512]{2,1,0:T(8,128)S(1)} %get-tuple-element.71), channel_id=1, source_target_pairs={{0,8},{4,12},{8,0},{12,4},{16,24},{20,28},{24,16},{28,20},{1,9},{5... | collective-permute-start | bytes 589832 | tf_op jit(solution)/shard_map/ppermute | solution.py:417
  39.3 16.9 %collective-permute-start.7 = (f32[56,1024]{1,0:T(8,128)S(1)}, f32[56,1024]{1,0:T(8,128)S(1)}, u32[]{:S(2)}, u32[]{:S(2)}) collective-permute-start(f32[56,1024]{1,0:T(8,128)S(1)} %get-tuple-element.64), channel_id=1, source_target_pairs={{0,4},{4,0},{8,12},{12,8},{16,20},{20,16},{24,28},{28,24},{1,5},{5... | collective-permute-start | bytes 688136 | tf_op jit(solution)/shard_map/ppermute | solution.py:313
  44.2 11.6 %collective-permute-start.10 = (f32[4,32,512]{2,1,0:T(8,128)S(1)}, f32[4,32,512]{2,1,0:T(8,128)S(1)}, u32[]{:S(2)}, u32[]{:S(2)}) collective-permute-start(f32[4,32,512]{2,1,0:T(8,128)S(1)} %get-tuple-element.68), channel_id=1, source_target_pairs={{0,8},{4,12},{8,0},{12,4},{16,24},{20,28},{24,16},{28,20},{1,9},{5... | collective-permute-start | bytes 786440 | tf_op jit(solution)/shard_map/ppermute | solution.py:417
  46.8 12.5 %collective-permute-start.15 = (f32[4,48,256]{2,1,0:T(8,128)S(1)}, f32[4,48,256]{2,1,0:T(8,128)S(1)}, u32[]{:S(2)}, u32[]{:S(2)}) collective-permute-start(f32[4,48,256]{2,1,0:T(8,128)S(1)} %get-tuple-element.83), channel_id=1, source_target_pairs={{0,16},{4,20},{8,24},{12,28},{16,0},{20,4},{24,8},{28,12},{1,17},{... | collective-permute-start | bytes 589832 | tf_op jit(solution)/shard_map/ppermute | solution.py:398
  53.2 12.4 %collective-permute-start.16 = (f32[4,32,512]{2,1,0:T(8,128)S(1)}, f32[4,32,512]{2,1,0:T(8,128)S(1)}, u32[]{:S(2)}, u32[]{:S(2)}) collective-permute-start(f32[4,32,512]{2,1,0:T(8,128)S(1)} %get-tuple-element.87), channel_id=1, source_target_pairs={{0,8},{4,12},{8,0},{12,4},{16,24},{20,28},{24,16},{28,20},{1,9},{5... | collective-permute-start | bytes 786440 | tf_op jit(solution)/shard_map/ppermute | solution.py:417
  55.9 11.2 %collective-permute-start.14 = (f32[4,32,256]{2,1,0:T(8,128)S(1)}, f32[4,32,256]{2,1,0:T(8,128)S(1)}, u32[]{:S(2)}, u32[]{:S(2)}) collective-permute-start(f32[4,32,256]{2,1,0:T(8,128)S(1)} %get-tuple-element.81), channel_id=1, source_target_pairs={{0,16},{4,20},{8,24},{12,28},{16,0},{20,4},{24,8},{28,12},{1,17},{... | collective-permute-start | bytes 393224 | tf_op jit(solution)/shard_map/ppermute | solution.py:398
  57.4 10.4 %collective-permute-start.13 = (f32[4,16,512]{2,1,0:T(8,128)S(1)}, f32[4,16,512]{2,1,0:T(8,128)S(1)}, u32[]{:S(2)}, u32[]{:S(2)}) collective-permute-start(f32[4,16,512]{2,1,0:T(8,128)S(1)} %get-tuple-element.79), channel_id=1, source_target_pairs={{0,8},{4,12},{8,0},{12,4},{16,24},{20,28},{24,16},{28,20},{1,9},{5... | collective-permute-start | bytes 393224 | tf_op jit(solution)/shard_map/ppermute | solution.py:417
  65.6 7.4 %collective-permute-start.18 = (f32[4,32,256]{2,1,0:T(8,128)S(1)}, f32[4,32,256]{2,1,0:T(8,128)S(1)}, u32[]{:S(2)}, u32[]{:S(2)}) collective-permute-start(f32[4,32,256]{2,1,0:T(8,128)S(1)} %get-tuple-element.94), channel_id=1, source_target_pairs={{0,16},{4,20},{8,24},{12,28},{16,0},{20,4},{24,8},{28,12},{1,17},{... | collective-permute-start | bytes 393224 | tf_op jit(solution)/shard_map/ppermute | solution.py:398
  67.8 5.9 %collective-permute-start.17 = (f32[4,16,256]{2,1,0:T(8,128)S(1)}, f32[4,16,256]{2,1,0:T(8,128)S(1)}, u32[]{:S(2)}, u32[]{:S(2)}) collective-permute-start(f32[4,16,256]{2,1,0:T(8,128)S(1)} %get-tuple-element.92), channel_id=1, source_target_pairs={{0,16},{4,20},{8,24},{12,28},{16,0},{20,4},{24,8},{28,12},{1,17},{... | collective-permute-start | bytes 196616 | tf_op jit(solution)/shard_map/ppermute | solution.py:398
